TPU v7x, 1024 devices: a whole 8x8x8 slice. The times are simulated.
1024 devices in a mesh: grp: 16 (over z, core), blk: 64 (over x, y).
Axes of the slice: x: 8, y: 8, z: 8, core: 2. Of those that a mesh axis runs over, the one named last changes fastest.
Arguments:
- ocean_fields: bfloat16 [40, 917504], P(None, ('grp', 'blk')), may hold values from -6 to 6
- ocean_mask: int32 [917504], P(('grp', 'blk')), may hold values 0 or 1
- entry_src: int32 [24576], P(('grp', 'blk')), may hold values from 0 to 13
- entry_route: int32 [24576, 1], P(('grp', 'blk')), may hold values from 0 to 63; in each aligned block of 24 rows (0 to 23, 24 to 47, ...) at most 2 rows name the same one
- entry_tile: int32 [24576], P(('grp', 'blk')), may hold values from 0 to 11
- weight_tiles: bfloat16 [24576, 4096], P(('grp', 'blk')), may hold values from 0 to 0.14941406
- atm_state: bfloat16 [40, 786432], P(None, ('grp', 'blk')), may hold values from -6 to 6
- atm_frac: float32 [786432], P(('grp', 'blk')), may hold values from 0 to 1
- couple: float32 [8, 40], replicated, may hold values from -1 to 1
- heat_coef: float32 [8], replicated, may hold values from -1 to 1
- kappa: float32 [30], replicated, may hold values from 0.02 to 0.15
- tracer: float32 [30, 917504], P(None, ('grp', 'blk')), may hold values from -6 to 6
- neighbours: int32 [6, 917504], P(None, ('grp', 'blk')), may hold values from 0 to 1023
Outputs:
- atm_fluxes: bfloat16 [8, 786432], P(None, ('grp', 'blk'))
- tracer_out: float32 [30, 917504], P(None, ('grp', 'blk'))
Inputs may be any that keep to these rules, and one draw needn't show every extreme that they name: `entry_route`: in each aligned block of 24 rows (one device's intersection tiles) no partition is named by more than 2 rows.
All inputs are finite; a program needn't handle non-finite values. No bound on the sum of `ocean_mask` on one device may be relied on, other than what follows from the above.
Results may differ from a plain program's by a relative error of at most 0.0035.
Values may be sent and summed in bfloat16 or wider, within the bound.
No kernel may reach another device: no remote copies, remote signals or barrier semaphores. Data moves between devices by JAX's collectives and lax.ppermute only.
A program may use at most 32 MiB of HBM per device.

v0:
```python
import jax
import jax.numpy as jnp
from jax import lax
from jax.sharding import PartitionSpec as P

TILE = 64
HALO = 64


def extended_2(block, sides, width):
    for axis, dim in sides:
        count = lax.axis_size(axis)
        forward = [(i, i + 1) for i in range(count - 1)]
        forward.append((count - 1, 0))
        backward = [(target, source) for source, target in forward]
        low = lax.ppermute(
            lax.slice_in_dim(block, block.shape[dim] - width, None, axis=dim), axis, forward
        )
        high = lax.ppermute(lax.slice_in_dim(block, 0, width, axis=dim), axis, backward)
        block = jnp.concatenate([low, block, high], axis=dim)
    return block


def shards(
    ocean_fields,
    ocean_mask,
    entry_src,
    entry_route,
    entry_tile,
    weight_tiles,
    atm_state,
    atm_frac,
    couple,
    heat_coef,
    kappa,
    tracer,
    neighbours,
):
    fields, ocean_cells = ocean_fields.shape
    tiles_ocean = ocean_cells // TILE
    entries = entry_src.shape[0]
    atm_cells = atm_state.shape[1]
    tiles_atm = atm_cells // TILE
    flux_rows = couple.shape[0]
    levels = tracer.shape[0]
    peers = lax.axis_size("blk")
    capacity = max(2, (entries + peers - 1) // peers + entries // (2 * peers))
    slots = peers * capacity
    mask_bf = ocean_mask.astype(jnp.bfloat16)
    mask_f = ocean_mask.astype(jnp.float32)
    masked = ocean_fields * mask_bf[None, :]
    tiled = (
        masked.reshape(fields, tiles_ocean, TILE)
        .transpose(1, 0, 2)
        .reshape(tiles_ocean, fields * TILE)
    )
    pick_src = (entry_src[:, None] == jnp.arange(tiles_ocean, dtype=jnp.int32)[None, :]).astype(
        jnp.bfloat16
    )
    src_tiles = jnp.dot(pick_src, tiled, preferred_element_type=jnp.float32).astype(jnp.bfloat16)
    weights = weight_tiles.reshape(entries, TILE, TILE)
    route = entry_route[:, 0]
    hits = (route[:, None] == jnp.arange(peers, dtype=jnp.int32)[None, :]).astype(jnp.int32)
    rank = jnp.sum((jnp.cumsum(hits, axis=0) - hits) * hits, axis=1)
    position = route * capacity + rank
    place = position[:, None] == jnp.arange(slots, dtype=jnp.int32)[None, :]
    place_bf = place.astype(jnp.bfloat16)
    slot_tile = jnp.sum(jnp.where(place, entry_tile[:, None] + 1, 0), axis=0) - 1
    contrib = (
        jnp.einsum(
            "efc,ecd->efd",
            src_tiles.reshape(entries, fields, TILE),
            weights,
            preferred_element_type=jnp.float32,
        )
        .astype(jnp.bfloat16)
        .reshape(entries, fields * TILE)
    )
    received = lax.all_to_all(
        jnp.einsum("es,ec->sc", place_bf, contrib, preferred_element_type=jnp.float32).astype(
            jnp.bfloat16
        ),
        "blk",
        split_axis=0,
        concat_axis=0,
        tiled=True,
    )
    got_ids = lax.all_to_all(slot_tile, "blk", split_axis=0, concat_axis=0, tiled=True)
    gather_atm = (got_ids[None, :] == jnp.arange(tiles_atm, dtype=jnp.int32)[:, None]).astype(
        jnp.bfloat16
    )
    remap = jnp.dot(gather_atm, received, preferred_element_type=jnp.float32)
    remap = remap.reshape(tiles_atm, fields, TILE).transpose(1, 0, 2).reshape(fields, atm_cells)
    diff = atm_state.astype(jnp.float32) - remap
    flux = jnp.dot(couple, diff, precision=lax.Precision.HIGHEST) * atm_frac[None, :]
    atm_fluxes = flux.astype(jnp.bfloat16)
    flux_tiles = (
        atm_fluxes.reshape(flux_rows, tiles_atm, TILE)
        .transpose(1, 0, 2)
        .reshape(tiles_atm, flux_rows * TILE)
    )
    slot_flux = jnp.einsum(
        "as,ac->sc", gather_atm, flux_tiles, preferred_element_type=jnp.float32
    ).astype(jnp.bfloat16)
    returned = lax.all_to_all(slot_flux, "blk", split_axis=0, concat_axis=0, tiled=True)
    entry_flux = jnp.dot(place_bf, returned, preferred_element_type=jnp.float32).astype(
        jnp.bfloat16
    )
    back_terms = (
        jnp.einsum(
            "ebd,ecd->ebc",
            entry_flux.reshape(entries, flux_rows, TILE),
            weights,
            preferred_element_type=jnp.float32,
        )
        .astype(jnp.bfloat16)
        .reshape(entries, flux_rows * TILE)
    )
    summed = jnp.einsum("et,ec->tc", pick_src, back_terms, preferred_element_type=jnp.float32)
    ocean_flux = (
        summed.reshape(tiles_ocean, flux_rows, TILE)
        .transpose(1, 0, 2)
        .reshape(flux_rows, ocean_cells)
        * mask_f[None, :]
    )
    heat = jnp.dot(heat_coef, ocean_flux, precision=lax.Precision.HIGHEST)
    profile = jnp.exp(-jnp.arange(levels, dtype=jnp.float32) / 10.0)
    forced = tracer + profile[:, None] * heat[None, :]
    sea = forced * mask_f[None, :]
    extended = extended_2(sea.astype(jnp.bfloat16), ((("grp", "blk"), 1),), HALO).astype(sea.dtype)
    spread = -6.0 * forced
    for which in range(6):
        spread = spread + jnp.take(extended, neighbours[which], axis=1)
    tracer_out = forced + mask_f[None, :] * kappa[:, None] * spread
    return (atm_fluxes, tracer_out)


def solution(mesh):
    return jax.shard_map(
        shards,
        mesh=mesh,
        in_specs=(
            P(None, ("grp", "blk")),
            P(("grp", "blk")),
            P(("grp", "blk")),
            P(("grp", "blk"), None),
            P(("grp", "blk")),
            P(("grp", "blk"), None),
            P(None, ("grp", "blk")),
            P(("grp", "blk")),
            P(),
            P(),
            P(),
            P(None, ("grp", "blk")),
            P(None, ("grp", "blk")),
        ),
        out_specs=(P(None, ("grp", "blk")), P(None, ("grp", "blk"))),
        check_vma=False,
    )
```

profile of v0, /device:TPU:511, one launch (start us, length us, event | category | flops | bytes accessed | tf_op | source)
XLA Modules:
  0.0 112.2 jit_solution(557136962506219077)
XLA Ops:
  0.6 0.0 copy-start
  0.7 0.7 broadcast_add_fusion.1
  1.3 0.7 fusion.9
  2.1 0.8 select_reduce_fusion.1
  2.9 0.7 fusion.21
  3.6 0.1 select_reduce_fusion
  3.7 0.8 sub.14
  4.5 11.6 %all-to-all-start = ((s32[64,2,1]{1,2,0:T(1,128)}), s32[64,2,1]{1,2,0:T(1,128)S(1)}, u32[]{:S(2)}, u32[]{:S(2)}) async-start(s32[64,2,1]{1,2,0:T(1,128)} %bitcast.3), calls=%async_computation | async-start | bytes 65536 | tf_op jit(solution)/shard_map/all_to_all | solution.py:88
  16.0 0.8 fusion.23
  16.8 1.0 slice_reduce_fusion.5
  17.8 0.9 broadcast_multiply_fusion
  18.7 0.2 reshape.81
  18.9 0.1 reshape.82
  19.1 0.2 convolution_convert_fusion.1
  19.3 0.2 reshape.83
  19.5 0.1 copy-done.1
  19.6 0.4 reshape.84
  20.0 0.3 convolution_convert_fusion.2
  20.3 0.2 reshape.85
  20.5 0.4 convolution_convert_fusion
  21.0 1.1 all_to_all.21
  22.1 0.3 all-to-all-done
  22.4 11.8 %all-to-all-start.1 = ((bf16[64,2,2560]{2,1,0:T(2,128)(2,1)}), bf16[64,2,2560]{2,1,0:T(2,128)(2,1)S(1)}, u32[]{:S(2)}, u32[]{:S(2)}) async-start(bf16[64,2,2560]{2,1,0:T(2,128)(2,1)} %all_to_all.21), calls=%async_computation.1 | async-start | bytes 1310720 | tf_op jit(solution)/shard_map/all_to_all | solution.py:79
  34.3 0.5 broadcast.123
  34.9 0.7 reduce.17
  35.6 0.1 eq.66
  35.7 13.4 %all-to-all-done.1 = bf16[64,2,2560]{2,1,0:T(2,128)(2,1)S(1)} async-done(((bf16[64,2,2560]{2,1,0:T(2,128)(2,1)}), bf16[64,2,2560]{2,1,0:T(2,128)(2,1)S(1)}, u32[]{:S(2)}, u32[]{:S(2)}) %all-to-all-start.1) | async-done | bytes 655392 | tf_op jit(solution)/shard_map/all_to_all | solution.py:79
  49.2 0.2 all_to_all.23
  49.4 0.3 copy.37
  49.8 0.0 copy-start.3
  49.8 0.0 copy-start.5
  49.8 0.6 convolution_bitcast_fusion
  50.4 0.1 reshape.86
  50.5 0.1 copy-done.3
  50.6 0.2 fusion.1
  50.8 0.1 reshape.87
  50.9 0.1 reshape.88
  51.0 0.2 convolution_convert_fusion.3
  51.3 0.7 all_to_all.24
  52.0 11.9 %all-to-all-start.2 = ((bf16[64,2,512]{2,1,0:T(2,128)(2,1)}), bf16[64,2,512]{2,1,0:T(2,128)(2,1)S(1)}, u32[]{:S(2)}, u32[]{:S(2)}) async-start(bf16[64,2,512]{2,1,0:T(2,128)(2,1)} %all_to_all.24), calls=%async_computation.2 | async-start | bytes 262144 | tf_op jit(solution)/shard_map/all_to_all | solution.py:105
  63.9 0.2 copy.40
  64.1 0.0 copy-start.7
  64.1 7.1 %all-to-all-done.2 = bf16[64,2,512]{2,1,0:T(2,128)(2,1)S(1)} async-done(((bf16[64,2,512]{2,1,0:T(2,128)(2,1)}), bf16[64,2,512]{2,1,0:T(2,128)(2,1)S(1)}, u32[]{:S(2)}, u32[]{:S(2)}) %all-to-all-start.2) | async-done | bytes 131104 | tf_op jit(solution)/shard_map/all_to_all | solution.py:105
  71.3 0.1 all_to_all.26
  71.3 0.2 convolution_convert_fusion.5
  71.5 0.1 reshape.89
  71.6 0.3 convolution_convert_fusion.4
  71.9 0.1 reshape.90
  72.0 0.1 dot_general.49
  72.1 0.1 convolution_bitcast_fusion.1
  72.3 0.1 reshape.91
  72.4 0.2 convolution_reduce_fusion
  72.5 0.3 multiply_convert_fusion
  72.9 12.7 %collective-permute-start = (bf16[30,64]{0,1:T(8,128)(2,1)S(1)}, bf16[30,64]{0,1:T(8,128)(2,1)S(1)}, u32[]{:S(2)}, u32[]{:S(2)}) collective-permute-start(bf16[30,64]{0,1:T(8,128)(2,1)S(1)} %get-tuple-element.17), channel_id=1, source_target_pairs={{0,1},{1,2},{2,3},{3,4},{4,5},{5,6},{6,7},{7,8},{8,9},{9,10},{10,1... | collective-permute-start | bytes 11528 | tf_op jit(solution)/shard_map/ppermute | solution.py:16
  85.6 1.9 %collective-permute-start.1 = (bf16[30,64]{0,1:T(8,128)(2,1)S(1)}, bf16[30,64]{0,1:T(8,128)(2,1)S(1)}, u32[]{:S(2)}, u32[]{:S(2)}) collective-permute-start(bf16[30,64]{0,1:T(8,128)(2,1)S(1)} %get-tuple-element.18), channel_id=1, source_target_pairs={{1,0},{2,1},{3,2},{4,3},{5,4},{6,5},{7,6},{8,7},{9,8},{10,9},{11,1... | collective-permute-start | bytes 11528 | tf_op jit(solution)/shard_map/ppermute | solution.py:19
  87.5 8.5 %collective-permute-done.1 = bf16[30,64]{0,1:T(8,128)(2,1)S(1)} collective-permute-done((bf16[30,64]{0,1:T(8,128)(2,1)S(1)}, bf16[30,64]{0,1:T(8,128)(2,1)S(1)}, u32[]{:S(2)}, u32[]{:S(2)}) %collective-permute-start.1) | collective-permute-done | bytes 3872 | tf_op jit(solution)/shard_map/ppermute | solution.py:19
  96.1 1.9 %gather_fusion.5 = f32[896,30]{1,0:T(8,128)S(1)} fusion(f32[30,1024]{0,1:T(8,128)S(1)} %maximum_convert_fusion, s32[1024]{0:T(1024)S(1)} %pad_clamp_fusion), kind=kCustom, calls=%fused_computation.5.clone | custom fusion | bytes 218624 | tf_op jit(solution)/shard_map/jit(_take)/gather | solution.py:133
  98.0 1.9 %gather_fusion.4 = f32[896,30]{1,0:T(8,128)S(1)} fusion(f32[30,1024]{0,1:T(8,128)S(1)} %maximum_convert_fusion, s32[1024]{0:T(1024)S(1)} %pad_clamp_fusion.1), kind=kCustom, calls=%fused_computation.4.clone | custom fusion | bytes 218624 | tf_op jit(solution)/shard_map/jit(_take)/gather | solution.py:133
  99.9 1.9 %gather_fusion.3 = f32[896,30]{1,0:T(8,128)S(1)} fusion(f32[30,1024]{0,1:T(8,128)S(1)} %maximum_convert_fusion, s32[1024]{0:T(1024)S(1)} %pad_clamp_fusion.2), kind=kCustom, calls=%fused_computation.3.clone | custom fusion | bytes 218624 | tf_op jit(solution)/shard_map/jit(_take)/gather | solution.py:133
  101.9 1.9 %gather_fusion.2 = f32[896,30]{1,0:T(8,128)S(1)} fusion(f32[30,1024]{0,1:T(8,128)S(1)} %maximum_convert_fusion, s32[1024]{0:T(1024)S(1)} %pad_clamp_fusion.3), kind=kCustom, calls=%fused_computation.2.clone | custom fusion | bytes 218624 | tf_op jit(solution)/shard_map/jit(_take)/gather | solution.py:133
  103.8 1.9 %gather_fusion.1 = f32[896,30]{1,0:T(8,128)S(1)} fusion(f32[30,1024]{0,1:T(8,128)S(1)} %maximum_convert_fusion, s32[1024]{0:T(1024)S(1)} %pad_clamp_fusion.4), kind=kCustom, calls=%fused_computation.1.clone | custom fusion | bytes 218624 | tf_op jit(solution)/shard_map/jit(_take)/gather | solution.py:133
  105.7 2.8 %gather_fusion = f32[896,30]{1,0:T(8,128)} fusion(f32[30,1024]{0,1:T(8,128)S(1)} %maximum_convert_fusion, s32[1024]{0:T(1024)S(1)} %pad_clamp_fusion.5), kind=kCustom, calls=%fused_computation.clone | custom fusion | bytes 218624 | tf_op jit(solution)/shard_map/jit(_take)/gather | solution.py:133
  108.5 2.9 %fusion.3 = f32[30,896]{0,1:T(8,128)S(1)} fusion(f32[896,30]{1,0:T(8,128)S(1)} %gather_fusion.5, f32[896,30]{1,0:T(8,128)S(1)} %gather_fusion.4, f32[896,30]{1,0:T(8,128)S(1)} %gather_fusion.3, f32[896,30]{1,0:T(8,128)S(1)} %gather_fusion.2, f32[896,30]{1,0:T(8,128)S(1)} %gather_fusion.1, f32[896,30]{1,0:T(8,128)} %gather_fusion, f32[30,896]{0,1:T(8,128)S(1)} %copy.40, ...), kind=kLoop, calls=%fused_computation.20 | loop fusion | flops 483840 | bytes 872944 | tf_op jit(solution)/shard_map/add | solution.py:134
  111.4 0.8 copy.41
  (32 shorter events, 0.3 us)
Async XLA Ops:
  0.6 49.9 %copy-start = (f32[8,40]{1,0:T(8,128)S(1)}, f32[8,40]{1,0:T(8,128)}, u32[]{:S(2)}) copy-start(f32[8,40]{1,0:T(8,128)} %param.23) | copy-start | bytes 3844
  0.6 18.5 %copy-start.6 = (s32[24]{0:T(128)S(1)}, s32[24]{0:T(128)}, u32[]{:S(2)}) copy-start(s32[24]{0:T(128)} %param.17) | copy-start | bytes 292
  4.5 18.0 %all-to-all-start = ((s32[64,2,1]{1,2,0:T(1,128)}), s32[64,2,1]{1,2,0:T(1,128)S(1)}, u32[]{:S(2)}, u32[]{:S(2)}) async-start(s32[64,2,1]{1,2,0:T(1,128)} %bitcast.3), calls=%async_computation | async-start | bytes 65536 | tf_op jit(solution)/shard_map/all_to_all | solution.py:88
  18.7 0.9 copy-start.1
  22.4 26.8 %all-to-all-start.1 = ((bf16[64,2,2560]{2,1,0:T(2,128)(2,1)}), bf16[64,2,2560]{2,1,0:T(2,128)(2,1)S(1)}, u32[]{:S(2)}, u32[]{:S(2)}) async-start(bf16[64,2,2560]{2,1,0:T(2,128)(2,1)} %all_to_all.21), calls=%async_computation.1 | async-start | bytes 1310720 | tf_op jit(solution)/shard_map/all_to_all | solution.py:79
  49.8 0.8 copy-start.3
  49.8 0.8 copy-start.5
  50.4 13.5 %copy-start.2 = (f32[30,896]{1,0:T(8,128)S(1)}, f32[30,896]{1,0:T(8,128)}, u32[]{:S(2)}) copy-start(f32[30,896]{1,0:T(8,128)} %param.26) | copy-start | bytes 322564
  50.8 13.3 %copy-start.4 = (bf16[8,768]{1,0:T(8,128)(2,1)}, bf16[8,768]{1,0:T(8,128)(2,1)S(1)}, u32[]{:S(2)}) copy-start(bf16[8,768]{1,0:T(8,128)(2,1)S(1)} %fusion.1) | copy-start | bytes 36868
  52.0 19.3 %all-to-all-start.2 = ((bf16[64,2,512]{2,1,0:T(2,128)(2,1)}), bf16[64,2,512]{2,1,0:T(2,128)(2,1)S(1)}, u32[]{:S(2)}, u32[]{:S(2)}) async-start(bf16[64,2,512]{2,1,0:T(2,128)(2,1)} %all_to_all.24), calls=%async_computation.2 | async-start | bytes 262144 | tf_op jit(solution)/shard_map/all_to_all | solution.py:105
  64.1 8.3 %copy-start.7 = (f32[8]{0:T(128)S(1)}, f32[8]{0:T(128)}, u32[]{:S(2)}) copy-start(f32[8]{0:T(128)} %param.24) | copy-start | bytes 100
  72.9 14.7 %collective-permute-start = (bf16[30,64]{0,1:T(8,128)(2,1)S(1)}, bf16[30,64]{0,1:T(8,128)(2,1)S(1)}, u32[]{:S(2)}, u32[]{:S(2)}) collective-permute-start(bf16[30,64]{0,1:T(8,128)(2,1)S(1)} %get-tuple-element.17), channel_id=1, source_target_pairs={{0,1},{1,2},{2,3},{3,4},{4,5},{5,6},{6,7},{7,8},{8,9},{9,10},{10,1... | collective-permute-start | bytes 11528 | tf_op jit(solution)/shard_map/ppermute | solution.py:16
  85.6 10.5 %collective-permute-start.1 = (bf16[30,64]{0,1:T(8,128)(2,1)S(1)}, bf16[30,64]{0,1:T(8,128)(2,1)S(1)}, u32[]{:S(2)}, u32[]{:S(2)}) collective-permute-start(bf16[30,64]{0,1:T(8,128)(2,1)S(1)} %get-tuple-element.18), channel_id=1, source_target_pairs={{1,0},{2,1},{3,2},{4,3},{5,4},{6,5},{7,6},{8,7},{9,8},{10,9},{11,1... | collective-permute-start | bytes 11528 | tf_op jit(solution)/shard_map/ppermute | solution.py:19
  105.7 2.8 %copy-start.8 = (f32[30]{0:T(128)S(1)}, f32[30]{0:T(128)}, u32[]{:S(2)}) copy-start(f32[30]{0:T(128)} %param.25) | copy-start | bytes 364
where the time goes:
time: 113 us; the launch traced here: 112 us
  starting transfers between devices  49.8 us (44%)
  waiting for transfers between devices  29.5 us (26%)
  local copies, waits for them, and re-layouts  20.3 us (18%)
  other arithmetic  8.72 us (8%)
  matrix products  2.77 us (2%)
    all_to_all x1, waiting for transfers between devices, shards(): lax.all_to_all(jnp.einsum('es,ec->sc', place_bf, contrib, preferred_eleme...  13.4 us
    ppermute x1, starting transfers between devices, extended_2(): lax.ppermute(lax.slice_in_dim(block, block.shape[dim] - width, None, axis...  12.7 us
    gather x6, local copies, waits for them, and re-layouts, shards(): spread = spread + jnp.take(extended, neighbours[which], axis=1)  12.3 us
    all_to_all x1, starting transfers between devices, shards(): lax.all_to_all(slot_flux, 'blk', split_axis=0, concat_axis=0, tiled=True)  11.9 us
    all_to_all x1, starting transfers between devices, shards(): lax.all_to_all(jnp.einsum('es,ec->sc', place_bf, contrib, preferred_eleme...  11.8 us
    all_to_all x1, starting transfers between devices, shards(): lax.all_to_all(slot_tile, 'blk', split_axis=0, concat_axis=0, tiled=True)  11.6 us
    ppermute x1, waiting for transfers between devices, extended_2(): lax.ppermute(lax.slice_in_dim(block, 0, width, axis=dim), axis, backward)  8.53 us
    all_to_all x1, waiting for transfers between devices, shards(): lax.all_to_all(slot_flux, 'blk', split_axis=0, concat_axis=0, tiled=True)  7.15 us
  transfers between devices with their start and end apart: 5, of which 4 were waited for; matrix products, arithmetic and copies ran while one was open for 6% of the time, Pallas kernels for 0%

commit v1 on v0

v1 whole, which is shorter than its diff:
```python
import jax
import jax.numpy as jnp
from jax import lax
from jax.experimental import pallas as pl
from jax.experimental.pallas import tpu as pltpu
from jax.sharding import PartitionSpec as P

TILE = 64
HALO = 64
LANES = 128
F32 = jnp.float32
BF16 = jnp.bfloat16
SMEM = pl.BlockSpec(memory_space=pltpu.SMEM)
VMEM = pl.BlockSpec(memory_space=pltpu.VMEM)


def iota(shape, dim):
    return lax.broadcasted_iota(jnp.int32, shape, dim)


def parts(value, count):
    out = []
    for _ in range(count - 1):
        high = value.astype(BF16).astype(F32)
        out.append(high)
        value = value - high
    out.append(value)
    return jnp.concatenate(out, axis=0).astype(BF16)


def column(scalars, count, rows):
    where = iota((rows, LANES), 0)
    out = jnp.zeros((rows, LANES), F32)
    for i in range(count):
        out = jnp.where(where == i, scalars[i], out)
    return out


def mm(a, b):
    return jnp.dot(a, b, preferred_element_type=F32)


def wide(col, width):
    return jnp.concatenate([col] * (width // LANES), axis=1)


def pack_kernel(src, route, tile, fields, mask, couple, weights, out, tiles, seen):
    entries = weights.shape[0]
    rows = couple.shape[0]
    for e in range(entries):
        seen[route[e]] = 0
    out[...] = jnp.zeros(out.shape, out.dtype)
    mixed = mm(parts(couple[...], 3), fields[...])
    mixed = mixed[:rows] + mixed[rows : 2 * rows] + mixed[2 * rows :]
    mixed = parts(mixed * mask[...].astype(F32), 2)
    for t in range(tiles.shape[0]):
        tiles[t] = mixed[:, t * TILE : (t + 1) * TILE]
    for e in range(entries):
        to = route[e]
        rank = seen[to]
        seen[to] = rank + 1
        sent = mm(tiles[src[e]], weights[e])
        sent = sent[:rows] + sent[rows:]
        mark = jnp.full((rows, TILE), tile[e] + 1, jnp.int32).astype(F32)
        out[to * 2 + rank] = jnp.concatenate([sent, mark], axis=1).astype(BF16)


def tables_kernel(
    src, route, near, state, frac, couple, own, edge, mixed, shares, chosen, slots, seen
):
    entries = src.shape[0]
    rows = couple.shape[0]
    cells = near.shape[1]
    for e in range(entries):
        seen[route[e]] = 0
    for e in range(entries):
        to = route[e]
        rank = seen[to]
        seen[to] = rank + 1
        slots[e] = to * 2 + rank

    part = mm(parts(couple[...], 3), state[...])
    part = part[:rows] + part[rows : 2 * rows] + part[2 * rows :]
    for t in range(state.shape[1] // TILE):
        mixed[t * rows : (t + 1) * rows, :] = part[:, t * TILE : (t + 1) * TILE]
        shares[t * rows : (t + 1) * rows, :] = jnp.broadcast_to(
            frac[:, t * TILE : (t + 1) * TILE], (rows, TILE)
        )

    low = iota((16, LANES), 1) < TILE
    for j in range(entries // 2):
        owner = jnp.where(low, src[2 * j], src[2 * j + 1])
        chosen[:, j * LANES : (j + 1) * LANES] = (iota((16, LANES), 0) == owner).astype(F32)

    def counts(place):
        total = jnp.zeros(place.shape, F32)
        for k in range(near.shape[0]):
            total = total + (near[k : k + 1, :] == place).astype(F32)
        return total.astype(BF16)

    place = iota((16, cells), 0)

    @pl.loop(0, cells // 16)
    def _(i):
        at = pl.multiple_of(i * 16, 16)
        own[pl.ds(at, 16), :] = counts(place + (at + HALO))

    @pl.loop(0, HALO // 16)
    def _(i):
        at = pl.multiple_of(i * 16, 16)
        edge[pl.ds(at, 16), :] = counts(place + at)
        edge[pl.ds(at + HALO, 16), :] = counts(place + (at + HALO + cells))


def merge_kernel(got, mixed, shares, heat_coef, fluxes, back):
    slots, rows, _ = got.shape
    peers = slots // 2
    tiles_atm = mixed.shape[0] // rows
    flat = got[...].reshape(slots * rows, LANES)
    pick = (iota((rows, LANES), 1) == TILE).astype(F32).astype(BF16)
    ids = lax.dot_general(pick, flat, (((1,), (1,)), ((), ())), preferred_element_type=F32)
    wanted = iota((peers, slots * rows), 0) * (2 * rows)
    at = iota((peers, slots * rows), 1)
    first = jnp.concatenate(
        [(at == wanted).astype(F32), (at == wanted + rows).astype(F32)], axis=0
    ).astype(BF16)
    by_slot = mm(first, flat)
    own_row = iota(ids.shape, 0) == lax.rem(iota(ids.shape, 1), rows)
    ids = jnp.where(own_row, ids, 0.0)
    member = jnp.concatenate(
        [(ids == (t + 1.0)).astype(F32) for t in range(tiles_atm)], axis=0
    ).astype(BF16)
    remap = mm(member, flat)[:, :TILE]
    flux = ((mixed[...] - remap) * shares[...]).astype(BF16)
    for t in range(tiles_atm):
        fluxes[:, t * TILE : (t + 1) * TILE] = flux[t * rows : (t + 1) * rows, :]
    coef = column(heat_coef, rows, rows)[:, :TILE]
    flux = flux.astype(F32)
    heat = [
        jnp.sum(flux[t * rows : (t + 1) * rows, :] * coef, axis=0, keepdims=True)
        for t in range(tiles_atm)
    ]
    heat = jnp.concatenate(heat + [jnp.zeros((16 - tiles_atm, TILE), F32)], axis=0)
    high = heat.astype(BF16).astype(F32)
    heat = jnp.concatenate([high, heat - high, jnp.zeros((32, TILE), F32)], axis=0)
    blank = jnp.zeros((TILE, TILE), F32)
    spread = jnp.concatenate(
        [jnp.concatenate([blank, heat], axis=1), jnp.concatenate([heat, blank], axis=1)], axis=0
    ).astype(BF16)
    lane = iota((peers, LANES), 1)
    offset = lax.rem(lane, TILE)
    target = jnp.where(offset < 32, lax.rem(lane, 16) + 1, -1).astype(F32)
    named = jnp.where(lane < TILE, pltpu.roll(by_slot[peers:], TILE, 1), by_slot[:peers])
    back[...] = mm((named == target).astype(F32).astype(BF16), spread).reshape(peers, 1, LANES)


def base_kernel(kappa, tracer, mask, own, base, edges):
    levels, cells = tracer.shape
    sea = mask[...].astype(F32)
    value = tracer[...]
    masked = value * sea
    pad = jnp.zeros((32 - levels, cells), F32)
    near = mm(parts(jnp.concatenate([masked, pad], axis=0), 2), own[...])
    near = (near[:32] + near[32:])[:levels]
    rate = wide(column(kappa, levels, levels), cells)
    base[...] = value + sea * rate * (near - 6.0 * value)
    edges[...] = jnp.concatenate([masked[:, cells - HALO :], masked[:, :HALO]], axis=1)


def profile(levels, width):
    return jnp.exp(-iota((levels, width), 0).astype(F32) / 10.0)


def heat_kernel(slots, got, chosen, flipped, mask, edges, heat, forced):
    entries = slots.shape[0]
    cells = mask.shape[1]
    low = iota((1, LANES), 1) < TILE
    pieces = []
    for j in range(entries // 2):
        one, two = slots[2 * j], slots[2 * j + 1]
        a, b = got[one // 2], got[two // 2]
        a = jnp.where(lax.rem(one, 2) == 0, a, pltpu.roll(a, TILE, 1))
        b = jnp.where(lax.rem(two, 2) == 1, b, pltpu.roll(b, TILE, 1))
        pieces.append(jnp.where(low, a, b))
    line = jnp.concatenate(pieces, axis=1)
    high = line.astype(BF16).astype(F32)
    pick = chosen[...]
    spread = jnp.concatenate([pick * high, pick * (line - high)], axis=0).astype(BF16)
    summed = mm(spread, flipped[...])
    summed = summed[:16] + summed[16:]
    row = jnp.concatenate([summed[t : t + 1, :] for t in range(cells // TILE)], axis=1)
    row = row * mask[...].astype(F32)
    heat[...] = row
    ends = jnp.concatenate([row[:, cells - HALO :], row[:, :HALO]], axis=1)
    levels = edges.shape[0]
    forced[...] = edges[...] + profile(levels, LANES) * ends


def partial_kernel(kappa, heat, own, base, mask, out):
    levels, cells = base.shape
    sea = mask[...].astype(F32)
    row = heat[...]
    high = row.astype(BF16).astype(F32)
    rows = jnp.concatenate([high, row - high, jnp.zeros((14, cells), F32)], axis=0)
    near = mm(rows.astype(BF16), own[...])
    near = near[0:1] + near[1:2]
    depth = wide(profile(levels, LANES), cells)
    rate = wide(column(kappa, levels, levels), cells)
    out[...] = base[...] + depth * (row + rate * (sea * (near - 6.0 * row)))


def finish_kernel(kappa, before, after, edge, part, mask, out):
    levels, cells = part.shape
    low = iota((levels, LANES), 1) < TILE
    halo = jnp.where(low, before[...], after[...])
    pad = jnp.zeros((32 - levels, LANES), F32)
    near = mm(parts(jnp.concatenate([halo, pad], axis=0), 2), edge[...])
    near = (near[:32] + near[32:])[:levels]
    rate = wide(column(kappa, levels, levels), cells)
    out[...] = part[...] + mask[...].astype(F32) * rate * near


def call(kernel, out_shape, in_specs, out_specs, scratch=(), flops=1_000_000):
    return pl.pallas_call(
        kernel,
        out_shape=out_shape,
        in_specs=in_specs,
        out_specs=out_specs,
        scratch_shapes=list(scratch),
        cost_estimate=pl.CostEstimate(flops=flops, bytes_accessed=2_000_000, transcendentals=0),
        compiler_params=pltpu.CompilerParams(vmem_limit_bytes=24 * 2**20),
    )


def shards(
    ocean_fields,
    ocean_mask,
    entry_src,
    entry_route,
    entry_tile,
    weight_tiles,
    atm_state,
    atm_frac,
    couple,
    heat_coef,
    kappa,
    tracer,
    neighbours,
):
    fields, cells = ocean_fields.shape
    entries = entry_src.shape[0]
    atm_cells = atm_state.shape[1]
    tiles_atm = atm_cells // TILE
    rows = couple.shape[0]
    levels = tracer.shape[0]
    peers = lax.axis_size("blk")
    shape = jax.ShapeDtypeStruct
    mask = ocean_mask.reshape(1, cells)
    route = entry_route.reshape(entries)
    weights = weight_tiles.reshape(entries, TILE, TILE)
    sent = call(
        pack_kernel,
        shape((peers * 2, rows, LANES), BF16),
        [SMEM, SMEM, SMEM, VMEM, VMEM, VMEM, VMEM],
        VMEM,
        [pltpu.VMEM((cells // TILE, 2 * rows, TILE), BF16), pltpu.SMEM((peers,), jnp.int32)],
    )(entry_src, route, entry_tile, ocean_fields, mask, couple, weights)
    got = lax.all_to_all(sent, "blk", split_axis=0, concat_axis=0, tiled=True)
    own, edge, mixed, shares, chosen, slots = call(
        tables_kernel,
        (
            shape((cells, cells), BF16),
            shape((2 * HALO, cells), BF16),
            shape((tiles_atm * rows, TILE), F32),
            shape((tiles_atm * rows, TILE), F32),
            shape((16, entries * TILE), F32),
            shape((entries,), jnp.int32),
        ),
        [SMEM, SMEM, VMEM, VMEM, VMEM, VMEM],
        (VMEM, VMEM, VMEM, VMEM, VMEM, SMEM),
        [pltpu.SMEM((peers,), jnp.int32)],
        flops=1_000_000_000,
    )(entry_src, route, neighbours, atm_state, atm_frac.reshape(1, atm_cells), couple)
    fluxes, back = call(
        merge_kernel,
        (shape((rows, atm_cells), BF16), shape((peers, 1, LANES), F32)),
        [VMEM, VMEM, VMEM, SMEM],
        (VMEM, VMEM),
    )(got, mixed, shares, heat_coef)
    returned = lax.all_to_all(back, "blk", split_axis=0, concat_axis=0, tiled=True)
    base, edges = call(
        base_kernel,
        (shape((levels, cells), F32), shape((levels, 2 * HALO), F32)),
        [SMEM, VMEM, VMEM, VMEM],
        (VMEM, VMEM),
        flops=1_000_000_000,
    )(kappa, tracer, mask, own)
    flipped = weights.transpose(0, 2, 1).reshape(entries * TILE, TILE)
    heat, forced = call(
        heat_kernel,
        (shape((1, cells), F32), shape((levels, 2 * HALO), F32)),
        [SMEM, VMEM, VMEM, VMEM, VMEM, VMEM],
        (VMEM, VMEM),
    )(slots, returned, chosen, flipped, mask, edges)
    count = lax.axis_size(("grp", "blk"))
    up = [(i, (i + 1) % count) for i in range(count)]
    down = [(target, source) for source, target in up]
    before = lax.ppermute(forced, ("grp", "blk"), up)
    after = lax.ppermute(forced, ("grp", "blk"), down)
    part = call(
        partial_kernel,
        shape((levels, cells), F32),
        [SMEM, VMEM, VMEM, VMEM, VMEM],
        VMEM,
        flops=100_000_000,
    )(kappa, heat, own, base, mask)
    tracer_out = call(
        finish_kernel,
        shape((levels, cells), F32),
        [SMEM, VMEM, VMEM, VMEM, VMEM, VMEM],
        VMEM,
    )(kappa, before, after, edge, part, mask)
    return (fluxes, tracer_out)


def solution(mesh):
    split = ("grp", "blk")
    return jax.shard_map(
        shards,
        mesh=mesh,
        in_specs=(
            P(None, split),
            P(split),
            P(split),
            P(split, None),
            P(split),
            P(split, None),
            P(None, split),
            P(split),
            P(),
            P(),
            P(),
            P(None, split),
            P(None, split),
        ),
        out_specs=(P(None, split), P(None, split)),
        check_vma=False,
    )
```

time: 113 us -> 75.7 us (0.67)
  the two profiles are of different devices: /device:TPU:511 before, /device:TPU:16 now
where the time goes in v1:
time: 75.7 us; the launch traced here: 75.2 us
  waiting for transfers between devices  28.5 us (38%)
  starting transfers between devices  28.1 us (37%)
  Pallas kernels  11.9 us (16%)
  local copies, waits for them, and re-layouts  5.87 us (8%)
  between operations  0.86 us (1%)
    all_to_all x1, starting transfers between devices, shards(): got = lax.all_to_all(sent, 'blk', split_axis=0, concat_axis=0, tiled=True)  17 us
    all_to_all x1, waiting for transfers between devices, shards(): lax.all_to_all(back, 'blk', split_axis=0, concat_axis=0, tiled=True)  10.1 us
    ppermute x1, waiting for transfers between devices, shards(): before = lax.ppermute(forced, ('grp', 'blk'), up)  10.1 us
    all_to_all x1, waiting for transfers between devices, shards(): got = lax.all_to_all(sent, 'blk', split_axis=0, concat_axis=0, tiled=True)  8.27 us
    all_to_all x1, starting transfers between devices, shards(): lax.all_to_all(back, 'blk', split_axis=0, concat_axis=0, tiled=True)  5.26 us
    pallas_call x1, Pallas kernels, shards(): call(tables_kernel, (shape((cells, cells), BF16), shape((2 * HALO, cells)...  4.3 us
    unnamed x28, local copies, waits for them, and re-layouts  3.58 us
    ppermute x1, starting transfers between devices, shards(): after = lax.ppermute(forced, ('grp', 'blk'), down)  3.33 us
  transfers between devices with their start and end apart: 4, of which 3 were waited for; matrix products, arithmetic and copies ran while one was open for 0% of the time, Pallas kernels for 8%

profile of v1, /device:TPU:16, one launch (start us, length us, event | category | flops | bytes accessed | tf_op | source)
XLA Modules:
  0.0 75.2 jit_solution(4066654478607141704)
XLA Ops:
  0.6 0.0 copy-start.2
  0.6 0.0 copy-start.7
  0.7 0.0 copy-start.9
  0.7 0.0 copy-start.13
  0.7 0.0 copy-start.12
  0.7 0.0 copy-start.11
  0.7 0.7 reshape.20.mask
  1.4 1.3 %reshape.21.weights = bf16[24,64,64]{2,1,0:T(8,128)(2,1)S(1)} reshape(bf16[24,4096]{1,0:T(8,128)(2,1)} %param.18) | data formatting | bytes 393216 | tf_op jit(solution)/shard_map/reshape | solution.py:260
  2.8 0.0 copy-start
  2.8 0.9 %copy-done = bf16[40,896]{1,0:T(8,128)(2,1)S(1)} copy-done((bf16[40,896]{1,0:T(8,128)(2,1)S(1)}, bf16[40,896]{1,0:T(8,128)(2,1)}, u32[]{:S(2)}) %copy-start) | copy-done | bytes 71704
  3.6 0.0 copy-start.1
  3.6 0.7 copy-done.1
  4.3 0.0 copy-start.5
  4.3 0.7 copy-done.5
  5.0 0.0 copy-start.6
  5.0 0.7 copy-done.6
  5.6 0.0 copy-start.8
  5.6 0.7 copy-done.8
  6.3 1.7 %shard_map.140 = bf16[128,8,128]{2,1,0:T(8,128)(2,1)} custom-call(s32[24]{0:T(128)S(1)} %copy-done.6, s32[24]{0:T(128)S(1)} %bitcast.5, s32[24]{0:T(128)S(1)} %copy-done.5, bf16[40,896]{1,0:T(8,128)(2,1)S(1)} %copy-done, s32[1,896]{1,0:T(1,128)S(1)} %reshape.20.mask, f32[8,40]{1,0:T(8,128)S(1)} %copy-done.1, bf16[24,64,64]{2,1,0:T(8,128)(2,1)S(1)} %reshape.21.weights), custom_call_target="tpu_custom_call" | custom-call | flops 1000000 | bytes 2000000 | tf_op jit(solution)/shard_map/pallas_call | solution.py:261
  8.0 17.0 %all-to-all-start = ((bf16[128,8,128]{2,1,0:T(8,128)(2,1)}), bf16[128,8,128]{2,1,0:T(8,128)(2,1)S(1)}, u32[]{:S(2)}, u32[]{:S(2)}) async-start(bf16[128,8,128]{2,1,0:T(8,128)(2,1)} %shard_map.140), calls=%async_computation | async-start | bytes 524288 | tf_op jit(solution)/shard_map/all_to_all | solution.py:268
  25.0 0.0 copy-done.13
  25.0 0.2 copy.15
  25.3 0.0 copy-done.2
  25.3 0.0 copy-done.7
  25.3 0.0 copy-done.9
  25.3 0.0 copy-done.12
  25.3 0.0 copy-done.11
  25.3 0.0 copy-start.4
  25.3 0.0 copy-start.3
  25.4 0.0 copy-start.10
  25.4 4.3 %shard_map.141 = (bf16[896,896]{1,0:T(8,128)(2,1)S(1)}, bf16[128,896]{1,0:T(8,128)(2,1)S(1)}, f32[96,64]{1,0:T(8,128)S(1)}, f32[96,64]{1,0:T(8,128)S(1)}, f32[16,1536]{1,0:T(8,128)S(1)}, /*index=5*/s32[24]{0:T(128)S(1)}) custom-call(s32[24]{0:T(128)S(1)} %copy-done.7, s32[24]{0:T(128)S(1)} %bitcast.6, s32[6,896]{1,0:T(8,128)S(1)} %copy-done.12, ...), custom_call_target="tpu_custom_call" | custom-call | flops 1000000000 | bytes 2000000 | tf_op jit(solution)/shard_map/pallas_call | solution.py:269
  29.7 8.3 %all-to-all-done.got = bf16[128,8,128]{2,1,0:T(8,128)(2,1)S(1)} async-done(((bf16[128,8,128]{2,1,0:T(8,128)(2,1)}), bf16[128,8,128]{2,1,0:T(8,128)(2,1)S(1)}, u32[]{:S(2)}, u32[]{:S(2)}) %all-to-all-start) | async-done | bytes 262176 | tf_op jit(solution)/shard_map/all_to_all | solution.py:268
  37.9 0.0 copy-done.4
  38.0 1.7 %shard_map.142 = (bf16[8,768]{1,0:T(8,128)(2,1)}, f32[64,1,128]{2,1,0:T(1,128)}) custom-call(bf16[128,8,128]{2,1,0:T(8,128)(2,1)S(1)} %all-to-all-done.got, f32[96,64]{1,0:T(8,128)S(1)} %get-tuple-element.14.mixed, f32[96,64]{1,0:T(8,128)S(1)} %get-tuple-element.15.shares, f32[8]{0:T(128)S(1)} %copy-done.4), custom_call_target="tpu_custom_call" | custom-call | flops 1000000 | bytes 2000000 | tf_op jit(solution)/shard_map/pallas_call | solution.py:284
  39.7 5.3 %all-to-all-start.1 = ((f32[64,1,128]{2,1,0:T(1,128)}), f32[64,1,128]{2,1,0:T(1,128)S(1)}, u32[]{:S(2)}, u32[]{:S(2)}) async-start(f32[64,1,128]{2,1,0:T(1,128)} %get-tuple-element.18), calls=%async_computation.1 | async-start | bytes 65536 | tf_op jit(solution)/shard_map/all_to_all | solution.py:290
  45.0 0.0 copy-done.3
  45.0 0.0 copy-done.10
  45.0 0.9 %shard_map.143 = (f32[30,896]{1,0:T(8,128)S(1)}, f32[30,128]{1,0:T(8,128)S(1)}) custom-call(f32[30]{0:T(128)S(1)} %copy-done.3, f32[30,896]{1,0:T(8,128)S(1)} %copy-done.10, s32[1,896]{1,0:T(1,128)S(1)} %reshape.20.mask, bf16[896,896]{1,0:T(8,128)(2,1)S(1)} %get-tuple-element.20.own), custom_call_target="tpu_custom_call" | custom-call | flops 1000000000 | bytes 2000000 | tf_op jit(solution)/shard_map/pallas_call | solution.py:291
  45.9 10.1 %all-to-all-done.1.got = f32[64,1,128]{2,1,0:T(1,128)S(1)} async-done(((f32[64,1,128]{2,1,0:T(1,128)}), f32[64,1,128]{2,1,0:T(1,128)S(1)}, u32[]{:S(2)}, u32[]{:S(2)}) %all-to-all-start.1) | async-done | bytes 32800 | tf_op jit(solution)/shard_map/all_to_all | solution.py:290
  56.0 1.0 %shard_map.144 = (f32[1,896]{1,0:T(1,128)S(1)}, f32[30,128]{1,0:T(8,128)S(1)}) custom-call(s32[24]{0:T(128)S(1)} %get-tuple-element.17.slots, f32[64,1,128]{2,1,0:T(1,128)S(1)} %all-to-all-done.1.got, f32[16,1536]{1,0:T(8,128)S(1)} %get-tuple-element.19.chosen, bf16[1536,64]{1,0:T(8,128)(2,1)S(1)} %bitcast.4, s32[1,896]{1,0:T(1,128)S(1)} %reshape.20.mask, ...), custom_call_target="tpu_custom_call" | custom-call | flops 1000000 | bytes 2000000 | tf_op jit(solution)/shard_map/pallas_call | solution.py:299
  57.0 3.3 %collective-permute-start.1 = (f32[30,128]{1,0:T(8,128)S(1)}, f32[30,128]{1,0:T(8,128)S(1)}, u32[]{:S(2)}, u32[]{:S(2)}) collective-permute-start(f32[30,128]{1,0:T(8,128)S(1)} %get-tuple-element.22), channel_id=1, source_target_pairs={{1,0},{2,1},{3,2},{4,3},{5,4},{6,5},{7,6},{8,7},{9,8},{10,9},{11,1... | collective-permute-start | bytes 46088 | tf_op jit(solution)/shard_map/ppermute | solution.py:309
  60.3 2.5 %collective-permute-start = (f32[30,128]{1,0:T(8,128)S(1)}, f32[30,128]{1,0:T(8,128)S(1)}, u32[]{:S(2)}, u32[]{:S(2)}) collective-permute-start(f32[30,128]{1,0:T(8,128)S(1)} %get-tuple-element.22), channel_id=1, source_target_pairs={{0,1},{1,2},{2,3},{3,4},{4,5},{5,6},{6,7},{7,8},{8,9},{9,10},{10,1... | collective-permute-start | bytes 46088 | tf_op jit(solution)/shard_map/ppermute | solution.py:308
  62.8 0.9 %shard_map.145.part = f32[30,896]{1,0:T(8,128)S(1)} custom-call(f32[30]{0:T(128)S(1)} %copy-done.3, f32[1,896]{1,0:T(1,128)S(1)} %get-tuple-element.24.heat, bf16[896,896]{1,0:T(8,128)(2,1)S(1)} %get-tuple-element.20.own, f32[30,896]{1,0:T(8,128)S(1)} %get-tuple-element.25.base, s32[1,896]{1,0:T(1,128)S(1)} %reshape.20.mask), custom_call_target="tpu_custom_call" | custom-call | flops 100000000 | bytes 2000000 | tf_op jit(solution)/shard_map/pallas_call | solution.py:310
  63.8 0.0 collective-permute-done.1.after
  63.8 10.1 %collective-permute-done.before = f32[30,128]{1,0:T(8,128)S(1)} collective-permute-done((f32[30,128]{1,0:T(8,128)S(1)}, f32[30,128]{1,0:T(8,128)S(1)}, u32[]{:S(2)}, u32[]{:S(2)}) %collective-permute-start) | collective-permute-done | bytes 15392 | tf_op jit(solution)/shard_map/ppermute | solution.py:308
  73.8 1.4 %shard_map.146 = f32[30,896]{1,0:T(8,128)} custom-call(f32[30]{0:T(128)S(1)} %copy-done.3, f32[30,128]{1,0:T(8,128)S(1)} %collective-permute-done.before, f32[30,128]{1,0:T(8,128)S(1)} %collective-permute-done.1.after, bf16[128,896]{1,0:T(8,128)(2,1)S(1)} %get-tuple-element.23.edge, f32[30,896]{1,0:T(8,128)S(1)} %shard_map.145.part, s32[1,896]{1,0:T(1,128)S(1)} %reshape.20.mask), custom_call_target="tpu_custom_call" | custom-call | flops 1000000 | bytes 2000000 | tf_op jit(solution)/shard_map/pallas_call | solution.py:317
  (1 shorter events, 0.0 us)
Async XLA Ops:
  0.6 24.6 %copy-start.2 = (f32[8,40]{1,0:T(8,128)S(1)}, f32[8,40]{1,0:T(8,128)}, u32[]{:S(2)}) copy-start(f32[8,40]{1,0:T(8,128)} %couple.3) | copy-start | bytes 3844
  0.6 24.6 %copy-start.7 = (s32[24]{0:T(128)S(1)}, s32[24]{0:T(128)}, u32[]{:S(2)}) copy-start(s32[24]{0:T(128)} %src.3) | copy-start | bytes 292
  0.7 24.6 %copy-start.9 = (s32[24,1]{0,1:T(1,128)S(1)}, s32[24,1]{0,1:T(1,128)}, u32[]{:S(2)}) copy-start(s32[24,1]{0,1:T(1,128)} %param.16) | copy-start | bytes 292
  0.7 24.4 %copy-start.13 = (f32[768]{0:T(1024)S(1)}, f32[768]{0:T(1024)}, u32[]{:S(2)}) copy-start(f32[768]{0:T(1024)} %param.20) | copy-start | bytes 9220
  0.7 24.6 %copy-start.12 = (s32[6,896]{1,0:T(8,128)S(1)}, s32[6,896]{1,0:T(8,128)}, u32[]{:S(2)}) copy-start(s32[6,896]{1,0:T(8,128)} %near.1) | copy-start | bytes 64516
  0.7 24.6 %copy-start.11 = (bf16[40,768]{1,0:T(8,128)(2,1)S(1)}, bf16[40,768]{1,0:T(8,128)(2,1)}, u32[]{:S(2)}) copy-start(bf16[40,768]{1,0:T(8,128)(2,1)} %state.1) | copy-start | bytes 184324
  2.8 0.9 %copy-start = (bf16[40,896]{1,0:T(8,128)(2,1)S(1)}, bf16[40,896]{1,0:T(8,128)(2,1)}, u32[]{:S(2)}) copy-start(bf16[40,896]{1,0:T(8,128)(2,1)} %fields.1) | copy-start | bytes 215044
  3.6 0.7 copy-start.1
  4.3 0.7 copy-start.5
  5.0 0.7 copy-start.6
  5.6 0.7 copy-start.8
  8.0 30.0 %all-to-all-start = ((bf16[128,8,128]{2,1,0:T(8,128)(2,1)}), bf16[128,8,128]{2,1,0:T(8,128)(2,1)S(1)}, u32[]{:S(2)}, u32[]{:S(2)}) async-start(bf16[128,8,128]{2,1,0:T(8,128)(2,1)} %shard_map.140), calls=%async_computation | async-start | bytes 524288 | tf_op jit(solution)/shard_map/all_to_all | solution.py:268
  25.3 12.6 %copy-start.4 = (f32[8]{0:T(128)S(1)}, f32[8]{0:T(128)}, u32[]{:S(2)}) copy-start(f32[8]{0:T(128)} %heat_coef.1) | copy-start | bytes 100
  25.3 19.6 %copy-start.3 = (f32[30]{0:T(128)S(1)}, f32[30]{0:T(128)}, u32[]{:S(2)}) copy-start(f32[30]{0:T(128)} %kappa.5) | copy-start | bytes 364
  25.4 19.6 %copy-start.10 = (f32[30,896]{1,0:T(8,128)S(1)}, f32[30,896]{1,0:T(8,128)}, u32[]{:S(2)}) copy-start(f32[30,896]{1,0:T(8,128)} %tracer.1) | copy-start | bytes 322564
  39.7 16.3 %all-to-all-start.1 = ((f32[64,1,128]{2,1,0:T(1,128)}), f32[64,1,128]{2,1,0:T(1,128)S(1)}, u32[]{:S(2)}, u32[]{:S(2)}) async-start(f32[64,1,128]{2,1,0:T(1,128)} %get-tuple-element.18), calls=%async_computation.1 | async-start | bytes 65536 | tf_op jit(solution)/shard_map/all_to_all | solution.py:290
  57.0 6.8 %collective-permute-start.1 = (f32[30,128]{1,0:T(8,128)S(1)}, f32[30,128]{1,0:T(8,128)S(1)}, u32[]{:S(2)}, u32[]{:S(2)}) collective-permute-start(f32[30,128]{1,0:T(8,128)S(1)} %get-tuple-element.22), channel_id=1, source_target_pairs={{1,0},{2,1},{3,2},{4,3},{5,4},{6,5},{7,6},{8,7},{9,8},{10,9},{11,1... | collective-permute-start | bytes 46088 | tf_op jit(solution)/shard_map/ppermute | solution.py:309
  60.3 13.5 %collective-permute-start = (f32[30,128]{1,0:T(8,128)S(1)}, f32[30,128]{1,0:T(8,128)S(1)}, u32[]{:S(2)}, u32[]{:S(2)}) collective-permute-start(f32[30,128]{1,0:T(8,128)S(1)} %get-tuple-element.22), channel_id=1, source_target_pairs={{0,1},{1,2},{2,3},{3,4},{4,5},{5,6},{6,7},{7,8},{8,9},{9,10},{10,1... | collective-permute-start | bytes 46088 | tf_op jit(solution)/shard_map/ppermute | solution.py:308

commit v2 on v1

v2 whole, which is shorter than its diff:
```python
import jax
import jax.numpy as jnp
from jax import lax
from jax.experimental import pallas as pl
from jax.experimental.pallas import tpu as pltpu
from jax.sharding import PartitionSpec as P

TILE = 64
HALO = 64
LANES = 128
PITCH = 33
F32 = jnp.float32
BF16 = jnp.bfloat16
SMEM = pl.BlockSpec(memory_space=pltpu.SMEM)
VMEM = pl.BlockSpec(memory_space=pltpu.VMEM)
HBM = pl.BlockSpec(memory_space=pltpu.HBM)


def iota(shape, dim):
    return lax.broadcasted_iota(jnp.int32, shape, dim)


def parts(value, count):
    out = []
    for _ in range(count - 1):
        high = value.astype(BF16).astype(F32)
        out.append(high)
        value = value - high
    out.append(value)
    return jnp.concatenate(out, axis=0).astype(BF16)


def column(scalars, count, rows):
    where = iota((rows, LANES), 0)
    out = jnp.zeros((rows, LANES), F32)
    for i in range(count):
        out = jnp.where(where == i, scalars[i], out)
    return out


def mm(a, b):
    return jnp.dot(a, b, preferred_element_type=F32)


def line(block):
    return jnp.concatenate([block[i : i + 1, :] for i in range(block.shape[0])], axis=1)


def across(col, width):
    return jnp.concatenate([col] * (width // LANES), axis=1)


def pack_kernel(
    src_hbm, route_hbm, tile_hbm, fields_hbm, mask_hbm, couple_hbm, weights_hbm, out,
    src, route, tile, fields, mask, couple, weights, tiles, wide, slots, seen, sems,
):
    pairs = (
        (fields_hbm, fields),
        (mask_hbm, mask),
        (couple_hbm, couple),
        (route_hbm, route),
        (src_hbm, src),
        (tile_hbm, tile),
        (weights_hbm, weights),
    )
    copies = [pltpu.make_async_copy(a, b, sems.at[i]) for i, (a, b) in enumerate(pairs)]
    for copy in copies:
        copy.start()
    entries = weights.shape[0]
    rows = couple.shape[0]
    half = rows // 2
    slots[...] = jnp.zeros(slots.shape, F32)
    for copy in copies[:3]:
        copy.wait()
    mixed = mm(parts(couple[...], 3), fields[...])
    mixed = mixed[:rows] + mixed[rows : 2 * rows] + mixed[2 * rows :]
    mixed = mixed * line(mask[...].astype(F32))
    high = mixed.astype(BF16).astype(F32)
    low = mixed - high
    flip = lambda x: jnp.concatenate([x[half:], x[:half]], axis=0)
    straight = jnp.concatenate([high, low], axis=0)
    swapped = jnp.concatenate([flip(high), flip(low)], axis=0)
    count = mixed.shape[1] // LANES
    stacks = [
        jnp.concatenate([x[:, j * LANES : (j + 1) * LANES] for j in range(count)], axis=0).astype(BF16)
        for x in (straight, swapped)
    ]
    for k in range(4):
        wanted = iota((LANES, TILE // 2), 1) * 2 + ((k // 2) * TILE + k % 2)
        pick = (iota((LANES, TILE // 2), 0) == wanted).astype(F32).astype(BF16)
        part = mm(stacks[k % 2], pick).astype(BF16)
        at = (k % 2) * 2 * rows
        for j in range(count):
            tiles[2 * j + k // 2, at : at + 2 * rows, :] = part[2 * rows * j : 2 * rows * (j + 1)]
    for copy in copies[3:]:
        copy.wait()
    for e in range(entries):
        seen[route[e]] = 0
    flat = weights[...].astype(F32)
    for g in range(entries // 8):
        for j in range(TILE // 2):
            wide[pl.ds(g * 8 * PITCH + j, 8, stride=PITCH), :] = flat[
                g * 8 : (g + 1) * 8, j * LANES : (j + 1) * LANES
            ]
    left = iota((rows, LANES), 1) < TILE
    for e in range(entries):
        to = route[e]
        rank = seen[to]
        seen[to] = rank + 1
        at = (to * 2 + rank) * (half + 1)
        sent = mm(tiles[src[e]], wide[e * PITCH : e * PITCH + TILE // 2, :].astype(BF16))
        even = sent[:rows] + sent[rows : 2 * rows]
        odd = sent[2 * rows : 3 * rows] + sent[3 * rows :]
        both = jnp.where(left, even, odd)
        slots[pl.ds(at, half), :] = both[:half] + pltpu.roll(both, TILE, 1)[half:]
        slots[pl.ds(at + half, 1), :] = jnp.full((1, LANES), tile[e] + 1, jnp.int32).astype(F32)
    out[...] = slots[...].astype(BF16)


def tables_kernel(
    src, route, near, state, frac, mask, couple, own, edge, mixed, shares, chosen, slots, seen
):
    entries = src.shape[0]
    rows = couple.shape[0]
    half = rows // 2
    cells = near.shape[1]
    for e in range(entries):
        seen[route[e]] = 0
    for e in range(entries):
        to = route[e]
        rank = seen[to]
        seen[to] = rank + 1
        slots[e] = to * 2 + rank

    part = mm(parts(couple[...], 3), state[...])
    part = part[:rows] + part[rows : 2 * rows] + part[2 * rows :]
    mixed[...] = jnp.zeros(mixed.shape, F32)
    shares[...] = jnp.zeros(shares.shape, F32)
    low = iota((half, LANES), 1) < TILE
    for i in range(state.shape[1] // LANES):
        here = part[:, i * LANES : (i + 1) * LANES]
        there = pltpu.roll(here, TILE, 1)
        one = jnp.where(low, here[:half], there[half:])
        two = jnp.where(low, there[:half], here[half:])
        for q in range(half):
            at = slice(q * LANES, (q + 1) * LANES)
            mixed[2 * i : 2 * i + 1, at] = one[q : q + 1]
            mixed[2 * i + 1 : 2 * i + 2, at] = two[q : q + 1]
        here = frac[i : i + 1, :]
        there = pltpu.roll(here, TILE, 1)
        shares[2 * i : 2 * i + 1, :] = jnp.where(low[:1], here, there)
        shares[2 * i + 1 : 2 * i + 2, :] = jnp.where(low[:1], there, here)

    low = iota((16, LANES), 1) < TILE
    for j in range(entries // 2):
        owner = jnp.where(low, src[2 * j], src[2 * j + 1])
        chosen[:, j * LANES : (j + 1) * LANES] = (iota((16, LANES), 0) == owner).astype(F32)

    def counts(place):
        total = jnp.zeros(place.shape, F32)
        for k in range(near.shape[0]):
            total = total + (near[k : k + 1, :] == place).astype(F32)
        return total

    place = iota((16, cells), 0)

    @pl.loop(0, cells // 16)
    def _(i):
        at = pl.multiple_of(i * 16, 16)
        own[pl.ds(at, 16), :] = counts(place + (at + HALO)).astype(BF16)

    sea = line(mask[...].astype(F32))

    @pl.loop(0, HALO // 16)
    def _(i):
        at = pl.multiple_of(i * 16, 16)
        edge[pl.ds(at, 16), :] = (sea * counts(place + at)).astype(BF16)
        edge[pl.ds(at + HALO, 16), :] = (sea * counts(place + (at + HALO + cells))).astype(BF16)


def merge_kernel(heat_coef, got, mixed, shares, fluxes, back, flat):
    half = mixed.shape[1] // LANES
    peers = back.shape[0]
    pitch = 2 * (half + 1)
    flat[...] = got[...].astype(F32)
    row = lambda rank, q: flat[pl.ds(rank * (half + 1) + q, peers, stride=pitch), :]
    first, second = row(0, half), row(1, half)
    named = jnp.concatenate([first, second], axis=0).astype(BF16)
    pick = (iota((16, LANES), 1) == 0).astype(F32).astype(BF16)
    ids = lax.dot_general(pick, named, (((1,), (1,)), ((), ())), preferred_element_type=F32)
    member = (ids == (iota(ids.shape, 0) + 1).astype(F32)).astype(F32).astype(BF16)
    values = jnp.concatenate(
        [jnp.concatenate([row(0, q), row(1, q)], axis=0) for q in range(half)], axis=1
    ).astype(BF16)
    remap = mm(member, values)
    low = iota((1, LANES), 1) < TILE
    heat = jnp.zeros((16, LANES), F32)
    for q in range(half):
        at = slice(q * LANES, (q + 1) * LANES)
        flux = ((mixed[:, at] - remap[:, at]) * shares[...]).astype(BF16).astype(F32)
        fluxes[:, at] = flux
        heat = heat + flux * jnp.where(low, heat_coef[q], heat_coef[q + half])
    heat = heat + pltpu.roll(heat, TILE, 1)
    high = heat.astype(BF16).astype(F32)
    heat = jnp.concatenate([high, heat - high], axis=0)
    blank = jnp.zeros((32, LANES), F32)
    spread = jnp.concatenate(
        [jnp.where(low, heat, 0.0), blank, jnp.where(low, 0.0, heat), blank], axis=0
    ).astype(BF16)
    lane = iota((peers, LANES), 1)
    target = jnp.where((lane & (TILE - 1)) < 32, (lane & 15) + 1, -1).astype(F32)
    asked = jnp.where(lane < TILE, first, second)
    back[...] = mm((asked == target).astype(F32).astype(BF16), spread).reshape(back.shape)


def base_kernel(kappa, tracer, mask, own, base, edges, depth, rate):
    levels, cells = tracer.shape
    sea = line(mask[...].astype(F32))
    value = tracer[...]
    masked = value * sea
    pad = jnp.zeros((32 - levels, cells), F32)
    near = mm(parts(jnp.concatenate([masked, pad], axis=0), 2), own[...])
    near = (near[:32] + near[32:])[:levels]
    speed = column(kappa, levels, levels)
    rate[...] = speed
    depth[...] = jnp.exp(-iota((levels, LANES), 0).astype(F32) / 10.0)
    base[...] = value + sea * (across(speed, cells) * (near - 6.0 * value))
    edges[...] = jnp.concatenate([masked[:, cells - HALO :], masked[:, :HALO]], axis=1)


def heat_kernel(slots, got, chosen, flipped, mask, edges, depth, heat, forced):
    entries = slots.shape[0]
    cells = heat.shape[1]
    low = iota((1, LANES), 1) < TILE
    pieces = []
    for j in range(entries // 2):
        one, two = slots[2 * j], slots[2 * j + 1]
        a, b = got[one >> 1], got[two >> 1]
        a = jnp.where((one & 1) == 0, a, pltpu.roll(a, TILE, 1))
        b = jnp.where((two & 1) == 1, b, pltpu.roll(b, TILE, 1))
        pieces.append(jnp.where(low, a, b))
    found = jnp.concatenate(pieces, axis=1)
    high = found.astype(BF16).astype(F32)
    pick = chosen[...]
    spread = jnp.concatenate([pick * high, pick * (found - high)], axis=0).astype(BF16)
    summed = mm(spread, flipped[...])
    summed = summed[:16] + summed[16:]
    row = jnp.concatenate([summed[t : t + 1, :] for t in range(cells // TILE)], axis=1)
    row = row * line(mask[...].astype(F32))
    heat[...] = row
    ends = jnp.concatenate([row[:, cells - HALO :], row[:, :HALO]], axis=1)
    forced[...] = edges[...] + depth[...] * ends


def partial_kernel(heat, own, base, mask, depth, rate, fluxes, out, placed):
    half = placed.shape[0] // 2
    low = iota((half, LANES), 1) < TILE
    for i in range(placed.shape[1] // LANES):
        piece = lambda t: jnp.concatenate(
            [fluxes[t : t + 1, q * LANES : (q + 1) * LANES] for q in range(half)], axis=0
        )
        one, two = piece(2 * i), piece(2 * i + 1)
        block = jnp.concatenate(
            [
                jnp.where(low, one, pltpu.roll(two, TILE, 1)),
                jnp.where(low, pltpu.roll(one, TILE, 1), two),
            ],
            axis=0,
        )
        placed[:, i * LANES : (i + 1) * LANES] = block.astype(BF16)
    levels, cells = base.shape
    sea = line(mask[...].astype(F32))
    row = heat[...]
    high = row.astype(BF16).astype(F32)
    rows = jnp.concatenate([high, row - high, jnp.zeros((14, cells), F32)], axis=0)
    near = mm(rows.astype(BF16), own[...])
    near = sea * (near[0:1] + near[1:2] - 6.0 * row)
    out[...] = base[...] + across(depth[...], cells) * (row + across(rate[...], cells) * near)


def finish_kernel(before, after, edge, part, rate, out):
    levels = part.shape[0]
    low = iota((levels, LANES), 1) < TILE
    halo = jnp.where(low, before[...], after[...]) * rate[...]
    pad = jnp.zeros((32 - levels, LANES), F32)
    near = mm(parts(jnp.concatenate([halo, pad], axis=0), 2), edge[...])
    out[...] = part[...] + (near[:32] + near[32:])[:levels]


def call(kernel, out_shape, in_specs, out_specs, scratch=(), flops=1_000_000, vmem=24 * 2**20):
    return pl.pallas_call(
        kernel,
        out_shape=out_shape,
        in_specs=in_specs,
        out_specs=out_specs,
        scratch_shapes=list(scratch),
        cost_estimate=pl.CostEstimate(flops=flops, bytes_accessed=2_000_000, transcendentals=0),
        compiler_params=pltpu.CompilerParams(vmem_limit_bytes=vmem),
    )


def shards(
    ocean_fields,
    ocean_mask,
    entry_src,
    entry_route,
    entry_tile,
    weight_tiles,
    atm_state,
    atm_frac,
    couple,
    heat_coef,
    kappa,
    tracer,
    neighbours,
):
    fields, cells = ocean_fields.shape
    entries = entry_src.shape[0]
    atm_cells = atm_state.shape[1]
    rows = couple.shape[0]
    levels = tracer.shape[0]
    peers = lax.axis_size("blk")
    shape = jax.ShapeDtypeStruct
    half = rows // 2
    mask = ocean_mask.reshape(cells // LANES, LANES)
    route = entry_route.reshape(entries)
    pitch = 2 * (half + 1)
    i32 = jnp.int32
    sent = call(
        pack_kernel,
        shape((peers * pitch, LANES), BF16),
        [HBM] * 7,
        VMEM,
        [
            pltpu.SMEM((entries,), i32),
            pltpu.SMEM((entries,), i32),
            pltpu.SMEM((entries,), i32),
            pltpu.VMEM((fields, cells), BF16),
            pltpu.VMEM((cells // LANES, LANES), i32),
            pltpu.VMEM((rows, fields), F32),
            pltpu.VMEM((entries, TILE * TILE), BF16),
            pltpu.VMEM((cells // TILE, 4 * rows, TILE // 2), BF16),
            pltpu.VMEM((entries * PITCH, LANES), F32),
            pltpu.VMEM((peers * pitch, LANES), F32),
            pltpu.SMEM((peers,), i32),
            pltpu.SemaphoreType.DMA((7,)),
        ],
        vmem=64 * 2**20,
    )(entry_src, route, entry_tile, ocean_fields, mask, couple, weight_tiles)
    sent, weight_tiles, neighbours, atm_state = lax.optimization_barrier(
        (sent, weight_tiles, neighbours, atm_state)
    )
    got = lax.all_to_all(
        sent.reshape(peers, half + 1, 2, LANES), "blk", split_axis=0, concat_axis=0, tiled=True
    ).reshape(peers * pitch, LANES)
    own, edge, mixed, shares, chosen, slots = call(
        tables_kernel,
        (
            shape((cells, cells), BF16),
            shape((2 * HALO, cells), BF16),
            shape((16, half * LANES), F32),
            shape((16, LANES), F32),
            shape((16, entries * TILE), F32),
            shape((entries,), i32),
        ),
        [SMEM, SMEM, VMEM, VMEM, VMEM, VMEM, VMEM],
        (VMEM, VMEM, VMEM, VMEM, VMEM, SMEM),
        [pltpu.SMEM((peers,), i32)],
        flops=1_000_000_000,
    )(
        entry_src,
        route,
        neighbours,
        atm_state,
        atm_frac.reshape(atm_cells // LANES, LANES),
        mask,
        couple,
    )
    base, edges, depth, rate = call(
        base_kernel,
        (
            shape((levels, cells), F32),
            shape((levels, 2 * HALO), F32),
            shape((levels, LANES), F32),
            shape((levels, LANES), F32),
        ),
        [SMEM, VMEM, VMEM, VMEM],
        (VMEM,) * 4,
        flops=1_000_000_000,
    )(kappa, tracer, mask, own)
    flipped = weight_tiles.reshape(entries, TILE, TILE).transpose(0, 2, 1)
    flipped = flipped.reshape(entries * TILE, TILE)
    got, mixed, base, edges, flipped, own = lax.optimization_barrier(
        (got, mixed, base, edges, flipped, own)
    )
    fluxes, back = call(
        merge_kernel,
        (shape((16, half * LANES), F32), shape((peers, 1, LANES), F32)),
        [SMEM, VMEM, VMEM, VMEM],
        (VMEM, VMEM),
        [pltpu.VMEM((peers * pitch, LANES), F32)],
    )(heat_coef, got, mixed, shares)
    returned = lax.all_to_all(back, "blk", split_axis=0, concat_axis=0, tiled=True)
    heat, forced = call(
        heat_kernel,
        (shape((1, cells), F32), shape((levels, 2 * HALO), F32)),
        [SMEM] + [VMEM] * 6,
        (VMEM, VMEM),
    )(slots, returned, chosen, flipped, mask, edges, depth)
    count = lax.axis_size(("grp", "blk"))
    up = [(i, (i + 1) % count) for i in range(count)]
    down = [(target, source) for source, target in up]
    before = lax.ppermute(forced, ("grp", "blk"), up)
    after = lax.ppermute(forced, ("grp", "blk"), down)
    part, fluxes = call(
        partial_kernel,
        (shape((levels, cells), F32), shape((rows, atm_cells), BF16)),
        [VMEM] * 7,
        (VMEM, VMEM),
        flops=100_000_000,
    )(heat, own, base, mask, depth, rate, fluxes)
    tracer_out = call(finish_kernel, shape((levels, cells), F32), [VMEM] * 5, VMEM)(
        before, after, edge, part, rate
    )
    return (fluxes, tracer_out)


def solution(mesh):
    split = ("grp", "blk")
    return jax.shard_map(
        shards,
        mesh=mesh,
        in_specs=(
            P(None, split),
            P(split),
            P(split),
            P(split, None),
            P(split),
            P(split, None),
            P(None, split),
            P(split),
            P(),
            P(),
            P(),
            P(None, split),
            P(None, split),
        ),
        out_specs=(P(None, split), P(None, split)),
        check_vma=False,
    )
```

time: 75.7 us -> 70 us (0.925)
  blocking collectives: 0 us -> 18.5 us
  waiting for transfers between devices: 28.5 us -> 14.5 us
  starting transfers between devices: 28.1 us -> 23 us
  local copies, waits for them, and re-layouts: 5.87 us -> 1.62 us
    all_to_all x0 -> x1, blocking collectives: none -> 18.5 us  [shards(): lax.all_to_all(back, 'blk', split_axis=0, concat_axis=0, tiled=True)]
    all_to_all x2 -> x1, waiting for transfers between devices: 18.4 us -> 5.17 us  [shards(): lax.all_to_all(sent.reshape(peers, half + 1, 2, LANES), 'blk', split_axis...]
    all_to_all x2 -> x1, starting transfers between devices: 22.3 us -> 17.2 us  [shards(): lax.all_to_all(sent.reshape(peers, half + 1, 2, LANES), 'blk', split_axis...]
    unnamed x28 -> x20, local copies, waits for them, and re-layouts: 3.58 us -> 0.06 us
    ppermute x1, waiting for transfers between devices: 10.1 us -> 9.29 us  [shards(): before = lax.ppermute(forced, ('grp', 'blk'), up)]
    reshape x3 -> x2, local copies, waits for them, and re-layouts: 2.06 us -> 1.56 us  [shards(): flipped = weight_tiles.reshape(entries, TILE, TILE).transpose(0, 2, 1)]
  transfers between devices with their start and end apart: 4 -> 3, of which waited for: 3 -> 2; matrix products, arithmetic and copies ran while one was open for 0% -> 2% of each run, Pallas kernels for 8% -> 9%
where the time goes in v2:
time: 70 us; the launch traced here: 69.6 us
  starting transfers between devices  23 us (33%)
  blocking collectives  18.5 us (26%)
  waiting for transfers between devices  14.5 us (21%)
  Pallas kernels  11.2 us (16%)
  local copies, waits for them, and re-layouts  1.62 us (2%)
  between operations  0.85 us (1%)
    all_to_all x1, blocking collectives, shards(): lax.all_to_all(back, 'blk', split_axis=0, concat_axis=0, tiled=True)  18.5 us
    all_to_all x1, starting transfers between devices, shards(): lax.all_to_all(sent.reshape(peers, half + 1, 2, LANES), 'blk', split_axis...  17.2 us
    ppermute x1, waiting for transfers between devices, shards(): before = lax.ppermute(forced, ('grp', 'blk'), up)  9.29 us
    all_to_all x1, waiting for transfers between devices, shards(): lax.all_to_all(sent.reshape(peers, half + 1, 2, LANES), 'blk', split_axis...  5.17 us
    pallas_call x1, Pallas kernels, shards(): call(tables_kernel, (shape((cells, cells), BF16), shape((2 * HALO, cells)...  4.33 us
    ppermute x1, starting transfers between devices, shards(): after = lax.ppermute(forced, ('grp', 'blk'), down)  3.35 us
    ppermute x1, starting transfers between devices, shards(): before = lax.ppermute(forced, ('grp', 'blk'), up)  2.49 us
    pallas_call x1, Pallas kernels, shards(): call(pack_kernel, shape((peers * pitch, LANES), BF16), [HBM] * 7, VMEM, [...  2.27 us
  transfers between devices with their start and end apart: 3, of which 2 were waited for; matrix products, arithmetic and copies ran while one was open for 2% of the time, Pallas kernels for 9%

profile of v2, /device:TPU:16, one launch (start us, length us, event | category | flops | bytes accessed | tf_op | source)
XLA Modules:
  0.0 69.6 jit_solution(7051079755349395057)
XLA Ops:
  0.6 2.3 %shard_map.140 = bf16[640,128]{1,0:T(8,128)(2,1)} custom-call(s32[24]{0:T(128)} %src.1, s32[24]{0:T(128)} %bitcast.15, s32[24]{0:T(128)} %tile_hbm.1, bf16[40,896]{1,0:T(8,128)(2,1)} %fields_hbm.1, s32[7,128]{1,0:T(8,128)} %bitcast.10, f32[8,40]{1,0:T(8,128)} %couple.1, bf16[24,4096]{1,0:T(8,128)(2,1)} %weights_hbm.1), custom_call_target="tpu_custom_call" | custom-call | flops 1000000 | bytes 2000000 | tf_op jit(solution)/shard_map/pallas_call | solution.py:329
  2.9 0.0 copy-start
  2.9 0.0 copy-start.1
  2.9 0.0 copy-start.3
  2.9 0.0 copy-start.4
  3.0 0.0 copy-start.6
  3.0 0.0 copy-start.7
  3.0 0.0 copy-start.8
  3.0 17.2 %all-to-all-start = ((bf16[64,5,2,128]{3,2,1,0:T(2,128)(2,1)}), bf16[64,5,2,128]{3,2,1,0:T(2,128)(2,1)S(1)}, u32[]{:S(2)}, u32[]{:S(2)}) async-start(bf16[64,5,2,128]{3,2,1,0:T(2,128)(2,1)} %bitcast.18), calls=%async_computation | async-start | bytes 327680 | tf_op jit(solution)/shard_map/all_to_all | solution.py:353
  20.2 1.3 %reshape.30 = bf16[24,64,64]{2,1,0:T(8,128)(2,1)S(1)} reshape(bf16[24,4096]{1,0:T(8,128)(2,1)} %weights_hbm.1) | data formatting | bytes 393216 | tf_op jit(solution)/shard_map/reshape | solution.py:391
  21.5 0.2 copy.15
  21.7 0.0 copy-done
  21.8 0.0 copy-done.1
  21.8 0.0 copy-done.3
  21.8 0.0 copy-done.4
  21.8 0.0 copy-done.6
  21.8 0.0 copy-done.7
  21.8 0.0 copy-done.8
  21.8 0.0 copy-start.5
  21.8 0.0 copy-start.9
  21.8 4.3 %shard_map.141 = (bf16[896,896]{1,0:T(8,128)(2,1)S(1)}, bf16[128,896]{1,0:T(8,128)(2,1)S(1)}, f32[16,512]{1,0:T(8,128)S(1)}, f32[16,128]{1,0:T(8,128)S(1)}, f32[16,1536]{1,0:T(8,128)S(1)}, /*index=5*/s32[24]{0:T(128)S(1)}) custom-call(s32[24]{0:T(128)S(1)} %copy-done.3, s32[24]{0:T(128)S(1)} %bitcast.16, s32[6,896]{1,0:T(8,128)S(1)} %copy-done.7, ...), custom_call_target="tpu_custom_call" | custom-call | flops 1000000000 | bytes 2000000 | tf_op jit(solution)/shard_map/pallas_call | solution.py:356
  26.2 0.0 copy-done.5
  26.2 0.0 copy-done.9
  26.2 0.0 copy-start.2
  26.2 0.9 %shard_map.142 = (f32[30,896]{1,0:T(8,128)S(1)}, f32[30,128]{1,0:T(8,128)S(1)}, f32[30,128]{1,0:T(8,128)S(1)}, f32[30,128]{1,0:T(8,128)S(1)}) custom-call(f32[30]{0:T(128)S(1)} %copy-done.9, f32[30,896]{1,0:T(8,128)S(1)} %copy-done.5, s32[7,128]{1,0:T(8,128)S(1)} %bitcast.12, bf16[896,896]{1,0:T(8,128)(2,1)S(1)} %get-tuple-element.46.own), custom_call_target="tpu_custom_call" | custom-call | flops 1000000000 | bytes 2000000 | tf_op jit(solution)/shard_map/pallas_call | solution.py:379
  27.1 5.2 %all-to-all-done = bf16[64,5,2,128]{3,2,1,0:T(2,128)(2,1)S(1)} async-done(((bf16[64,5,2,128]{3,2,1,0:T(2,128)(2,1)}), bf16[64,5,2,128]{3,2,1,0:T(2,128)(2,1)S(1)}, u32[]{:S(2)}, u32[]{:S(2)}) %all-to-all-start) | async-done | bytes 163872 | tf_op jit(solution)/shard_map/all_to_all | solution.py:353
  32.3 0.0 copy-done.2
  32.3 1.1 %shard_map.143 = (f32[16,512]{1,0:T(8,128)S(1)}, f32[64,1,128]{2,1,0:T(1,128)S(1)}) custom-call(f32[8]{0:T(128)S(1)} %copy-done.2, bf16[640,128]{1,0:T(8,128)(2,1)S(1)} %bitcast.9, f32[16,512]{1,0:T(8,128)S(1)} %get-tuple-element.38.mixed, f32[16,128]{1,0:T(8,128)S(1)} %get-tuple-element.39.shares), custom_call_target="tpu_custom_call" | custom-call | flops 1000000 | bytes 2000000 | tf_op jit(solution)/shard_map/pallas_call | solution.py:396
  33.4 18.5 %all_to_all.10.got = f32[64,1,128]{2,1,0:T(1,128)S(1)} all-to-all(f32[64,1,128]{2,1,0:T(1,128)S(1)} %get-tuple-element.40), channel_id=1, replica_groups=mesh['grp'=16,'blk'=64] {'blk'}, dimensions={0} | all-to-all | bytes 65536 | tf_op jit(solution)/shard_map/all_to_all | solution.py:403
  51.8 0.9 %shard_map.144 = (f32[1,896]{1,0:T(1,128)S(1)}, f32[30,128]{1,0:T(8,128)S(1)}) custom-call(s32[24]{0:T(128)S(1)} %get-tuple-element.30.slots, f32[64,1,128]{2,1,0:T(1,128)S(1)} %all_to_all.10.got, f32[16,1536]{1,0:T(8,128)S(1)} %get-tuple-element.41.chosen, bf16[1536,64]{1,0:T(8,128)(2,1)S(1)} %bitcast.8, s32[7,128]{1,0:T(8,128)S(1)} %bitcast.13, ...), custom_call_target="tpu_custom_call" | custom-call | flops 1000000 | bytes 2000000 | tf_op jit(solution)/shard_map/pallas_call | solution.py:404
  52.8 3.4 %collective-permute-start.1 = (f32[30,128]{1,0:T(8,128)S(1)}, f32[30,128]{1,0:T(8,128)S(1)}, u32[]{:S(2)}, u32[]{:S(2)}) collective-permute-start(f32[30,128]{1,0:T(8,128)S(1)} %get-tuple-element.51), channel_id=1, source_target_pairs={{1,0},{2,1},{3,2},{4,3},{5,4},{6,5},{7,6},{8,7},{9,8},{10,9},{11,1... | collective-permute-start | bytes 46088 | tf_op jit(solution)/shard_map/ppermute | solution.py:414
  56.1 2.5 %collective-permute-start = (f32[30,128]{1,0:T(8,128)S(1)}, f32[30,128]{1,0:T(8,128)S(1)}, u32[]{:S(2)}, u32[]{:S(2)}) collective-permute-start(f32[30,128]{1,0:T(8,128)S(1)} %get-tuple-element.51), channel_id=1, source_target_pairs={{0,1},{1,2},{2,3},{3,4},{4,5},{5,6},{6,7},{7,8},{8,9},{9,10},{10,1... | collective-permute-start | bytes 46088 | tf_op jit(solution)/shard_map/ppermute | solution.py:413
  58.6 0.9 %shard_map.145 = (f32[30,896]{1,0:T(8,128)S(1)}, bf16[8,768]{1,0:T(8,128)(2,1)}) custom-call(f32[1,896]{1,0:T(1,128)S(1)} %get-tuple-element.45.heat, bf16[896,896]{1,0:T(8,128)(2,1)S(1)} %get-tuple-element.46.own, f32[30,896]{1,0:T(8,128)S(1)} %get-tuple-element.47.base, s32[7,128]{1,0:T(8,128)S(1)} %bitcast.14, f32[30,128]{1,0:T(8,128)S(1)} %get-tuple-element.44.depth, ...), custom_call_target="tpu_custom_call" | custom-call | flops 100000000 | bytes 2000000 | tf_op jit(solution)/shard_map/pallas_call | solution.py:415
  59.5 0.0 collective-permute-done.1.after
  59.5 9.3 %collective-permute-done.before = f32[30,128]{1,0:T(8,128)S(1)} collective-permute-done((f32[30,128]{1,0:T(8,128)S(1)}, f32[30,128]{1,0:T(8,128)S(1)}, u32[]{:S(2)}, u32[]{:S(2)}) %collective-permute-start) | collective-permute-done | bytes 15392 | tf_op jit(solution)/shard_map/ppermute | solution.py:413
  68.8 0.8 %shard_map.146 = f32[30,896]{1,0:T(8,128)} custom-call(f32[30,128]{1,0:T(8,128)S(1)} %collective-permute-done.before, f32[30,128]{1,0:T(8,128)S(1)} %collective-permute-done.1.after, bf16[128,896]{1,0:T(8,128)(2,1)S(1)} %get-tuple-element.52.edge, f32[30,896]{1,0:T(8,128)S(1)} %get-tuple-element.53.part, f32[30,128]{1,0:T(8,128)S(1)} %get-tuple-element.48.rate), custom_call_target="tpu_custom_call" | custom-call | flops 1000000 | bytes 2000000 | tf_op jit(solution)/shard_map/pallas_call | solution.py:422
Async XLA Ops:
  2.9 18.8 %copy-start = (s32[896]{0:T(1024)S(1)}, s32[896]{0:T(1024)}, u32[]{:S(2)}) copy-start(s32[896]{0:T(1024)} %param.14) | copy-start | bytes 10756
  2.9 18.8 %copy-start.1 = (f32[8,40]{1,0:T(8,128)S(1)}, f32[8,40]{1,0:T(8,128)}, u32[]{:S(2)}) copy-start(f32[8,40]{1,0:T(8,128)} %couple.1) | copy-start | bytes 3844
  2.9 18.8 %copy-start.3 = (s32[24]{0:T(128)S(1)}, s32[24]{0:T(128)}, u32[]{:S(2)}) copy-start(s32[24]{0:T(128)} %src.1) | copy-start | bytes 292
  2.9 18.8 %copy-start.4 = (s32[24,1]{0,1:T(1,128)S(1)}, s32[24,1]{0,1:T(1,128)}, u32[]{:S(2)}) copy-start(s32[24,1]{0,1:T(1,128)} %param.16) | copy-start | bytes 292
  3.0 18.8 %copy-start.6 = (bf16[40,768]{1,0:T(8,128)(2,1)S(1)}, bf16[40,768]{1,0:T(8,128)(2,1)}, u32[]{:S(2)}) copy-start(bf16[40,768]{1,0:T(8,128)(2,1)} %state) | copy-start | bytes 184324
  3.0 18.8 %copy-start.7 = (s32[6,896]{1,0:T(8,128)S(1)}, s32[6,896]{1,0:T(8,128)}, u32[]{:S(2)}) copy-start(s32[6,896]{1,0:T(8,128)} %near) | copy-start | bytes 64516
  3.0 18.8 %copy-start.8 = (f32[768]{0:T(1024)S(1)}, f32[768]{0:T(1024)}, u32[]{:S(2)}) copy-start(f32[768]{0:T(1024)} %param.20) | copy-start | bytes 9220
  3.0 29.3 %all-to-all-start = ((bf16[64,5,2,128]{3,2,1,0:T(2,128)(2,1)}), bf16[64,5,2,128]{3,2,1,0:T(2,128)(2,1)S(1)}, u32[]{:S(2)}, u32[]{:S(2)}) async-start(bf16[64,5,2,128]{3,2,1,0:T(2,128)(2,1)} %bitcast.18), calls=%async_computation | async-start | bytes 327680 | tf_op jit(solution)/shard_map/all_to_all | solution.py:353
  21.8 4.4 %copy-start.5 = (f32[30,896]{1,0:T(8,128)S(1)}, f32[30,896]{1,0:T(8,128)}, u32[]{:S(2)}) copy-start(f32[30,896]{1,0:T(8,128)} %tracer.1) | copy-start | bytes 322564
  21.8 4.4 %copy-start.9 = (f32[30]{0:T(128)S(1)}, f32[30]{0:T(128)}, u32[]{:S(2)}) copy-start(f32[30]{0:T(128)} %kappa.1) | copy-start | bytes 364
  26.2 6.1 %copy-start.2 = (f32[8]{0:T(128)S(1)}, f32[8]{0:T(128)}, u32[]{:S(2)}) copy-start(f32[8]{0:T(128)} %heat_coef.1) | copy-start | bytes 100
  52.8 6.7 %collective-permute-start.1 = (f32[30,128]{1,0:T(8,128)S(1)}, f32[30,128]{1,0:T(8,128)S(1)}, u32[]{:S(2)}, u32[]{:S(2)}) collective-permute-start(f32[30,128]{1,0:T(8,128)S(1)} %get-tuple-element.51), channel_id=1, source_target_pairs={{1,0},{2,1},{3,2},{4,3},{5,4},{6,5},{7,6},{8,7},{9,8},{10,9},{11,1... | collective-permute-start | bytes 46088 | tf_op jit(solution)/shard_map/ppermute | solution.py:414
  56.1 12.7 %collective-permute-start = (f32[30,128]{1,0:T(8,128)S(1)}, f32[30,128]{1,0:T(8,128)S(1)}, u32[]{:S(2)}, u32[]{:S(2)}) collective-permute-start(f32[30,128]{1,0:T(8,128)S(1)} %get-tuple-element.51), channel_id=1, source_target_pairs={{0,1},{1,2},{2,3},{3,4},{4,5},{5,6},{6,7},{7,8},{8,9},{9,10},{10,1... | collective-permute-start | bytes 46088 | tf_op jit(solution)/shard_map/ppermute | solution.py:413

commit v3 on v2

--- a/solution.py
+++ b/solution.py
@@ -117,21 +117,40 @@
     out[...] = slots[...].astype(BF16)
 
 
-def tables_kernel(
-    src, route, near, state, frac, mask, couple, own, edge, mixed, shares, chosen, slots, seen
-):
+def ship_kernel(src, route, flipped, tracer, mask, out, seen):
     entries = src.shape[0]
-    rows = couple.shape[0]
-    half = rows // 2
-    cells = near.shape[1]
+    levels, cells = tracer.shape
+    half = entries * TILE // 2
     for e in range(entries):
         seen[route[e]] = 0
+    slots = []
     for e in range(entries):
         to = route[e]
         rank = seen[to]
         seen[to] = rank + 1
-        slots[e] = to * 2 + rank
-
+        slots.append(to * 2 + rank)
+    out[:half, :] = jnp.concatenate([flipped[:half, :], flipped[half:, :]], axis=1)
+    ends = lambda x: jnp.concatenate([x[:, cells - HALO :], x[:, :HALO]], axis=1)
+    sea = ends(line(mask[...].astype(F32)))
+    edge = ends(tracer[...]) * sea
+    out[half : half + 32, :] = jnp.concatenate(
+        [edge, jnp.broadcast_to(sea, (32 - levels, LANES))], axis=0
+    ).astype(BF16)
+    where = iota((32, LANES), 0)
+    slot_rows = jnp.full((32, LANES), -1, jnp.int32)
+    tile_rows = jnp.full((32, LANES), -1, jnp.int32)
+    for e in range(entries):
+        here = where == (e // 2 + 16 * (e % 2))
+        slot_rows = jnp.where(here, slots[e], slot_rows)
+        tile_rows = jnp.where(here, src[e], tile_rows)
+    out[half + 32 : half + 64, :] = slot_rows.astype(F32).astype(BF16)
+    out[half + 64 : half + 96, :] = tile_rows.astype(F32).astype(BF16)
+
+
+def tables_kernel(src, state, frac, couple, mixed, shares, chosen):
+    entries = src.shape[0]
+    rows = couple.shape[0]
+    half = rows // 2
     part = mm(parts(couple[...], 3), state[...])
     part = part[:rows] + part[rows : 2 * rows] + part[2 * rows :]
     mixed[...] = jnp.zeros(mixed.shape, F32)
@@ -156,31 +175,10 @@
         owner = jnp.where(low, src[2 * j], src[2 * j + 1])
         chosen[:, j * LANES : (j + 1) * LANES] = (iota((16, LANES), 0) == owner).astype(F32)
 
-    def counts(place):
-        total = jnp.zeros(place.shape, F32)
-        for k in range(near.shape[0]):
-            total = total + (near[k : k + 1, :] == place).astype(F32)
-        return total
-
-    place = iota((16, cells), 0)
-
-    @pl.loop(0, cells // 16)
-    def _(i):
-        at = pl.multiple_of(i * 16, 16)
-        own[pl.ds(at, 16), :] = counts(place + (at + HALO)).astype(BF16)
-
-    sea = line(mask[...].astype(F32))
-
-    @pl.loop(0, HALO // 16)
-    def _(i):
-        at = pl.multiple_of(i * 16, 16)
-        edge[pl.ds(at, 16), :] = (sea * counts(place + at)).astype(BF16)
-        edge[pl.ds(at + HALO, 16), :] = (sea * counts(place + (at + HALO + cells))).astype(BF16)
-
 
 def merge_kernel(heat_coef, got, mixed, shares, fluxes, back, flat):
     half = mixed.shape[1] // LANES
-    peers = back.shape[0]
+    peers = back.shape[0] // 4
     pitch = 2 * (half + 1)
     flat[...] = got[...].astype(F32)
     row = lambda rank, q: flat[pl.ds(rank * (half + 1) + q, peers, stride=pitch), :]
@@ -210,46 +208,116 @@
     lane = iota((peers, LANES), 1)
     target = jnp.where((lane & (TILE - 1)) < 32, (lane & 15) + 1, -1).astype(F32)
     asked = jnp.where(lane < TILE, first, second)
-    back[...] = mm((asked == target).astype(F32).astype(BF16), spread).reshape(back.shape)
-
-
-def base_kernel(kappa, tracer, mask, own, base, edges, depth, rate):
+    reply = mm((asked == target).astype(F32).astype(BF16), spread)
+    high = reply.astype(BF16).astype(F32)
+    four = (high, reply - high, pltpu.roll(high, 1, 0), pltpu.roll(high, peers - 1, 0))
+    for k, rows in enumerate(four):
+        flat[pl.ds(k, peers, stride=4), :] = rows
+    back[...] = flat[: 4 * peers, :].astype(BF16)
+
+
+def base_kernel(kappa, near, tracer, mask, own, edge, base, depth, speed, rate):
     levels, cells = tracer.shape
+    place = iota((LANES, cells), 0).astype(F32).astype(BF16)
+
+    def counts(start):
+        total = jnp.zeros(place.shape, BF16)
+        for k in range(near.shape[0]):
+            at = jnp.clip(near[k : k + 1, :] - start, -1, LANES).astype(F32).astype(BF16)
+            total = total + jnp.where(at == place, jnp.ones((), BF16), jnp.zeros((), BF16))
+        return total
+
+    @pl.loop(0, cells // LANES)
+    def _(i):
+        at = pl.multiple_of(i * LANES, LANES)
+        own[pl.ds(at, LANES), :] = counts(at + HALO)
+
     sea = line(mask[...].astype(F32))
+    land = sea.astype(BF16)
+    edge[:HALO, :] = (land * counts(0))[:HALO]
+    edge[HALO:, :] = (land * counts(cells + HALO))[:HALO]
+
     value = tracer[...]
-    masked = value * sea
     pad = jnp.zeros((32 - levels, cells), F32)
-    near = mm(parts(jnp.concatenate([masked, pad], axis=0), 2), own[...])
-    near = (near[:32] + near[32:])[:levels]
-    speed = column(kappa, levels, levels)
-    rate[...] = speed
-    depth[...] = jnp.exp(-iota((levels, LANES), 0).astype(F32) / 10.0)
-    base[...] = value + sea * (across(speed, cells) * (near - 6.0 * value))
-    edges[...] = jnp.concatenate([masked[:, cells - HALO :], masked[:, :HALO]], axis=1)
-
-
-def heat_kernel(slots, got, chosen, flipped, mask, edges, depth, heat, forced):
-    entries = slots.shape[0]
+    total = mm(parts(jnp.concatenate([value * sea, pad], axis=0), 2), own[...])
+    total = sea * ((total[:32] + total[32:])[:levels] - 6.0 * value)
+    pace = column(kappa, levels, levels)
+    deep = jnp.exp(-iota((levels, LANES), 0).astype(F32) / 10.0)
+    depth[...] = deep
+    speed[...] = pace
+    rate[...] = deep * pace
+    base[...] = value + across(pace, cells) * total
+
+
+def in_group(shape):
+    me = lax.axis_index("blk")
+    low = iota(shape, 1) < TILE
+    return jnp.where(low, me, lax.axis_size("blk") - 1 - me) > 0
+
+
+def heat_kernel(got, chosen, here, before, after, mask, depth, heat, forced, halo, flat):
     cells = heat.shape[1]
-    low = iota((1, LANES), 1) < TILE
-    pieces = []
-    for j in range(entries // 2):
-        one, two = slots[2 * j], slots[2 * j + 1]
-        a, b = got[one >> 1], got[two >> 1]
-        a = jnp.where((one & 1) == 0, a, pltpu.roll(a, TILE, 1))
-        b = jnp.where((two & 1) == 1, b, pltpu.roll(b, TILE, 1))
-        pieces.append(jnp.where(low, a, b))
-    found = jnp.concatenate(pieces, axis=1)
-    high = found.astype(BF16).astype(F32)
-    pick = chosen[...]
-    spread = jnp.concatenate([pick * high, pick * (found - high)], axis=0).astype(BF16)
-    summed = mm(spread, flipped[...])
-    summed = summed[:16] + summed[16:]
-    row = jnp.concatenate([summed[t : t + 1, :] for t in range(cells // TILE)], axis=1)
+    half = here.shape[0] - 96
+    lane = iota((32, LANES), 1)
+    target = ((lane & (TILE - 1)) * 2 + (lane >> 6)).astype(F32)
+    meta = lambda ref, at: ref[half + at : half + at + 32, :].astype(F32)
+    found = lambda ref: meta(ref, 32) == target
+    last = float(cells // TILE - 1)
+    picks = [
+        pick.astype(F32).astype(BF16)
+        for pick in (
+            found(here),
+            found(before) & (meta(before, 64) == last),
+            found(after) & (meta(after, 64) == 0.0),
+        )
+    ]
+    peers = got.shape[0] // 4
+    count = half // LANES
+    flat[...] = got[...].astype(F32)
+    low = iota((16, LANES), 1) < TILE
+
+    def lookup(k, which):
+        rows = flat[pl.ds(k, peers, stride=4), :]
+        turned = pltpu.roll(rows, TILE, 1)
+        one = jnp.concatenate([rows, turned], axis=0).astype(BF16)
+        two = jnp.concatenate([turned, rows], axis=0).astype(BF16)
+        return jnp.where(low, mm(picks[which][:16], one), mm(picks[which][16:], two))
+
+    def laid(rows, start):
+        return jnp.concatenate([rows[j : j + 1] for j in range(start, start + count)], axis=1)
+
+    high, rest = lookup(0, 0), lookup(1, 0)
+    previous, following = lookup(2, 1), lookup(3, 2)
+    spread = []
+    for h in range(2):
+        pick = chosen[:, h * half : (h + 1) * half]
+        for rows in (high, rest):
+            spread.append(pick * laid(rows, h * count))
+    summed = mm(jnp.concatenate(spread, axis=0).astype(BF16), here[:half, :])
+    summed = summed[:16] + summed[16:32] + pltpu.roll(summed[32:48] + summed[48:], TILE, 1)
+    blank = jnp.zeros((14, half), F32)
+
+    def side(rows, ref):
+        rows = jnp.concatenate([laid(rows, 0), laid(rows, count), blank], axis=0)
+        return mm(rows.astype(BF16), ref[:half, :])
+
+    left, right = side(previous, before), side(following, after)
+    left = left[0:1] + pltpu.roll(left, TILE, 1)[1:2]
+    right = right[1:2] + pltpu.roll(right, TILE, 1)[0:1]
+    levels = depth.shape[0]
+    coast = jnp.where(low[:1], meta(before, 0)[levels : levels + 1], meta(after, 0)[levels : levels + 1])
+    halo[...] = jnp.where(low[:1], left, right) * coast
+    row = jnp.concatenate([summed[t : t + 1, :TILE] for t in range(cells // TILE)], axis=1)
     row = row * line(mask[...].astype(F32))
     heat[...] = row
     ends = jnp.concatenate([row[:, cells - HALO :], row[:, :HALO]], axis=1)
-    forced[...] = edges[...] + depth[...] * ends
+    forced[...] = meta(here, 0)[:levels] + depth[...] * ends
+
+
+def halves(row):
+    high = row.astype(BF16).astype(F32)
+    blank = jnp.zeros((14, row.shape[1]), F32)
+    return jnp.concatenate([high, row - high, blank], axis=0).astype(BF16)
 
 
 def partial_kernel(heat, own, base, mask, depth, rate, fluxes, out, placed):
@@ -268,23 +336,27 @@
             axis=0,
         )
         placed[:, i * LANES : (i + 1) * LANES] = block.astype(BF16)
-    levels, cells = base.shape
+    cells = base.shape[1]
     sea = line(mask[...].astype(F32))
     row = heat[...]
-    high = row.astype(BF16).astype(F32)
-    rows = jnp.concatenate([high, row - high, jnp.zeros((14, cells), F32)], axis=0)
-    near = mm(rows.astype(BF16), own[...])
+    near = mm(halves(row), own[...])
     near = sea * (near[0:1] + near[1:2] - 6.0 * row)
-    out[...] = base[...] + across(depth[...], cells) * (row + across(rate[...], cells) * near)
-
-
-def finish_kernel(before, after, edge, part, rate, out):
-    levels = part.shape[0]
-    low = iota((levels, LANES), 1) < TILE
-    halo = jnp.where(low, before[...], after[...]) * rate[...]
+    out[...] = base[...] + across(depth[...], cells) * row + across(rate[...], cells) * near
+
+
+def finish_kernel(halo, swapped, before, after, edge, part, speed, rate, out):
+    levels, cells = part.shape
+    first = before.shape[0] - 96
+    rows = slice(first, first + 32)
+    low = iota((32, LANES), 1) < TILE
+    outer = jnp.where(low, before[rows, :].astype(F32), after[rows, :].astype(F32))[:levels]
+    outer = jnp.where(in_group((levels, LANES)), outer, swapped[...]) * speed[...]
     pad = jnp.zeros((32 - levels, LANES), F32)
-    near = mm(parts(jnp.concatenate([halo, pad], axis=0), 2), edge[...])
-    out[...] = part[...] + (near[:32] + near[32:])[:levels]
+    outer = parts(jnp.concatenate([outer, pad], axis=0), 2)
+    inner = halves(jnp.where(in_group((1, LANES)), halo[...], 0.0))
+    near = mm(jnp.concatenate([outer, inner], axis=0), edge[...])
+    inner = near[64:65] + near[65:66]
+    out[...] = part[...] + (near[:32] + near[32:64])[:levels] + across(rate[...], cells) * inner
 
 
 def call(kernel, out_shape, in_specs, out_specs, scratch=(), flops=1_000_000, vmem=24 * 2**20):
@@ -347,71 +419,71 @@
         ],
         vmem=64 * 2**20,
     )(entry_src, route, entry_tile, ocean_fields, mask, couple, weight_tiles)
-    sent, weight_tiles, neighbours, atm_state = lax.optimization_barrier(
-        (sent, weight_tiles, neighbours, atm_state)
+    sent, weight_tiles, neighbours, atm_state, tracer = lax.optimization_barrier(
+        (sent, weight_tiles, neighbours, atm_state, tracer)
     )
     got = lax.all_to_all(
         sent.reshape(peers, half + 1, 2, LANES), "blk", split_axis=0, concat_axis=0, tiled=True
     ).reshape(peers * pitch, LANES)
-    own, edge, mixed, shares, chosen, slots = call(
+    flipped = weight_tiles.reshape(entries, TILE, TILE).transpose(0, 2, 1)
+    here = call(
+        ship_kernel,
+        shape((entries * TILE // 2 + 96, LANES), BF16),
+        [SMEM, SMEM, VMEM, VMEM, VMEM],
+        VMEM,
+        [pltpu.SMEM((peers,), i32)],
+    )(entry_src, route, flipped.reshape(entries * TILE, TILE), tracer, mask)
+    axes = ("grp", "blk")
+    count = lax.axis_size(axes)
+    ring = [(i, (i + 1) % count) for i in range(count)]
+    up = [pair for pair in ring if pair[1] % peers]
+    seams = [pair for pair in ring if pair[1] % peers == 0]
+    down = [(target, source) for source, target in up]
+    before = lax.ppermute(here, axes, up)
+    after = lax.ppermute(here, axes, down)
+    mixed, shares, chosen = call(
         tables_kernel,
+        (
+            shape((16, half * LANES), F32),
+            shape((16, LANES), F32),
+            shape((16, entries * TILE), F32),
+        ),
+        [SMEM, VMEM, VMEM, VMEM],
+        (VMEM,) * 3,
+    )(entry_src, atm_state, atm_frac.reshape(atm_cells // LANES, LANES), couple)
+    fluxes, back = call(
+        merge_kernel,
+        (shape((16, half * LANES), F32), shape((peers * 4, LANES), BF16)),
+        [SMEM, VMEM, VMEM, VMEM],
+        (VMEM, VMEM),
+        [pltpu.VMEM((peers * pitch, LANES), F32)],
+    )(heat_coef, got, mixed, shares)
+    back, neighbours, tracer = lax.optimization_barrier((back, neighbours, tracer))
+    returned = lax.all_to_all(
+        back.reshape(peers, 2, 2, LANES), "blk", split_axis=0, concat_axis=0, tiled=True
+    ).reshape(peers * 4, LANES)
+    own, edge, base, depth, speed, rate = call(
+        base_kernel,
         (
             shape((cells, cells), BF16),
             shape((2 * HALO, cells), BF16),
-            shape((16, half * LANES), F32),
-            shape((16, LANES), F32),
-            shape((16, entries * TILE), F32),
-            shape((entries,), i32),
-        ),
-        [SMEM, SMEM, VMEM, VMEM, VMEM, VMEM, VMEM],
-        (VMEM, VMEM, VMEM, VMEM, VMEM, SMEM),
-        [pltpu.SMEM((peers,), i32)],
-        flops=1_000_000_000,
-    )(
-        entry_src,
-        route,
-        neighbours,
-        atm_state,
-        atm_frac.reshape(atm_cells // LANES, LANES),
-        mask,
-        couple,
-    )
-    base, edges, depth, rate = call(
-        base_kernel,
-        (
             shape((levels, cells), F32),
-            shape((levels, 2 * HALO), F32),
+            shape((levels, LANES), F32),
             shape((levels, LANES), F32),
             shape((levels, LANES), F32),
         ),
         [SMEM, VMEM, VMEM, VMEM],
-        (VMEM,) * 4,
+        (VMEM,) * 6,
         flops=1_000_000_000,
-    )(kappa, tracer, mask, own)
-    flipped = weight_tiles.reshape(entries, TILE, TILE).transpose(0, 2, 1)
-    flipped = flipped.reshape(entries * TILE, TILE)
-    got, mixed, base, edges, flipped, own = lax.optimization_barrier(
-        (got, mixed, base, edges, flipped, own)
-    )
-    fluxes, back = call(
-        merge_kernel,
-        (shape((16, half * LANES), F32), shape((peers, 1, LANES), F32)),
-        [SMEM, VMEM, VMEM, VMEM],
-        (VMEM, VMEM),
-        [pltpu.VMEM((peers * pitch, LANES), F32)],
-    )(heat_coef, got, mixed, shares)
-    returned = lax.all_to_all(back, "blk", split_axis=0, concat_axis=0, tiled=True)
-    heat, forced = call(
+    )(kappa, neighbours, tracer, mask)
+    heat, forced, halo = call(
         heat_kernel,
-        (shape((1, cells), F32), shape((levels, 2 * HALO), F32)),
-        [SMEM] + [VMEM] * 6,
-        (VMEM, VMEM),
-    )(slots, returned, chosen, flipped, mask, edges, depth)
-    count = lax.axis_size(("grp", "blk"))
-    up = [(i, (i + 1) % count) for i in range(count)]
-    down = [(target, source) for source, target in up]
-    before = lax.ppermute(forced, ("grp", "blk"), up)
-    after = lax.ppermute(forced, ("grp", "blk"), down)
+        (shape((1, cells), F32), shape((levels, LANES), F32), shape((1, LANES), F32)),
+        [VMEM] * 7,
+        (VMEM,) * 3,
+        [pltpu.VMEM((peers * 4, LANES), F32)],
+    )(returned, chosen, here, before, after, mask, depth)
+    swapped = lax.ppermute(forced, axes, seams + [(target, source) for source, target in seams])
     part, fluxes = call(
         partial_kernel,
         (shape((levels, cells), F32), shape((rows, atm_cells), BF16)),
@@ -419,8 +491,8 @@
         (VMEM, VMEM),
         flops=100_000_000,
     )(heat, own, base, mask, depth, rate, fluxes)
-    tracer_out = call(finish_kernel, shape((levels, cells), F32), [VMEM] * 5, VMEM)(
-        before, after, edge, part, rate
+    tracer_out = call(finish_kernel, shape((levels, cells), F32), [VMEM] * 8, VMEM)(
+        halo, swapped, before, after, edge, part, speed, rate
     )
     return (fluxes, tracer_out)
 

time: 70 us -> 64.6 us (0.923)
  the two profiles are of different devices: /device:TPU:16 before, /device:TPU:512 now
where the time goes in v3:
time: 64.6 us; the launch traced here: 64.2 us
  starting transfers between devices  29.9 us (46%)
  waiting for transfers between devices  21.7 us (34%)
  Pallas kernels  10 us (15%)
  local copies, waits for them, and re-layouts  1.65 us (3%)
  between operations  0.88 us (1%)
    all_to_all x1, starting transfers between devices, shards(): lax.all_to_all(sent.reshape(peers, half + 1, 2, LANES), 'blk', split_axis...  13.6 us
    all_to_all x1, waiting for transfers between devices, shards(): lax.all_to_all(back.reshape(peers, 2, 2, LANES), 'blk', split_axis=0, con...  9.85 us
    all_to_all x1, starting transfers between devices, shards(): lax.all_to_all(back.reshape(peers, 2, 2, LANES), 'blk', split_axis=0, con...  8.5 us
    ppermute x1, waiting for transfers between devices, shards(): lax.ppermute(forced, axes, seams + [(target, source) for source, target i...  7.67 us
    ppermute x1, starting transfers between devices, shards(): before = lax.ppermute(here, axes, up)  4.56 us
    all_to_all x1, waiting for transfers between devices, shards(): lax.all_to_all(sent.reshape(peers, half + 1, 2, LANES), 'blk', split_axis...  4.2 us
    pallas_call x1, Pallas kernels, shards(): call(base_kernel, (shape((cells, cells), BF16), shape((2 * HALO, cells),...  2.31 us
    pallas_call x1, Pallas kernels, shards(): call(pack_kernel, shape((peers * pitch, LANES), BF16), [HBM] * 7, VMEM, [...  2.26 us
  transfers between devices with their start and end apart: 5, of which 3 were waited for; matrix products, arithmetic and copies ran while one was open for 2% of the time, Pallas kernels for 10%

profile of v3, /device:TPU:512, one launch (start us, length us, event | category | flops | bytes accessed | tf_op | source)
XLA Modules:
  0.0 64.2 jit_solution(11887165092657129614)
XLA Ops:
  0.6 2.3 %shard_map.140 = bf16[640,128]{1,0:T(8,128)(2,1)} custom-call(s32[24]{0:T(128)} %src.3, s32[24]{0:T(128)} %bitcast.19, s32[24]{0:T(128)} %tile_hbm.1, bf16[40,896]{1,0:T(8,128)(2,1)} %fields_hbm.1, s32[7,128]{1,0:T(8,128)} %bitcast.13, f32[8,40]{1,0:T(8,128)} %couple.1, bf16[24,4096]{1,0:T(8,128)(2,1)} %weights_hbm.1), custom_call_target="tpu_custom_call" | custom-call | flops 1000000 | bytes 2000000 | tf_op jit(solution)/shard_map/pallas_call | solution.py:401
  2.9 0.0 copy-start
  2.9 0.0 copy-start.1
  2.9 0.0 copy-start.4
  2.9 0.0 copy-start.6
  3.0 0.0 copy-start.2
  3.0 0.0 copy-start.3
  3.0 0.0 copy-start.5
  3.0 0.0 copy-start.7
  3.0 0.0 copy-start.8
  3.0 0.0 copy-start.9
  3.0 13.6 %all-to-all-start = ((bf16[64,5,2,128]{3,2,1,0:T(2,128)(2,1)}), bf16[64,5,2,128]{3,2,1,0:T(2,128)(2,1)S(1)}, u32[]{:S(2)}, u32[]{:S(2)}) async-start(bf16[64,5,2,128]{3,2,1,0:T(2,128)(2,1)} %bitcast.21), calls=%async_computation | async-start | bytes 327680 | tf_op jit(solution)/shard_map/all_to_all | solution.py:425
  16.7 1.3 %reshape.38 = bf16[24,64,64]{2,1,0:T(8,128)(2,1)S(1)} reshape(bf16[24,4096]{1,0:T(8,128)(2,1)} %weights_hbm.1) | data formatting | bytes 393216 | tf_op jit(solution)/shard_map/reshape | solution.py:428
  18.0 0.3 copy.15
  18.3 0.0 copy-done
  18.3 0.0 copy-done.1
  18.3 0.0 copy-done.4
  18.3 0.0 copy-done.6
  18.3 0.7 %shard_map.143.here = bf16[864,128]{1,0:T(8,128)(2,1)S(1)} custom-call(s32[24]{0:T(128)S(1)} %copy-done.4, s32[24]{0:T(128)S(1)} %bitcast.20, bf16[1536,64]{1,0:T(8,128)(2,1)S(1)} %bitcast.10, f32[30,896]{1,0:T(8,128)S(1)} %copy-done, s32[7,128]{1,0:T(8,128)S(1)} %bitcast.14), custom_call_target="tpu_custom_call" | custom-call | flops 1000000 | bytes 2000000 | tf_op jit(solution)/shard_map/pallas_call | solution.py:429
  19.0 1.3 %collective-permute-start.1 = (bf16[864,128]{1,0:T(8,128)(2,1)S(1)}, bf16[864,128]{1,0:T(8,128)(2,1)S(1)}, u32[]{:S(2)}, u32[]{:S(2)}) collective-permute-start(bf16[864,128]{1,0:T(8,128)(2,1)S(1)} %shard_map.143.here), channel_id=1, source_target_pairs={{1,0},{2,1},{3,2},{4,3},{5,4},{6,5},{7,6},{8,7},{9,8},{10,9},{11,1... | collective-permute-start | bytes 663560 | tf_op jit(solution)/shard_map/ppermute | solution.py:443
  20.3 4.6 %collective-permute-start = (bf16[864,128]{1,0:T(8,128)(2,1)S(1)}, bf16[864,128]{1,0:T(8,128)(2,1)S(1)}, u32[]{:S(2)}, u32[]{:S(2)}) collective-permute-start(bf16[864,128]{1,0:T(8,128)(2,1)S(1)} %shard_map.143.here), channel_id=1, source_target_pairs={{0,1},{1,2},{2,3},{3,4},{4,5},{5,6},{6,7},{7,8},{8,9},{9,10},{10,1... | collective-permute-start | bytes 663560 | tf_op jit(solution)/shard_map/ppermute | solution.py:442
  24.9 0.0 copy-done.2
  24.9 0.0 copy-done.3
  24.9 0.0 copy-done.5
  24.9 0.7 %shard_map.141 = (f32[16,512]{1,0:T(8,128)S(1)}, f32[16,128]{1,0:T(8,128)S(1)}, f32[16,1536]{1,0:T(8,128)S(1)}) custom-call(s32[24]{0:T(128)S(1)} %copy-done.4, bf16[40,768]{1,0:T(8,128)(2,1)S(1)} %copy-done.2, f32[6,128]{1,0:T(8,128)S(1)} %bitcast.18, f32[8,40]{1,0:T(8,128)S(1)} %copy-done.3), custom_call_target="tpu_custom_call" | custom-call | flops 1000000 | bytes 2000000 | tf_op jit(solution)/shard_map/pallas_call | solution.py:444
  25.7 4.2 %all-to-all-done = bf16[64,5,2,128]{3,2,1,0:T(2,128)(2,1)S(1)} async-done(((bf16[64,5,2,128]{3,2,1,0:T(2,128)(2,1)}), bf16[64,5,2,128]{3,2,1,0:T(2,128)(2,1)S(1)}, u32[]{:S(2)}, u32[]{:S(2)}) %all-to-all-start) | async-done | bytes 163872 | tf_op jit(solution)/shard_map/all_to_all | solution.py:425
  29.9 0.0 copy-done.7
  29.9 1.7 %shard_map.142 = (f32[16,512]{1,0:T(8,128)S(1)}, bf16[256,128]{1,0:T(8,128)(2,1)}) custom-call(f32[8]{0:T(128)S(1)} %copy-done.7, bf16[640,128]{1,0:T(8,128)(2,1)S(1)} %bitcast.11, f32[16,512]{1,0:T(8,128)S(1)} %get-tuple-element.28.mixed, f32[16,128]{1,0:T(8,128)S(1)} %get-tuple-element.29.shares), custom_call_target="tpu_custom_call" | custom-call | flops 1000000 | bytes 2000000 | tf_op jit(solution)/shard_map/pallas_call | solution.py:454
  31.6 8.5 %all-to-all-start.1 = ((bf16[64,2,2,128]{3,2,1,0:T(2,128)(2,1)}), bf16[64,2,2,128]{3,2,1,0:T(2,128)(2,1)S(1)}, u32[]{:S(2)}, u32[]{:S(2)}) async-start(bf16[64,2,2,128]{3,2,1,0:T(2,128)(2,1)} %bitcast.5), calls=%async_computation.1 | async-start | bytes 131072 | tf_op jit(solution)/shard_map/all_to_all | solution.py:462
  40.1 0.0 copy-done.8
  40.1 0.0 copy-done.9
  40.1 2.3 %shard_map.144 = (bf16[896,896]{1,0:T(8,128)(2,1)S(1)}, bf16[128,896]{1,0:T(8,128)(2,1)S(1)}, f32[30,896]{1,0:T(8,128)S(1)}, f32[30,128]{1,0:T(8,128)S(1)}, f32[...) custom-call(f32[30]{0:T(128)S(1)} %copy-done.9, s32[6,896]{1,0:T(8,128)S(1)} %copy-done.8, f32[30,896]{1,0:T(8,128)S(1)} %copy-done, ...), custom_call_target="tpu_custom_call" | custom-call | flops 1000000000 | bytes 2000000 | tf_op jit(solution)/shard_map/pallas_call | solution.py:465
  42.4 0.0 collective-permute-done.1.after
  42.4 0.0 collective-permute-done.before
  42.4 9.9 %all-to-all-done.1 = bf16[64,2,2,128]{3,2,1,0:T(2,128)(2,1)S(1)} async-done(((bf16[64,2,2,128]{3,2,1,0:T(2,128)(2,1)}), bf16[64,2,2,128]{3,2,1,0:T(2,128)(2,1)S(1)}, u32[]{:S(2)}, u32[]{:S(2)}) %all-to-all-start.1) | async-done | bytes 65568 | tf_op jit(solution)/shard_map/all_to_all | solution.py:462
  52.3 0.6 shard_map.145
  52.9 1.9 %collective-permute-start.2 = (f32[30,128]{1,0:T(8,128)S(1)}, f32[30,128]{1,0:T(8,128)S(1)}, u32[]{:S(2)}, u32[]{:S(2)}) collective-permute-start(f32[30,128]{1,0:T(8,128)S(1)} %get-tuple-element.46), channel_id=1, source_target_pairs={{63,64},{127,128},{191,192},{255,256},{319,320},{383,384},{447,448... | collective-permute-start | bytes 46088 | tf_op jit(solution)/shard_map/ppermute | solution.py:486
  54.8 0.9 %shard_map.146 = (f32[30,896]{1,0:T(8,128)S(1)}, bf16[8,768]{1,0:T(8,128)(2,1)}) custom-call(f32[1,896]{1,0:T(1,128)S(1)} %get-tuple-element.39.heat, bf16[896,896]{1,0:T(8,128)(2,1)S(1)} %get-tuple-element.40.own, f32[30,896]{1,0:T(8,128)S(1)} %get-tuple-element.41.base, s32[7,128]{1,0:T(8,128)S(1)} %bitcast.17, f32[30,128]{1,0:T(8,128)S(1)} %get-tuple-element.38.depth, ...), custom_call_target="tpu_custom_call" | custom-call | flops 100000000 | bytes 2000000 | tf_op jit(solution)/shard_map/pallas_call | solution.py:487
  55.7 7.7 %collective-permute-done.2.swapped = f32[30,128]{1,0:T(8,128)S(1)} collective-permute-done((f32[30,128]{1,0:T(8,128)S(1)}, f32[30,128]{1,0:T(8,128)S(1)}, u32[]{:S(2)}, u32[]{:S(2)}) %collective-permute-start.2) | collective-permute-done | bytes 15392 | tf_op jit(solution)/shard_map/ppermute | solution.py:486
  63.4 0.8 %shard_map.147 = f32[30,896]{1,0:T(8,128)} custom-call(f32[1,128]{1,0:T(1,128)S(1)} %get-tuple-element.45.halo, f32[30,128]{1,0:T(8,128)S(1)} %collective-permute-done.2.swapped, bf16[864,128]{1,0:T(8,128)(2,1)S(1)} %collective-permute-done.before, bf16[864,128]{1,0:T(8,128)(2,1)S(1)} %collective-permute-done.1.after, ...), custom_call_target="tpu_custom_call" | custom-call | flops 1000000 | bytes 2000000 | tf_op jit(solution)/shard_map/pallas_call | solution.py:494
Async XLA Ops:
  2.9 15.4 %copy-start = (f32[30,896]{1,0:T(8,128)S(1)}, f32[30,896]{1,0:T(8,128)}, u32[]{:S(2)}) copy-start(f32[30,896]{1,0:T(8,128)} %tracer.1) | copy-start | bytes 322564
  2.9 15.4 %copy-start.1 = (s32[896]{0:T(1024)S(1)}, s32[896]{0:T(1024)}, u32[]{:S(2)}) copy-start(s32[896]{0:T(1024)} %param.14) | copy-start | bytes 10756
  2.9 15.3 %copy-start.4 = (s32[24]{0:T(128)S(1)}, s32[24]{0:T(128)}, u32[]{:S(2)}) copy-start(s32[24]{0:T(128)} %src.3) | copy-start | bytes 292
  2.9 15.3 %copy-start.6 = (s32[24,1]{0,1:T(1,128)S(1)}, s32[24,1]{0,1:T(1,128)}, u32[]{:S(2)}) copy-start(s32[24,1]{0,1:T(1,128)} %param.16) | copy-start | bytes 292
  3.0 21.9 %copy-start.2 = (bf16[40,768]{1,0:T(8,128)(2,1)S(1)}, bf16[40,768]{1,0:T(8,128)(2,1)}, u32[]{:S(2)}) copy-start(bf16[40,768]{1,0:T(8,128)(2,1)} %state) | copy-start | bytes 184324
  3.0 21.9 %copy-start.3 = (f32[8,40]{1,0:T(8,128)S(1)}, f32[8,40]{1,0:T(8,128)}, u32[]{:S(2)}) copy-start(f32[8,40]{1,0:T(8,128)} %couple.1) | copy-start | bytes 3844
  3.0 21.9 %copy-start.5 = (f32[768]{0:T(1024)S(1)}, f32[768]{0:T(1024)}, u32[]{:S(2)}) copy-start(f32[768]{0:T(1024)} %param.20) | copy-start | bytes 9220
  3.0 26.9 %copy-start.7 = (f32[8]{0:T(128)S(1)}, f32[8]{0:T(128)}, u32[]{:S(2)}) copy-start(f32[8]{0:T(128)} %heat_coef.1) | copy-start | bytes 100
  3.0 37.1 %copy-start.8 = (s32[6,896]{1,0:T(8,128)S(1)}, s32[6,896]{1,0:T(8,128)}, u32[]{:S(2)}) copy-start(s32[6,896]{1,0:T(8,128)} %near) | copy-start | bytes 64516
  3.0 37.1 %copy-start.9 = (f32[30]{0:T(128)S(1)}, f32[30]{0:T(128)}, u32[]{:S(2)}) copy-start(f32[30]{0:T(128)} %kappa.1) | copy-start | bytes 364
  3.0 26.8 %all-to-all-start = ((bf16[64,5,2,128]{3,2,1,0:T(2,128)(2,1)}), bf16[64,5,2,128]{3,2,1,0:T(2,128)(2,1)S(1)}, u32[]{:S(2)}, u32[]{:S(2)}) async-start(bf16[64,5,2,128]{3,2,1,0:T(2,128)(2,1)} %bitcast.21), calls=%async_computation | async-start | bytes 327680 | tf_op jit(solution)/shard_map/all_to_all | solution.py:425
  19.0 23.4 %collective-permute-start.1 = (bf16[864,128]{1,0:T(8,128)(2,1)S(1)}, bf16[864,128]{1,0:T(8,128)(2,1)S(1)}, u32[]{:S(2)}, u32[]{:S(2)}) collective-permute-start(bf16[864,128]{1,0:T(8,128)(2,1)S(1)} %shard_map.143.here), channel_id=1, source_target_pairs={{1,0},{2,1},{3,2},{4,3},{5,4},{6,5},{7,6},{8,7},{9,8},{10,9},{11,1... | collective-permute-start | bytes 663560 | tf_op jit(solution)/shard_map/ppermute | solution.py:443
  20.3 22.1 %collective-permute-start = (bf16[864,128]{1,0:T(8,128)(2,1)S(1)}, bf16[864,128]{1,0:T(8,128)(2,1)S(1)}, u32[]{:S(2)}, u32[]{:S(2)}) collective-permute-start(bf16[864,128]{1,0:T(8,128)(2,1)S(1)} %shard_map.143.here), channel_id=1, source_target_pairs={{0,1},{1,2},{2,3},{3,4},{4,5},{5,6},{6,7},{7,8},{8,9},{9,10},{10,1... | collective-permute-start | bytes 663560 | tf_op jit(solution)/shard_map/ppermute | solution.py:442
  31.6 20.7 %all-to-all-start.1 = ((bf16[64,2,2,128]{3,2,1,0:T(2,128)(2,1)}), bf16[64,2,2,128]{3,2,1,0:T(2,128)(2,1)S(1)}, u32[]{:S(2)}, u32[]{:S(2)}) async-start(bf16[64,2,2,128]{3,2,1,0:T(2,128)(2,1)} %bitcast.5), calls=%async_computation.1 | async-start | bytes 131072 | tf_op jit(solution)/shard_map/all_to_all | solution.py:462
  52.9 10.5 %collective-permute-start.2 = (f32[30,128]{1,0:T(8,128)S(1)}, f32[30,128]{1,0:T(8,128)S(1)}, u32[]{:S(2)}, u32[]{:S(2)}) collective-permute-start(f32[30,128]{1,0:T(8,128)S(1)} %get-tuple-element.46), channel_id=1, source_target_pairs={{63,64},{127,128},{191,192},{255,256},{319,320},{383,384},{447,448... | collective-permute-start | bytes 46088 | tf_op jit(solution)/shard_map/ppermute | solution.py:486

commit v4 on v3

--- a/solution.py
+++ b/solution.py
@@ -306,12 +306,17 @@
     right = right[1:2] + pltpu.roll(right, TILE, 1)[0:1]
     levels = depth.shape[0]
     coast = jnp.where(low[:1], meta(before, 0)[levels : levels + 1], meta(after, 0)[levels : levels + 1])
-    halo[...] = jnp.where(low[:1], left, right) * coast
+    beside = jnp.where(low[:1], left, right) * coast
+    halo[...] = beside
+    edges = jnp.where(lane < TILE, meta(before, 0), meta(after, 0))[:levels]
+    deep = depth[...]
+    beside = edges + deep * beside
     row = jnp.concatenate([summed[t : t + 1, :TILE] for t in range(cells // TILE)], axis=1)
     row = row * line(mask[...].astype(F32))
     heat[...] = row
     ends = jnp.concatenate([row[:, cells - HALO :], row[:, :HALO]], axis=1)
-    forced[...] = meta(here, 0)[:levels] + depth[...] * ends
+    ends = meta(here, 0)[:levels] + deep * ends
+    forced[...] = jnp.where(lax.axis_index("grp") == 0, ends, beside)
 
 
 def halves(row):
@@ -435,10 +440,10 @@
     )(entry_src, route, flipped.reshape(entries * TILE, TILE), tracer, mask)
     axes = ("grp", "blk")
     count = lax.axis_size(axes)
-    ring = [(i, (i + 1) % count) for i in range(count)]
-    up = [pair for pair in ring if pair[1] % peers]
-    seams = [pair for pair in ring if pair[1] % peers == 0]
+    up = [(i, i - i % peers + (i + 1) % peers) for i in range(count)]
     down = [(target, source) for source, target in up]
+    seams = [(i, (i + peers) % count) for i in range(peers, count, peers)] + [(0, count - 1)]
+    seams += [(i, i - peers) for i in range(2 * peers - 1, count, peers)] + [(peers - 1, peers)]
     before = lax.ppermute(here, axes, up)
     after = lax.ppermute(here, axes, down)
     mixed, shares, chosen = call(
@@ -483,7 +488,7 @@
         (VMEM,) * 3,
         [pltpu.VMEM((peers * 4, LANES), F32)],
     )(returned, chosen, here, before, after, mask, depth)
-    swapped = lax.ppermute(forced, axes, seams + [(target, source) for source, target in seams])
+    swapped = lax.ppermute(forced, axes, seams)
     part, fluxes = call(
         partial_kernel,
         (shape((levels, cells), F32), shape((rows, atm_cells), BF16)),

time: 64.6 us -> 62.9 us (0.974)
  the two profiles are of different devices: /device:TPU:512 before, /device:TPU:1 now
where the time goes in v4:
time: 62.9 us; the launch traced here: 62.5 us
  starting transfers between devices  39.5 us (63%)
  waiting for transfers between devices  10.4 us (17%)
  Pallas kernels  10.1 us (16%)
  local copies, waits for them, and re-layouts  1.65 us (3%)
  between operations  0.88 us (1%)
    all_to_all x1, starting transfers between devices, shards(): lax.all_to_all(sent.reshape(peers, half + 1, 2, LANES), 'blk', split_axis...  14.2 us
    all_to_all x1, starting transfers between devices, shards(): lax.all_to_all(back.reshape(peers, 2, 2, LANES), 'blk', split_axis=0, con...  8.88 us
    all_to_all x1, waiting for transfers between devices, shards(): lax.all_to_all(back.reshape(peers, 2, 2, LANES), 'blk', split_axis=0, con...  8.76 us
    ppermute x1, starting transfers between devices, shards(): swapped = lax.ppermute(forced, axes, seams)  7.96 us
    ppermute x1, starting transfers between devices, shards(): after = lax.ppermute(here, axes, down)  6.55 us
    pallas_call x1, Pallas kernels, shards(): call(base_kernel, (shape((cells, cells), BF16), shape((2 * HALO, cells),...  2.31 us
    pallas_call x1, Pallas kernels, shards(): call(pack_kernel, shape((peers * pitch, LANES), BF16), [HBM] * 7, VMEM, [...  2.27 us
    ppermute x1, starting transfers between devices, shards(): before = lax.ppermute(here, axes, up)  1.92 us
  transfers between devices with their start and end apart: 5, of which 3 were waited for; matrix products, arithmetic and copies ran while one was open for 3% of the time, Pallas kernels for 10%

profile of v4, /device:TPU:1, one launch (start us, length us, event | category | flops | bytes accessed | tf_op | source)
XLA Modules:
  0.0 62.5 jit_solution(17048603916554138976)
XLA Ops:
  0.6 2.3 %shard_map.140 = bf16[640,128]{1,0:T(8,128)(2,1)} custom-call(s32[24]{0:T(128)} %src.3, s32[24]{0:T(128)} %bitcast.19, s32[24]{0:T(128)} %tile_hbm.1, bf16[40,896]{1,0:T(8,128)(2,1)} %fields_hbm.1, s32[7,128]{1,0:T(8,128)} %bitcast.13, f32[8,40]{1,0:T(8,128)} %couple.1, bf16[24,4096]{1,0:T(8,128)(2,1)} %weights_hbm.1), custom_call_target="tpu_custom_call" | custom-call | flops 1000000 | bytes 2000000 | tf_op jit(solution)/shard_map/pallas_call | solution.py:406
  2.9 0.0 copy-start
  2.9 0.0 copy-start.1
  2.9 0.0 copy-start.4
  2.9 0.0 copy-start.6
  3.0 0.0 copy-start.2
  3.0 0.0 copy-start.3
  3.0 0.0 copy-start.5
  3.0 0.0 copy-start.7
  3.0 0.0 copy-start.8
  3.0 0.0 copy-start.9
  3.0 14.2 %all-to-all-start = ((bf16[64,5,2,128]{3,2,1,0:T(2,128)(2,1)}), bf16[64,5,2,128]{3,2,1,0:T(2,128)(2,1)S(1)}, u32[]{:S(2)}, u32[]{:S(2)}) async-start(bf16[64,5,2,128]{3,2,1,0:T(2,128)(2,1)} %bitcast.21), calls=%async_computation | async-start | bytes 327680 | tf_op jit(solution)/shard_map/all_to_all | solution.py:430
  17.2 1.3 %reshape.38 = bf16[24,64,64]{2,1,0:T(8,128)(2,1)S(1)} reshape(bf16[24,4096]{1,0:T(8,128)(2,1)} %weights_hbm.1) | data formatting | bytes 393216 | tf_op jit(solution)/shard_map/reshape | solution.py:433
  18.5 0.3 copy.15
  18.8 0.0 copy-done
  18.8 0.0 copy-done.1
  18.8 0.0 copy-done.4
  18.8 0.0 copy-done.6
  18.8 0.7 %shard_map.143.here = bf16[864,128]{1,0:T(8,128)(2,1)S(1)} custom-call(s32[24]{0:T(128)S(1)} %copy-done.4, s32[24]{0:T(128)S(1)} %bitcast.20, bf16[1536,64]{1,0:T(8,128)(2,1)S(1)} %bitcast.10, f32[30,896]{1,0:T(8,128)S(1)} %copy-done, s32[7,128]{1,0:T(8,128)S(1)} %bitcast.14), custom_call_target="tpu_custom_call" | custom-call | flops 1000000 | bytes 2000000 | tf_op jit(solution)/shard_map/pallas_call | solution.py:434
  19.6 6.6 %collective-permute-start.1 = (bf16[864,128]{1,0:T(8,128)(2,1)S(1)}, bf16[864,128]{1,0:T(8,128)(2,1)S(1)}, u32[]{:S(2)}, u32[]{:S(2)}) collective-permute-start(bf16[864,128]{1,0:T(8,128)(2,1)S(1)} %shard_map.143.here), channel_id=1, source_target_pairs={{1,0},{2,1},{3,2},{4,3},{5,4},{6,5},{7,6},{8,7},{9,8},{10,9},{11,1... | collective-permute-start | bytes 663560 | tf_op jit(solution)/shard_map/ppermute | solution.py:448
  26.1 1.9 %collective-permute-start = (bf16[864,128]{1,0:T(8,128)(2,1)S(1)}, bf16[864,128]{1,0:T(8,128)(2,1)S(1)}, u32[]{:S(2)}, u32[]{:S(2)}) collective-permute-start(bf16[864,128]{1,0:T(8,128)(2,1)S(1)} %shard_map.143.here), channel_id=1, source_target_pairs={{0,1},{1,2},{2,3},{3,4},{4,5},{5,6},{6,7},{7,8},{8,9},{9,10},{10,1... | collective-permute-start | bytes 663560 | tf_op jit(solution)/shard_map/ppermute | solution.py:447
  28.1 0.0 copy-done.2
  28.1 0.0 copy-done.3
  28.1 0.0 copy-done.5
  28.1 0.7 %shard_map.141 = (f32[16,512]{1,0:T(8,128)S(1)}, f32[16,128]{1,0:T(8,128)S(1)}, f32[16,1536]{1,0:T(8,128)S(1)}) custom-call(s32[24]{0:T(128)S(1)} %copy-done.4, bf16[40,768]{1,0:T(8,128)(2,1)S(1)} %copy-done.2, f32[6,128]{1,0:T(8,128)S(1)} %bitcast.18, f32[8,40]{1,0:T(8,128)S(1)} %copy-done.3), custom_call_target="tpu_custom_call" | custom-call | flops 1000000 | bytes 2000000 | tf_op jit(solution)/shard_map/pallas_call | solution.py:449
  28.8 0.1 all-to-all-done
  28.9 0.0 copy-done.7
  28.9 1.7 %shard_map.142 = (f32[16,512]{1,0:T(8,128)S(1)}, bf16[256,128]{1,0:T(8,128)(2,1)}) custom-call(f32[8]{0:T(128)S(1)} %copy-done.7, bf16[640,128]{1,0:T(8,128)(2,1)S(1)} %bitcast.11, f32[16,512]{1,0:T(8,128)S(1)} %get-tuple-element.28.mixed, f32[16,128]{1,0:T(8,128)S(1)} %get-tuple-element.29.shares), custom_call_target="tpu_custom_call" | custom-call | flops 1000000 | bytes 2000000 | tf_op jit(solution)/shard_map/pallas_call | solution.py:459
  30.6 8.9 %all-to-all-start.1 = ((bf16[64,2,2,128]{3,2,1,0:T(2,128)(2,1)}), bf16[64,2,2,128]{3,2,1,0:T(2,128)(2,1)S(1)}, u32[]{:S(2)}, u32[]{:S(2)}) async-start(bf16[64,2,2,128]{3,2,1,0:T(2,128)(2,1)} %bitcast.5), calls=%async_computation.1 | async-start | bytes 131072 | tf_op jit(solution)/shard_map/all_to_all | solution.py:467
  39.5 0.0 copy-done.8
  39.5 0.0 copy-done.9
  39.5 2.3 %shard_map.144 = (bf16[896,896]{1,0:T(8,128)(2,1)S(1)}, bf16[128,896]{1,0:T(8,128)(2,1)S(1)}, f32[30,896]{1,0:T(8,128)S(1)}, f32[30,128]{1,0:T(8,128)S(1)}, f32[...) custom-call(f32[30]{0:T(128)S(1)} %copy-done.9, s32[6,896]{1,0:T(8,128)S(1)} %copy-done.8, f32[30,896]{1,0:T(8,128)S(1)} %copy-done, ...), custom_call_target="tpu_custom_call" | custom-call | flops 1000000000 | bytes 2000000 | tf_op jit(solution)/shard_map/pallas_call | solution.py:470
  41.9 0.0 collective-permute-done.1.after
  41.9 0.0 collective-permute-done.before
  41.9 8.8 %all-to-all-done.1 = bf16[64,2,2,128]{3,2,1,0:T(2,128)(2,1)S(1)} async-done(((bf16[64,2,2,128]{3,2,1,0:T(2,128)(2,1)}), bf16[64,2,2,128]{3,2,1,0:T(2,128)(2,1)S(1)}, u32[]{:S(2)}, u32[]{:S(2)}) %all-to-all-start.1) | async-done | bytes 65568 | tf_op jit(solution)/shard_map/all_to_all | solution.py:467
  50.6 0.6 shard_map.145
  51.2 8.0 %collective-permute-start.2 = (f32[30,128]{1,0:T(8,128)S(1)}, f32[30,128]{1,0:T(8,128)S(1)}, u32[]{:S(2)}, u32[]{:S(2)}) collective-permute-start(f32[30,128]{1,0:T(8,128)S(1)} %get-tuple-element.46), channel_id=1, source_target_pairs={{64,128},{128,192},{192,256},{256,320},{320,384},{384,448},{448,51... | collective-permute-start | bytes 46088 | tf_op jit(solution)/shard_map/ppermute | solution.py:491
  59.2 0.9 %shard_map.146 = (f32[30,896]{1,0:T(8,128)S(1)}, bf16[8,768]{1,0:T(8,128)(2,1)}) custom-call(f32[1,896]{1,0:T(1,128)S(1)} %get-tuple-element.39.heat, bf16[896,896]{1,0:T(8,128)(2,1)S(1)} %get-tuple-element.40.own, f32[30,896]{1,0:T(8,128)S(1)} %get-tuple-element.41.base, s32[7,128]{1,0:T(8,128)S(1)} %bitcast.17, f32[30,128]{1,0:T(8,128)S(1)} %get-tuple-element.38.depth, ...), custom_call_target="tpu_custom_call" | custom-call | flops 100000000 | bytes 2000000 | tf_op jit(solution)/shard_map/pallas_call | solution.py:492
  60.1 1.6 %collective-permute-done.2.swapped = f32[30,128]{1,0:T(8,128)S(1)} collective-permute-done((f32[30,128]{1,0:T(8,128)S(1)}, f32[30,128]{1,0:T(8,128)S(1)}, u32[]{:S(2)}, u32[]{:S(2)}) %collective-permute-start.2) | collective-permute-done | bytes 15392 | tf_op jit(solution)/shard_map/ppermute | solution.py:491
  61.7 0.8 %shard_map.147 = f32[30,896]{1,0:T(8,128)} custom-call(f32[1,128]{1,0:T(1,128)S(1)} %get-tuple-element.45.halo, f32[30,128]{1,0:T(8,128)S(1)} %collective-permute-done.2.swapped, bf16[864,128]{1,0:T(8,128)(2,1)S(1)} %collective-permute-done.before, bf16[864,128]{1,0:T(8,128)(2,1)S(1)} %collective-permute-done.1.after, ...), custom_call_target="tpu_custom_call" | custom-call | flops 1000000 | bytes 2000000 | tf_op jit(solution)/shard_map/pallas_call | solution.py:499
Async XLA Ops:
  2.9 15.9 %copy-start = (f32[30,896]{1,0:T(8,128)S(1)}, f32[30,896]{1,0:T(8,128)}, u32[]{:S(2)}) copy-start(f32[30,896]{1,0:T(8,128)} %tracer.1) | copy-start | bytes 322564
  2.9 15.9 %copy-start.1 = (s32[896]{0:T(1024)S(1)}, s32[896]{0:T(1024)}, u32[]{:S(2)}) copy-start(s32[896]{0:T(1024)} %param.14) | copy-start | bytes 10756
  2.9 15.9 %copy-start.4 = (s32[24]{0:T(128)S(1)}, s32[24]{0:T(128)}, u32[]{:S(2)}) copy-start(s32[24]{0:T(128)} %src.3) | copy-start | bytes 292
  2.9 15.9 %copy-start.6 = (s32[24,1]{0,1:T(1,128)S(1)}, s32[24,1]{0,1:T(1,128)}, u32[]{:S(2)}) copy-start(s32[24,1]{0,1:T(1,128)} %param.16) | copy-start | bytes 292
  3.0 25.1 %copy-start.2 = (bf16[40,768]{1,0:T(8,128)(2,1)S(1)}, bf16[40,768]{1,0:T(8,128)(2,1)}, u32[]{:S(2)}) copy-start(bf16[40,768]{1,0:T(8,128)(2,1)} %state) | copy-start | bytes 184324
  3.0 25.1 %copy-start.3 = (f32[8,40]{1,0:T(8,128)S(1)}, f32[8,40]{1,0:T(8,128)}, u32[]{:S(2)}) copy-start(f32[8,40]{1,0:T(8,128)} %couple.1) | copy-start | bytes 3844
  3.0 25.1 %copy-start.5 = (f32[768]{0:T(1024)S(1)}, f32[768]{0:T(1024)}, u32[]{:S(2)}) copy-start(f32[768]{0:T(1024)} %param.20) | copy-start | bytes 9220
  3.0 25.9 %copy-start.7 = (f32[8]{0:T(128)S(1)}, f32[8]{0:T(128)}, u32[]{:S(2)}) copy-start(f32[8]{0:T(128)} %heat_coef.1) | copy-start | bytes 100
  3.0 36.5 %copy-start.8 = (s32[6,896]{1,0:T(8,128)S(1)}, s32[6,896]{1,0:T(8,128)}, u32[]{:S(2)}) copy-start(s32[6,896]{1,0:T(8,128)} %near) | copy-start | bytes 64516
  3.0 36.5 %copy-start.9 = (f32[30]{0:T(128)S(1)}, f32[30]{0:T(128)}, u32[]{:S(2)}) copy-start(f32[30]{0:T(128)} %kappa.1) | copy-start | bytes 364
  3.0 25.9 %all-to-all-start = ((bf16[64,5,2,128]{3,2,1,0:T(2,128)(2,1)}), bf16[64,5,2,128]{3,2,1,0:T(2,128)(2,1)S(1)}, u32[]{:S(2)}, u32[]{:S(2)}) async-start(bf16[64,5,2,128]{3,2,1,0:T(2,128)(2,1)} %bitcast.21), calls=%async_computation | async-start | bytes 327680 | tf_op jit(solution)/shard_map/all_to_all | solution.py:430
  19.6 22.3 %collective-permute-start.1 = (bf16[864,128]{1,0:T(8,128)(2,1)S(1)}, bf16[864,128]{1,0:T(8,128)(2,1)S(1)}, u32[]{:S(2)}, u32[]{:S(2)}) collective-permute-start(bf16[864,128]{1,0:T(8,128)(2,1)S(1)} %shard_map.143.here), channel_id=1, source_target_pairs={{1,0},{2,1},{3,2},{4,3},{5,4},{6,5},{7,6},{8,7},{9,8},{10,9},{11,1... | collective-permute-start | bytes 663560 | tf_op jit(solution)/shard_map/ppermute | solution.py:448
  26.1 15.7 %collective-permute-start = (bf16[864,128]{1,0:T(8,128)(2,1)S(1)}, bf16[864,128]{1,0:T(8,128)(2,1)S(1)}, u32[]{:S(2)}, u32[]{:S(2)}) collective-permute-start(bf16[864,128]{1,0:T(8,128)(2,1)S(1)} %shard_map.143.here), channel_id=1, source_target_pairs={{0,1},{1,2},{2,3},{3,4},{4,5},{5,6},{6,7},{7,8},{8,9},{9,10},{10,1... | collective-permute-start | bytes 663560 | tf_op jit(solution)/shard_map/ppermute | solution.py:447
  30.6 20.0 %all-to-all-start.1 = ((bf16[64,2,2,128]{3,2,1,0:T(2,128)(2,1)}), bf16[64,2,2,128]{3,2,1,0:T(2,128)(2,1)S(1)}, u32[]{:S(2)}, u32[]{:S(2)}) async-start(bf16[64,2,2,128]{3,2,1,0:T(2,128)(2,1)} %bitcast.5), calls=%async_computation.1 | async-start | bytes 131072 | tf_op jit(solution)/shard_map/all_to_all | solution.py:467
  51.2 10.4 %collective-permute-start.2 = (f32[30,128]{1,0:T(8,128)S(1)}, f32[30,128]{1,0:T(8,128)S(1)}, u32[]{:S(2)}, u32[]{:S(2)}) collective-permute-start(f32[30,128]{1,0:T(8,128)S(1)} %get-tuple-element.46), channel_id=1, source_target_pairs={{64,128},{128,192},{192,256},{256,320},{320,384},{384,448},{448,51... | collective-permute-start | bytes 46088 | tf_op jit(solution)/shard_map/ppermute | solution.py:491

commit v5 on v4

--- a/solution.py
+++ b/solution.py
@@ -9,6 +9,7 @@
 HALO = 64
 LANES = 128
 PITCH = 33
+WIDE = 65
 F32 = jnp.float32
 BF16 = jnp.bfloat16
 SMEM = pl.BlockSpec(memory_space=pltpu.SMEM)
@@ -117,7 +118,7 @@
     out[...] = slots[...].astype(BF16)
 
 
-def ship_kernel(src, route, flipped, tracer, mask, out, seen):
+def ship_kernel(src, route, weights, tracer, mask, out, seen, wide):
     entries = src.shape[0]
     levels, cells = tracer.shape
     half = entries * TILE // 2
@@ -129,7 +130,21 @@
         rank = seen[to]
         seen[to] = rank + 1
         slots.append(to * 2 + rank)
-    out[:half, :] = jnp.concatenate([flipped[:half, :], flipped[half:, :]], axis=1)
+    flat = weights[...].astype(F32)
+    low = iota((8, LANES), 1) < TILE
+    for g in range(entries // 8):
+        for j in range(TILE // 2):
+            block = flat[g * 8 : (g + 1) * 8, j * LANES : (j + 1) * LANES]
+            at = g * 8 * WIDE + 2 * j
+            wide[pl.ds(at, 8, stride=WIDE), :] = jnp.where(low, block, 0.0)
+            wide[pl.ds(at + 1, 8, stride=WIDE), :] = jnp.where(low, 0.0, block)
+    eye = iota((TILE, LANES), 0) == (iota((TILE, LANES), 1) & (TILE - 1))
+    eye = eye.astype(F32).astype(BF16)
+    for e in range(entries // 2):
+        pair = [wide[i * WIDE : i * WIDE + TILE, :] for i in (e, e + entries // 2)]
+        rows = jnp.concatenate(pair, axis=0).astype(BF16)
+        turned = lax.dot_general(eye, rows, (((1,), (1,)), ((), ())), preferred_element_type=F32)
+        out[e * TILE : (e + 1) * TILE, :] = turned.astype(BF16)
     ends = lambda x: jnp.concatenate([x[:, cells - HALO :], x[:, :HALO]], axis=1)
     sea = ends(line(mask[...].astype(F32)))
     edge = ends(tracer[...]) * sea
@@ -364,16 +379,20 @@
     out[...] = part[...] + (near[:32] + near[32:64])[:levels] + across(rate[...], cells) * inner
 
 
-def call(kernel, out_shape, in_specs, out_specs, scratch=(), flops=1_000_000, vmem=24 * 2**20):
+def call(kernel, out_shape, in_specs, out_specs, scratch=(), flops=2_000_000_000, vmem=24 * 2**20):
     return pl.pallas_call(
         kernel,
         out_shape=out_shape,
         in_specs=in_specs,
         out_specs=out_specs,
         scratch_shapes=list(scratch),
-        cost_estimate=pl.CostEstimate(flops=flops, bytes_accessed=2_000_000, transcendentals=0),
+        cost_estimate=pl.CostEstimate(flops=flops, bytes_accessed=30_000_000, transcendentals=0),
         compiler_params=pltpu.CompilerParams(vmem_limit_bytes=vmem),
     )
+
+
+def in_hbm(array):
+    return pltpu.with_memory_space_constraint(array, pltpu.HBM)
 
 
 def shards(
@@ -430,14 +449,13 @@
     got = lax.all_to_all(
         sent.reshape(peers, half + 1, 2, LANES), "blk", split_axis=0, concat_axis=0, tiled=True
     ).reshape(peers * pitch, LANES)
-    flipped = weight_tiles.reshape(entries, TILE, TILE).transpose(0, 2, 1)
     here = call(
         ship_kernel,
         shape((entries * TILE // 2 + 96, LANES), BF16),
         [SMEM, SMEM, VMEM, VMEM, VMEM],
         VMEM,
-        [pltpu.SMEM((peers,), i32)],
-    )(entry_src, route, flipped.reshape(entries * TILE, TILE), tracer, mask)
+        [pltpu.SMEM((peers,), i32), pltpu.VMEM((entries * WIDE, LANES), F32)],
+    )(*(in_hbm(x) for x in (entry_src, route, weight_tiles, tracer, mask)))
     axes = ("grp", "blk")
     count = lax.axis_size(axes)
     up = [(i, i - i % peers + (i + 1) % peers) for i in range(count)]

time: 62.9 us -> 61.8 us (0.983)
  local copies, waits for them, and re-layouts: 1.65 us -> 0.05 us
  waiting for transfers between devices: 10.4 us -> 11.3 us
  starting transfers between devices: 39.5 us -> 38.6 us
  Pallas kernels: 10.1 us -> 10.8 us
    reshape x2 -> x0, local copies, waits for them, and re-layouts: 1.59 us -> none  [shards(): flipped = weight_tiles.reshape(entries, TILE, TILE).transpose(0, 2, 1)]
    all_to_all x1, waiting for transfers between devices: 0.09 us -> 0.91 us  [shards(): lax.all_to_all(sent.reshape(peers, half + 1, 2, LANES), 'blk', split_axis...]
    all_to_all x1, starting transfers between devices: 8.88 us -> 8.08 us  [shards(): lax.all_to_all(back.reshape(peers, 2, 2, LANES), 'blk', split_axis=0, con...]
    pallas_call x1, Pallas kernels: 0.71 us -> 1.45 us  [shards(): call(ship_kernel, shape((entries * TILE // 2 + 96, LANES), BF16), [SMEM,...]
  transfers between devices with their start and end apart: 5 -> 5, of which waited for: 3 -> 3; matrix products, arithmetic and copies ran while one was open for 3% -> 0% of each run, Pallas kernels for 10% -> 12%
where the time goes in v5:
time: 61.8 us; the launch traced here: 61.5 us
  starting transfers between devices  38.6 us (62%)
  waiting for transfers between devices  11.3 us (18%)
  Pallas kernels  10.8 us (17%)
  between operations  0.84 us (1%)
    all_to_all x1, starting transfers between devices, shards(): lax.all_to_all(sent.reshape(peers, half + 1, 2, LANES), 'blk', split_axis...  14 us
    all_to_all x1, waiting for transfers between devices, shards(): lax.all_to_all(back.reshape(peers, 2, 2, LANES), 'blk', split_axis=0, con...  8.74 us
    all_to_all x1, starting transfers between devices, shards(): lax.all_to_all(back.reshape(peers, 2, 2, LANES), 'blk', split_axis=0, con...  8.08 us
    ppermute x1, starting transfers between devices, shards(): swapped = lax.ppermute(forced, axes, seams)  7.96 us
    ppermute x1, starting transfers between devices, shards(): after = lax.ppermute(here, axes, down)  6.55 us
    pallas_call x1, Pallas kernels, shards(): call(base_kernel, (shape((cells, cells), BF16), shape((2 * HALO, cells),...  2.31 us
    pallas_call x1, Pallas kernels, shards(): call(pack_kernel, shape((peers * pitch, LANES), BF16), [HBM] * 7, VMEM, [...  2.27 us
    ppermute x1, starting transfers between devices, shards(): before = lax.ppermute(here, axes, up)  1.92 us
  transfers between devices with their start and end apart: 5, of which 3 were waited for; matrix products, arithmetic and copies ran while one was open for 0% of the time, Pallas kernels for 12%

profile of v5, /device:TPU:1, one launch (start us, length us, event | category | flops | bytes accessed | tf_op | source)
XLA Modules:
  0.0 61.5 jit_solution(2487779657381543013)
XLA Ops:
  0.6 2.3 %shard_map.140 = bf16[640,128]{1,0:T(8,128)(2,1)} custom-call(s32[24]{0:T(128)} %src.3, s32[24]{0:T(128)} %bitcast.16, s32[24]{0:T(128)} %tile_hbm.1, bf16[40,896]{1,0:T(8,128)(2,1)} %fields_hbm.1, s32[7,128]{1,0:T(8,128)} %bitcast.9, f32[8,40]{1,0:T(8,128)} %couple.1, bf16[24,4096]{1,0:T(8,128)(2,1)} %weights), custom_call_target="tpu_custom_call" | custom-call | flops 2000000000 | bytes 30000000 | tf_op jit(solution)/shard_map/pallas_call | solution.py:425
  2.9 14.0 %all-to-all-start = ((bf16[64,5,2,128]{3,2,1,0:T(2,128)(2,1)}), bf16[64,5,2,128]{3,2,1,0:T(2,128)(2,1)S(1)}, u32[]{:S(2)}, u32[]{:S(2)}) async-start(bf16[64,5,2,128]{3,2,1,0:T(2,128)(2,1)} %bitcast.15), calls=%async_computation | async-start | bytes 327680 | tf_op jit(solution)/shard_map/all_to_all | solution.py:449
  17.0 0.0 copy-start.2
  17.0 0.0 copy-start.4
  17.0 0.0 copy-start.5
  17.0 0.0 copy-start.6
  17.0 1.4 %shard_map.143.here = bf16[864,128]{1,0:T(8,128)(2,1)S(1)} custom-call(s32[24]{0:T(128)} %src.3, s32[24]{0:T(128)} %bitcast.17, bf16[24,4096]{1,0:T(8,128)(2,1)} %weights, f32[30,896]{1,0:T(8,128)} %tracer.1, s32[7,128]{1,0:T(8,128)} %bitcast.10), custom_call_target="tpu_custom_call" | custom-call | flops 2000000000 | bytes 30000000 | tf_op jit(solution)/shard_map/pallas_call | solution.py:452
  18.5 6.6 %collective-permute-start.1 = (bf16[864,128]{1,0:T(8,128)(2,1)S(1)}, bf16[864,128]{1,0:T(8,128)(2,1)S(1)}, u32[]{:S(2)}, u32[]{:S(2)}) collective-permute-start(bf16[864,128]{1,0:T(8,128)(2,1)S(1)} %shard_map.143.here), channel_id=1, source_target_pairs={{1,0},{2,1},{3,2},{4,3},{5,4},{6,5},{7,6},{8,7},{9,8},{10,9},{11,1... | collective-permute-start | bytes 663560 | tf_op jit(solution)/shard_map/ppermute | solution.py:466
  25.0 1.9 %collective-permute-start = (bf16[864,128]{1,0:T(8,128)(2,1)S(1)}, bf16[864,128]{1,0:T(8,128)(2,1)S(1)}, u32[]{:S(2)}, u32[]{:S(2)}) collective-permute-start(bf16[864,128]{1,0:T(8,128)(2,1)S(1)} %shard_map.143.here), channel_id=1, source_target_pairs={{0,1},{1,2},{2,3},{3,4},{4,5},{5,6},{6,7},{7,8},{8,9},{9,10},{10,1... | collective-permute-start | bytes 663560 | tf_op jit(solution)/shard_map/ppermute | solution.py:465
  27.0 0.0 copy-done.2
  27.0 0.0 copy-done.4
  27.0 0.0 copy-done.5
  27.0 0.0 copy-done.6
  27.0 0.0 copy-start.7
  27.0 0.7 %shard_map.141 = (f32[16,512]{1,0:T(8,128)S(1)}, f32[16,128]{1,0:T(8,128)S(1)}, f32[16,1536]{1,0:T(8,128)S(1)}) custom-call(s32[24]{0:T(128)S(1)} %copy-done.6, bf16[40,768]{1,0:T(8,128)(2,1)S(1)} %copy-done.2, f32[6,128]{1,0:T(8,128)S(1)} %bitcast.14, f32[8,40]{1,0:T(8,128)S(1)} %copy-done.4), custom_call_target="tpu_custom_call" | custom-call | flops 2000000000 | bytes 30000000 | tf_op jit(solution)/shard_map/pallas_call | solution.py:467
  27.8 0.9 %all-to-all-done = bf16[64,5,2,128]{3,2,1,0:T(2,128)(2,1)S(1)} async-done(((bf16[64,5,2,128]{3,2,1,0:T(2,128)(2,1)}), bf16[64,5,2,128]{3,2,1,0:T(2,128)(2,1)S(1)}, u32[]{:S(2)}, u32[]{:S(2)}) %all-to-all-start) | async-done | bytes 163872 | tf_op jit(solution)/shard_map/all_to_all | solution.py:449
  28.7 0.0 copy-done.7
  28.7 0.0 copy-start
  28.7 0.0 copy-start.1
  28.7 0.0 copy-start.3
  28.7 0.0 copy-start.8
  28.7 1.7 %shard_map.142 = (f32[16,512]{1,0:T(8,128)S(1)}, bf16[256,128]{1,0:T(8,128)(2,1)}) custom-call(f32[8]{0:T(128)S(1)} %copy-done.7, bf16[640,128]{1,0:T(8,128)(2,1)S(1)} %bitcast.7, f32[16,512]{1,0:T(8,128)S(1)} %get-tuple-element.28.mixed, f32[16,128]{1,0:T(8,128)S(1)} %get-tuple-element.29.shares), custom_call_target="tpu_custom_call" | custom-call | flops 2000000000 | bytes 30000000 | tf_op jit(solution)/shard_map/pallas_call | solution.py:477
  30.4 8.1 %all-to-all-start.1 = ((bf16[64,2,2,128]{3,2,1,0:T(2,128)(2,1)}), bf16[64,2,2,128]{3,2,1,0:T(2,128)(2,1)S(1)}, u32[]{:S(2)}, u32[]{:S(2)}) async-start(bf16[64,2,2,128]{3,2,1,0:T(2,128)(2,1)} %bitcast.5), calls=%async_computation.1 | async-start | bytes 131072 | tf_op jit(solution)/shard_map/all_to_all | solution.py:485
  38.5 0.0 copy-done
  38.5 0.0 copy-done.1
  38.5 0.0 copy-done.3
  38.5 0.0 copy-done.8
  38.5 2.3 %shard_map.144 = (bf16[896,896]{1,0:T(8,128)(2,1)S(1)}, bf16[128,896]{1,0:T(8,128)(2,1)S(1)}, f32[30,896]{1,0:T(8,128)S(1)}, f32[30,128]{1,0:T(8,128)S(1)}, f32[...) custom-call(f32[30]{0:T(128)S(1)} %copy-done.8, s32[6,896]{1,0:T(8,128)S(1)} %copy-done.3, f32[30,896]{1,0:T(8,128)S(1)} %copy-done.1, ...), custom_call_target="tpu_custom_call" | custom-call | flops 1000000000 | bytes 30000000 | tf_op jit(solution)/shard_map/pallas_call | solution.py:488
  40.8 0.0 collective-permute-done.1.after
  40.9 0.0 collective-permute-done.before
  40.9 8.7 %all-to-all-done.1 = bf16[64,2,2,128]{3,2,1,0:T(2,128)(2,1)S(1)} async-done(((bf16[64,2,2,128]{3,2,1,0:T(2,128)(2,1)}), bf16[64,2,2,128]{3,2,1,0:T(2,128)(2,1)S(1)}, u32[]{:S(2)}, u32[]{:S(2)}) %all-to-all-start.1) | async-done | bytes 65568 | tf_op jit(solution)/shard_map/all_to_all | solution.py:485
  49.6 0.6 shard_map.145
  50.2 8.0 %collective-permute-start.2 = (f32[30,128]{1,0:T(8,128)S(1)}, f32[30,128]{1,0:T(8,128)S(1)}, u32[]{:S(2)}, u32[]{:S(2)}) collective-permute-start(f32[30,128]{1,0:T(8,128)S(1)} %get-tuple-element.46), channel_id=1, source_target_pairs={{64,128},{128,192},{192,256},{256,320},{320,384},{384,448},{448,51... | collective-permute-start | bytes 46088 | tf_op jit(solution)/shard_map/ppermute | solution.py:509
  58.2 0.9 %shard_map.146 = (f32[30,896]{1,0:T(8,128)S(1)}, bf16[8,768]{1,0:T(8,128)(2,1)}) custom-call(f32[1,896]{1,0:T(1,128)S(1)} %get-tuple-element.39.heat, bf16[896,896]{1,0:T(8,128)(2,1)S(1)} %get-tuple-element.40.own, f32[30,896]{1,0:T(8,128)S(1)} %get-tuple-element.41.base, s32[7,128]{1,0:T(8,128)S(1)} %bitcast.13, f32[30,128]{1,0:T(8,128)S(1)} %get-tuple-element.38.depth, ...), custom_call_target="tpu_custom_call" | custom-call | flops 100000000 | bytes 30000000 | tf_op jit(solution)/shard_map/pallas_call | solution.py:510
  59.0 1.6 %collective-permute-done.2.swapped = f32[30,128]{1,0:T(8,128)S(1)} collective-permute-done((f32[30,128]{1,0:T(8,128)S(1)}, f32[30,128]{1,0:T(8,128)S(1)}, u32[]{:S(2)}, u32[]{:S(2)}) %collective-permute-start.2) | collective-permute-done | bytes 15392 | tf_op jit(solution)/shard_map/ppermute | solution.py:509
  60.7 0.8 %shard_map.147 = f32[30,896]{1,0:T(8,128)} custom-call(f32[1,128]{1,0:T(1,128)S(1)} %get-tuple-element.45.halo, f32[30,128]{1,0:T(8,128)S(1)} %collective-permute-done.2.swapped, bf16[864,128]{1,0:T(8,128)(2,1)S(1)} %collective-permute-done.before, bf16[864,128]{1,0:T(8,128)(2,1)S(1)} %collective-permute-done.1.after, ...), custom_call_target="tpu_custom_call" | custom-call | flops 2000000000 | bytes 30000000 | tf_op jit(solution)/shard_map/pallas_call | solution.py:517
Async XLA Ops:
  2.9 25.8 %all-to-all-start = ((bf16[64,5,2,128]{3,2,1,0:T(2,128)(2,1)}), bf16[64,5,2,128]{3,2,1,0:T(2,128)(2,1)S(1)}, u32[]{:S(2)}, u32[]{:S(2)}) async-start(bf16[64,5,2,128]{3,2,1,0:T(2,128)(2,1)} %bitcast.15), calls=%async_computation | async-start | bytes 327680 | tf_op jit(solution)/shard_map/all_to_all | solution.py:449
  17.0 10.0 %copy-start.2 = (bf16[40,768]{1,0:T(8,128)(2,1)S(1)}, bf16[40,768]{1,0:T(8,128)(2,1)}, u32[]{:S(2)}) copy-start(bf16[40,768]{1,0:T(8,128)(2,1)} %state) | copy-start | bytes 184324
  17.0 10.0 %copy-start.4 = (f32[8,40]{1,0:T(8,128)S(1)}, f32[8,40]{1,0:T(8,128)}, u32[]{:S(2)}) copy-start(f32[8,40]{1,0:T(8,128)} %couple.1) | copy-start | bytes 3844
  17.0 10.0 %copy-start.5 = (f32[768]{0:T(1024)S(1)}, f32[768]{0:T(1024)}, u32[]{:S(2)}) copy-start(f32[768]{0:T(1024)} %param.20) | copy-start | bytes 9220
  17.0 10.0 %copy-start.6 = (s32[24]{0:T(128)S(1)}, s32[24]{0:T(128)}, u32[]{:S(2)}) copy-start(s32[24]{0:T(128)} %src.3) | copy-start | bytes 292
  18.5 22.4 %collective-permute-start.1 = (bf16[864,128]{1,0:T(8,128)(2,1)S(1)}, bf16[864,128]{1,0:T(8,128)(2,1)S(1)}, u32[]{:S(2)}, u32[]{:S(2)}) collective-permute-start(bf16[864,128]{1,0:T(8,128)(2,1)S(1)} %shard_map.143.here), channel_id=1, source_target_pairs={{1,0},{2,1},{3,2},{4,3},{5,4},{6,5},{7,6},{8,7},{9,8},{10,9},{11,1... | collective-permute-start | bytes 663560 | tf_op jit(solution)/shard_map/ppermute | solution.py:466
  25.0 15.8 %collective-permute-start = (bf16[864,128]{1,0:T(8,128)(2,1)S(1)}, bf16[864,128]{1,0:T(8,128)(2,1)S(1)}, u32[]{:S(2)}, u32[]{:S(2)}) collective-permute-start(bf16[864,128]{1,0:T(8,128)(2,1)S(1)} %shard_map.143.here), channel_id=1, source_target_pairs={{0,1},{1,2},{2,3},{3,4},{4,5},{5,6},{6,7},{7,8},{8,9},{9,10},{10,1... | collective-permute-start | bytes 663560 | tf_op jit(solution)/shard_map/ppermute | solution.py:465
  27.0 1.7 %copy-start.7 = (f32[8]{0:T(128)S(1)}, f32[8]{0:T(128)}, u32[]{:S(2)}) copy-start(f32[8]{0:T(128)} %heat_coef.1) | copy-start | bytes 100
  28.7 9.8 %copy-start = (s32[896]{0:T(1024)S(1)}, s32[896]{0:T(1024)}, u32[]{:S(2)}) copy-start(s32[896]{0:T(1024)} %param.14) | copy-start | bytes 10756
  28.7 9.8 %copy-start.1 = (f32[30,896]{1,0:T(8,128)S(1)}, f32[30,896]{1,0:T(8,128)}, u32[]{:S(2)}) copy-start(f32[30,896]{1,0:T(8,128)} %tracer.1) | copy-start | bytes 322564
  28.7 9.8 %copy-start.3 = (s32[6,896]{1,0:T(8,128)S(1)}, s32[6,896]{1,0:T(8,128)}, u32[]{:S(2)}) copy-start(s32[6,896]{1,0:T(8,128)} %near) | copy-start | bytes 64516
  28.7 9.8 %copy-start.8 = (f32[30]{0:T(128)S(1)}, f32[30]{0:T(128)}, u32[]{:S(2)}) copy-start(f32[30]{0:T(128)} %kappa.1) | copy-start | bytes 364
  30.4 19.2 %all-to-all-start.1 = ((bf16[64,2,2,128]{3,2,1,0:T(2,128)(2,1)}), bf16[64,2,2,128]{3,2,1,0:T(2,128)(2,1)S(1)}, u32[]{:S(2)}, u32[]{:S(2)}) async-start(bf16[64,2,2,128]{3,2,1,0:T(2,128)(2,1)} %bitcast.5), calls=%async_computation.1 | async-start | bytes 131072 | tf_op jit(solution)/shard_map/all_to_all | solution.py:485
  50.2 10.5 %collective-permute-start.2 = (f32[30,128]{1,0:T(8,128)S(1)}, f32[30,128]{1,0:T(8,128)S(1)}, u32[]{:S(2)}, u32[]{:S(2)}) collective-permute-start(f32[30,128]{1,0:T(8,128)S(1)} %get-tuple-element.46), channel_id=1, source_target_pairs={{64,128},{128,192},{192,256},{256,320},{320,384},{384,448},{448,51... | collective-permute-start | bytes 46088 | tf_op jit(solution)/shard_map/ppermute | solution.py:509

commit v6 on v5

--- a/solution.py
+++ b/solution.py
@@ -270,7 +270,7 @@
     return jnp.where(low, me, lax.axis_size("blk") - 1 - me) > 0
 
 
-def heat_kernel(got, chosen, here, before, after, mask, depth, heat, forced, halo, flat):
+def heat_kernel(got, chosen, here, before, after, mask, depth, heat, forced, ends, halo, flat):
     cells = heat.shape[1]
     half = here.shape[0] - 96
     lane = iota((32, LANES), 1)
@@ -325,13 +325,12 @@
     halo[...] = beside
     edges = jnp.where(lane < TILE, meta(before, 0), meta(after, 0))[:levels]
     deep = depth[...]
-    beside = edges + deep * beside
+    forced[...] = edges + deep * beside
     row = jnp.concatenate([summed[t : t + 1, :TILE] for t in range(cells // TILE)], axis=1)
     row = row * line(mask[...].astype(F32))
     heat[...] = row
-    ends = jnp.concatenate([row[:, cells - HALO :], row[:, :HALO]], axis=1)
-    ends = meta(here, 0)[:levels] + deep * ends
-    forced[...] = jnp.where(lax.axis_index("grp") == 0, ends, beside)
+    edge = jnp.concatenate([row[:, cells - HALO :], row[:, :HALO]], axis=1)
+    ends[...] = meta(here, 0)[:levels] + deep * edge
 
 
 def halves(row):
@@ -364,13 +363,13 @@
     out[...] = base[...] + across(depth[...], cells) * row + across(rate[...], cells) * near
 
 
-def finish_kernel(halo, swapped, before, after, edge, part, speed, rate, out):
+def finish_kernel(halo, swapped, closing, before, after, edge, part, speed, rate, out):
     levels, cells = part.shape
     first = before.shape[0] - 96
     rows = slice(first, first + 32)
     low = iota((32, LANES), 1) < TILE
     outer = jnp.where(low, before[rows, :].astype(F32), after[rows, :].astype(F32))[:levels]
-    outer = jnp.where(in_group((levels, LANES)), outer, swapped[...]) * speed[...]
+    outer = jnp.where(in_group((levels, LANES)), outer, swapped[...] + closing[...]) * speed[...]
     pad = jnp.zeros((32 - levels, LANES), F32)
     outer = parts(jnp.concatenate([outer, pad], axis=0), 2)
     inner = halves(jnp.where(in_group((1, LANES)), halo[...], 0.0))
@@ -460,8 +459,8 @@
     count = lax.axis_size(axes)
     up = [(i, i - i % peers + (i + 1) % peers) for i in range(count)]
     down = [(target, source) for source, target in up]
-    seams = [(i, (i + peers) % count) for i in range(peers, count, peers)] + [(0, count - 1)]
-    seams += [(i, i - peers) for i in range(2 * peers - 1, count, peers)] + [(peers - 1, peers)]
+    seams = [(i, (i + peers) % count) for i in range(0, count, peers)]
+    seams += [(i, i - peers) for i in range(2 * peers - 1, count, peers)]
     before = lax.ppermute(here, axes, up)
     after = lax.ppermute(here, axes, down)
     mixed, shares, chosen = call(
@@ -499,14 +498,20 @@
         (VMEM,) * 6,
         flops=1_000_000_000,
     )(kappa, neighbours, tracer, mask)
-    heat, forced, halo = call(
+    heat, forced, ends, halo = call(
         heat_kernel,
-        (shape((1, cells), F32), shape((levels, LANES), F32), shape((1, LANES), F32)),
+        (
+            shape((1, cells), F32),
+            shape((levels, LANES), F32),
+            shape((levels, LANES), F32),
+            shape((1, LANES), F32),
+        ),
         [VMEM] * 7,
-        (VMEM,) * 3,
+        (VMEM,) * 4,
         [pltpu.VMEM((peers * 4, LANES), F32)],
     )(returned, chosen, here, before, after, mask, depth)
     swapped = lax.ppermute(forced, axes, seams)
+    closing = lax.ppermute(ends, axes, [(0, count - 1)])
     part, fluxes = call(
         partial_kernel,
         (shape((levels, cells), F32), shape((rows, atm_cells), BF16)),
@@ -514,8 +519,8 @@
         (VMEM, VMEM),
         flops=100_000_000,
     )(heat, own, base, mask, depth, rate, fluxes)
-    tracer_out = call(finish_kernel, shape((levels, cells), F32), [VMEM] * 8, VMEM)(
-        halo, swapped, before, after, edge, part, speed, rate
+    tracer_out = call(finish_kernel, shape((levels, cells), F32), [VMEM] * 9, VMEM)(
+        halo, swapped, closing, before, after, edge, part, speed, rate
     )
     return (fluxes, tracer_out)
 

time: 61.8 us -> 61.3 us (level)
  waiting for transfers between devices: 11.3 us -> 9.71 us
    ppermute x1, waiting for transfers between devices: 1.6 us -> 0.05 us  [shards(): swapped = lax.ppermute(forced, axes, seams)]
    ppermute x0 -> x1, starting transfers between devices: none -> 0.66 us  [shards(): closing = lax.ppermute(ends, axes, [(0, count - 1)])]
  transfers between devices with their start and end apart: 5 -> 6, of which waited for: 3 -> 2; matrix products, arithmetic and copies ran while one was open for 0% -> 0% of each run, Pallas kernels for 12% -> 12%
where the time goes in v6:
time: 61.3 us; the launch traced here: 60.6 us
  starting transfers between devices  39.2 us (64%)
  Pallas kernels  10.8 us (18%)
  waiting for transfers between devices  9.71 us (16%)
  between operations  0.85 us (1%)
    all_to_all x1, starting transfers between devices, shards(): lax.all_to_all(sent.reshape(peers, half + 1, 2, LANES), 'blk', split_axis...  14 us
    all_to_all x1, waiting for transfers between devices, shards(): lax.all_to_all(back.reshape(peers, 2, 2, LANES), 'blk', split_axis=0, con...  8.74 us
    all_to_all x1, starting transfers between devices, shards(): lax.all_to_all(back.reshape(peers, 2, 2, LANES), 'blk', split_axis=0, con...  8.07 us
    ppermute x1, starting transfers between devices, shards(): swapped = lax.ppermute(forced, axes, seams)  7.96 us
    ppermute x1, starting transfers between devices, shards(): after = lax.ppermute(here, axes, down)  6.55 us
    pallas_call x1, Pallas kernels, shards(): call(base_kernel, (shape((cells, cells), BF16), shape((2 * HALO, cells),...  2.31 us
    pallas_call x1, Pallas kernels, shards(): call(pack_kernel, shape((peers * pitch, LANES), BF16), [HBM] * 7, VMEM, [...  2.27 us
    ppermute x1, starting transfers between devices, shards(): before = lax.ppermute(here, axes, up)  1.92 us
  transfers between devices with their start and end apart: 6, of which 2 were waited for; matrix products, arithmetic and copies ran while one was open for 0% of the time, Pallas kernels for 12%

profile of v6, /device:TPU:1, one launch (start us, length us, event | category | flops | bytes accessed | tf_op | source)
XLA Modules:
  0.0 60.6 jit_solution(6584709252601655987)
XLA Ops:
  0.6 2.3 %shard_map.140 = bf16[640,128]{1,0:T(8,128)(2,1)} custom-call(s32[24]{0:T(128)} %src.3, s32[24]{0:T(128)} %bitcast.16, s32[24]{0:T(128)} %tile_hbm.1, bf16[40,896]{1,0:T(8,128)(2,1)} %fields_hbm.1, s32[7,128]{1,0:T(8,128)} %bitcast.9, f32[8,40]{1,0:T(8,128)} %couple.1, bf16[24,4096]{1,0:T(8,128)(2,1)} %weights), custom_call_target="tpu_custom_call" | custom-call | flops 2000000000 | bytes 30000000 | tf_op jit(solution)/shard_map/pallas_call | solution.py:424
  2.9 14.0 %all-to-all-start = ((bf16[64,5,2,128]{3,2,1,0:T(2,128)(2,1)}), bf16[64,5,2,128]{3,2,1,0:T(2,128)(2,1)S(1)}, u32[]{:S(2)}, u32[]{:S(2)}) async-start(bf16[64,5,2,128]{3,2,1,0:T(2,128)(2,1)} %bitcast.15), calls=%async_computation | async-start | bytes 327680 | tf_op jit(solution)/shard_map/all_to_all | solution.py:448
  17.0 0.0 copy-start.2
  17.0 0.0 copy-start.4
  17.0 0.0 copy-start.5
  17.0 0.0 copy-start.6
  17.0 1.4 %shard_map.143.here = bf16[864,128]{1,0:T(8,128)(2,1)S(1)} custom-call(s32[24]{0:T(128)} %src.3, s32[24]{0:T(128)} %bitcast.17, bf16[24,4096]{1,0:T(8,128)(2,1)} %weights, f32[30,896]{1,0:T(8,128)} %tracer.1, s32[7,128]{1,0:T(8,128)} %bitcast.10), custom_call_target="tpu_custom_call" | custom-call | flops 2000000000 | bytes 30000000 | tf_op jit(solution)/shard_map/pallas_call | solution.py:451
  18.5 6.6 %collective-permute-start.1 = (bf16[864,128]{1,0:T(8,128)(2,1)S(1)}, bf16[864,128]{1,0:T(8,128)(2,1)S(1)}, u32[]{:S(2)}, u32[]{:S(2)}) collective-permute-start(bf16[864,128]{1,0:T(8,128)(2,1)S(1)} %shard_map.143.here), channel_id=1, source_target_pairs={{1,0},{2,1},{3,2},{4,3},{5,4},{6,5},{7,6},{8,7},{9,8},{10,9},{11,1... | collective-permute-start | bytes 663560 | tf_op jit(solution)/shard_map/ppermute | solution.py:465
  25.0 1.9 %collective-permute-start = (bf16[864,128]{1,0:T(8,128)(2,1)S(1)}, bf16[864,128]{1,0:T(8,128)(2,1)S(1)}, u32[]{:S(2)}, u32[]{:S(2)}) collective-permute-start(bf16[864,128]{1,0:T(8,128)(2,1)S(1)} %shard_map.143.here), channel_id=1, source_target_pairs={{0,1},{1,2},{2,3},{3,4},{4,5},{5,6},{6,7},{7,8},{8,9},{9,10},{10,1... | collective-permute-start | bytes 663560 | tf_op jit(solution)/shard_map/ppermute | solution.py:464
  27.0 0.0 copy-done.2
  27.0 0.0 copy-done.4
  27.0 0.0 copy-done.5
  27.0 0.0 copy-done.6
  27.0 0.0 copy-start.7
  27.0 0.7 %shard_map.141 = (f32[16,512]{1,0:T(8,128)S(1)}, f32[16,128]{1,0:T(8,128)S(1)}, f32[16,1536]{1,0:T(8,128)S(1)}) custom-call(s32[24]{0:T(128)S(1)} %copy-done.6, bf16[40,768]{1,0:T(8,128)(2,1)S(1)} %copy-done.2, f32[6,128]{1,0:T(8,128)S(1)} %bitcast.14, f32[8,40]{1,0:T(8,128)S(1)} %copy-done.4), custom_call_target="tpu_custom_call" | custom-call | flops 2000000000 | bytes 30000000 | tf_op jit(solution)/shard_map/pallas_call | solution.py:466
  27.8 0.9 %all-to-all-done = bf16[64,5,2,128]{3,2,1,0:T(2,128)(2,1)S(1)} async-done(((bf16[64,5,2,128]{3,2,1,0:T(2,128)(2,1)}), bf16[64,5,2,128]{3,2,1,0:T(2,128)(2,1)S(1)}, u32[]{:S(2)}, u32[]{:S(2)}) %all-to-all-start) | async-done | bytes 163872 | tf_op jit(solution)/shard_map/all_to_all | solution.py:448
  28.7 0.0 copy-done.7
  28.7 0.0 copy-start
  28.7 0.0 copy-start.1
  28.7 0.0 copy-start.3
  28.7 0.0 copy-start.8
  28.7 1.7 %shard_map.142 = (f32[16,512]{1,0:T(8,128)S(1)}, bf16[256,128]{1,0:T(8,128)(2,1)}) custom-call(f32[8]{0:T(128)S(1)} %copy-done.7, bf16[640,128]{1,0:T(8,128)(2,1)S(1)} %bitcast.7, f32[16,512]{1,0:T(8,128)S(1)} %get-tuple-element.29.mixed, f32[16,128]{1,0:T(8,128)S(1)} %get-tuple-element.30.shares), custom_call_target="tpu_custom_call" | custom-call | flops 2000000000 | bytes 30000000 | tf_op jit(solution)/shard_map/pallas_call | solution.py:476
  30.4 8.1 %all-to-all-start.1 = ((bf16[64,2,2,128]{3,2,1,0:T(2,128)(2,1)}), bf16[64,2,2,128]{3,2,1,0:T(2,128)(2,1)S(1)}, u32[]{:S(2)}, u32[]{:S(2)}) async-start(bf16[64,2,2,128]{3,2,1,0:T(2,128)(2,1)} %bitcast.5), calls=%async_computation.1 | async-start | bytes 131072 | tf_op jit(solution)/shard_map/all_to_all | solution.py:484
  38.5 0.0 copy-done
  38.5 0.0 copy-done.1
  38.5 0.0 copy-done.3
  38.5 0.0 copy-done.8
  38.5 2.3 %shard_map.144 = (bf16[896,896]{1,0:T(8,128)(2,1)S(1)}, bf16[128,896]{1,0:T(8,128)(2,1)S(1)}, f32[30,896]{1,0:T(8,128)S(1)}, f32[30,128]{1,0:T(8,128)S(1)}, f32[...) custom-call(f32[30]{0:T(128)S(1)} %copy-done.8, s32[6,896]{1,0:T(8,128)S(1)} %copy-done.3, f32[30,896]{1,0:T(8,128)S(1)} %copy-done.1, ...), custom_call_target="tpu_custom_call" | custom-call | flops 1000000000 | bytes 30000000 | tf_op jit(solution)/shard_map/pallas_call | solution.py:487
  40.8 0.0 collective-permute-done.1.after
  40.9 0.0 collective-permute-done.before
  40.9 8.7 %all-to-all-done.1 = bf16[64,2,2,128]{3,2,1,0:T(2,128)(2,1)S(1)} async-done(((bf16[64,2,2,128]{3,2,1,0:T(2,128)(2,1)}), bf16[64,2,2,128]{3,2,1,0:T(2,128)(2,1)S(1)}, u32[]{:S(2)}, u32[]{:S(2)}) %all-to-all-start.1) | async-done | bytes 65568 | tf_op jit(solution)/shard_map/all_to_all | solution.py:484
  49.6 0.6 shard_map.145
  50.2 8.0 %collective-permute-start.2 = (f32[30,128]{1,0:T(8,128)S(1)}, f32[30,128]{1,0:T(8,128)S(1)}, u32[]{:S(2)}, u32[]{:S(2)}) collective-permute-start(f32[30,128]{1,0:T(8,128)S(1)} %get-tuple-element.47), channel_id=1, source_target_pairs={{0,64},{64,128},{128,192},{192,256},{256,320},{320,384},{384,448},... | collective-permute-start | bytes 46088 | tf_op jit(solution)/shard_map/ppermute | solution.py:513
  58.2 0.7 %collective-permute-start.3 = (f32[30,128]{1,0:T(8,128)S(1)}, f32[30,128]{1,0:T(8,128)S(1)}, u32[]{:S(2)}, u32[]{:S(2)}) collective-permute-start(f32[30,128]{1,0:T(8,128)S(1)} %get-tuple-element.48), channel_id=1, source_target_pairs={{0,1023}} | collective-permute-start | bytes 46088 | tf_op jit(solution)/shard_map/ppermute | solution.py:514
  58.8 0.9 %shard_map.146 = (f32[30,896]{1,0:T(8,128)S(1)}, bf16[8,768]{1,0:T(8,128)(2,1)}) custom-call(f32[1,896]{1,0:T(1,128)S(1)} %get-tuple-element.40.heat, bf16[896,896]{1,0:T(8,128)(2,1)S(1)} %get-tuple-element.41.own, f32[30,896]{1,0:T(8,128)S(1)} %get-tuple-element.42.base, s32[7,128]{1,0:T(8,128)S(1)} %bitcast.13, f32[30,128]{1,0:T(8,128)S(1)} %get-tuple-element.39.depth, ...), custom_call_target="tpu_custom_call" | custom-call | flops 100000000 | bytes 30000000 | tf_op jit(solution)/shard_map/pallas_call | solution.py:515
  59.7 0.0 collective-permute-done.2.swapped
  59.8 0.0 collective-permute-done.3.closing
  59.8 0.8 %shard_map.147 = f32[30,896]{1,0:T(8,128)} custom-call(f32[1,128]{1,0:T(1,128)S(1)} %get-tuple-element.46.halo, f32[30,128]{1,0:T(8,128)S(1)} %collective-permute-done.2.swapped, f32[30,128]{1,0:T(8,128)S(1)} %collective-permute-done.3.closing, bf16[864,128]{1,0:T(8,128)(2,1)S(1)} %collective-permute-done.before, ...), custom_call_target="tpu_custom_call" | custom-call | flops 2000000000 | bytes 30000000 | tf_op jit(solution)/shard_map/pallas_call | solution.py:522
Async XLA Ops:
  2.9 25.8 %all-to-all-start = ((bf16[64,5,2,128]{3,2,1,0:T(2,128)(2,1)}), bf16[64,5,2,128]{3,2,1,0:T(2,128)(2,1)S(1)}, u32[]{:S(2)}, u32[]{:S(2)}) async-start(bf16[64,5,2,128]{3,2,1,0:T(2,128)(2,1)} %bitcast.15), calls=%async_computation | async-start | bytes 327680 | tf_op jit(solution)/shard_map/all_to_all | solution.py:448
  17.0 10.0 %copy-start.2 = (bf16[40,768]{1,0:T(8,128)(2,1)S(1)}, bf16[40,768]{1,0:T(8,128)(2,1)}, u32[]{:S(2)}) copy-start(bf16[40,768]{1,0:T(8,128)(2,1)} %state) | copy-start | bytes 184324
  17.0 10.0 %copy-start.4 = (f32[8,40]{1,0:T(8,128)S(1)}, f32[8,40]{1,0:T(8,128)}, u32[]{:S(2)}) copy-start(f32[8,40]{1,0:T(8,128)} %couple.1) | copy-start | bytes 3844
  17.0 10.0 %copy-start.5 = (f32[768]{0:T(1024)S(1)}, f32[768]{0:T(1024)}, u32[]{:S(2)}) copy-start(f32[768]{0:T(1024)} %param.20) | copy-start | bytes 9220
  17.0 10.0 %copy-start.6 = (s32[24]{0:T(128)S(1)}, s32[24]{0:T(128)}, u32[]{:S(2)}) copy-start(s32[24]{0:T(128)} %src.3) | copy-start | bytes 292
  18.5 22.4 %collective-permute-start.1 = (bf16[864,128]{1,0:T(8,128)(2,1)S(1)}, bf16[864,128]{1,0:T(8,128)(2,1)S(1)}, u32[]{:S(2)}, u32[]{:S(2)}) collective-permute-start(bf16[864,128]{1,0:T(8,128)(2,1)S(1)} %shard_map.143.here), channel_id=1, source_target_pairs={{1,0},{2,1},{3,2},{4,3},{5,4},{6,5},{7,6},{8,7},{9,8},{10,9},{11,1... | collective-permute-start | bytes 663560 | tf_op jit(solution)/shard_map/ppermute | solution.py:465
  25.0 15.8 %collective-permute-start = (bf16[864,128]{1,0:T(8,128)(2,1)S(1)}, bf16[864,128]{1,0:T(8,128)(2,1)S(1)}, u32[]{:S(2)}, u32[]{:S(2)}) collective-permute-start(bf16[864,128]{1,0:T(8,128)(2,1)S(1)} %shard_map.143.here), channel_id=1, source_target_pairs={{0,1},{1,2},{2,3},{3,4},{4,5},{5,6},{6,7},{7,8},{8,9},{9,10},{10,1... | collective-permute-start | bytes 663560 | tf_op jit(solution)/shard_map/ppermute | solution.py:464
  27.0 1.7 %copy-start.7 = (f32[8]{0:T(128)S(1)}, f32[8]{0:T(128)}, u32[]{:S(2)}) copy-start(f32[8]{0:T(128)} %heat_coef.1) | copy-start | bytes 100
  28.7 9.8 %copy-start = (s32[896]{0:T(1024)S(1)}, s32[896]{0:T(1024)}, u32[]{:S(2)}) copy-start(s32[896]{0:T(1024)} %param.14) | copy-start | bytes 10756
  28.7 9.8 %copy-start.1 = (f32[30,896]{1,0:T(8,128)S(1)}, f32[30,896]{1,0:T(8,128)}, u32[]{:S(2)}) copy-start(f32[30,896]{1,0:T(8,128)} %tracer.1) | copy-start | bytes 322564
  28.7 9.8 %copy-start.3 = (s32[6,896]{1,0:T(8,128)S(1)}, s32[6,896]{1,0:T(8,128)}, u32[]{:S(2)}) copy-start(s32[6,896]{1,0:T(8,128)} %near) | copy-start | bytes 64516
  28.7 9.8 %copy-start.8 = (f32[30]{0:T(128)S(1)}, f32[30]{0:T(128)}, u32[]{:S(2)}) copy-start(f32[30]{0:T(128)} %kappa.1) | copy-start | bytes 364
  30.4 19.2 %all-to-all-start.1 = ((bf16[64,2,2,128]{3,2,1,0:T(2,128)(2,1)}), bf16[64,2,2,128]{3,2,1,0:T(2,128)(2,1)S(1)}, u32[]{:S(2)}, u32[]{:S(2)}) async-start(bf16[64,2,2,128]{3,2,1,0:T(2,128)(2,1)} %bitcast.5), calls=%async_computation.1 | async-start | bytes 131072 | tf_op jit(solution)/shard_map/all_to_all | solution.py:484
  50.2 9.6 %collective-permute-start.2 = (f32[30,128]{1,0:T(8,128)S(1)}, f32[30,128]{1,0:T(8,128)S(1)}, u32[]{:S(2)}, u32[]{:S(2)}) collective-permute-start(f32[30,128]{1,0:T(8,128)S(1)} %get-tuple-element.47), channel_id=1, source_target_pairs={{0,64},{64,128},{128,192},{192,256},{256,320},{320,384},{384,448},... | collective-permute-start | bytes 46088 | tf_op jit(solution)/shard_map/ppermute | solution.py:513
  58.2 1.6 %collective-permute-start.3 = (f32[30,128]{1,0:T(8,128)S(1)}, f32[30,128]{1,0:T(8,128)S(1)}, u32[]{:S(2)}, u32[]{:S(2)}) collective-permute-start(f32[30,128]{1,0:T(8,128)S(1)} %get-tuple-element.48), channel_id=1, source_target_pairs={{0,1023}} | collective-permute-start | bytes 46088 | tf_op jit(solution)/shard_map/ppermute | solution.py:514

commit v7 on v6

--- a/solution.py
+++ b/solution.py
@@ -115,7 +115,7 @@
         both = jnp.where(left, even, odd)
         slots[pl.ds(at, half), :] = both[:half] + pltpu.roll(both, TILE, 1)[half:]
         slots[pl.ds(at + half, 1), :] = jnp.full((1, LANES), tile[e] + 1, jnp.int32).astype(F32)
-    out[...] = slots[...].astype(BF16)
+    out[...] = slots[: out.shape[0], :].astype(BF16)
 
 
 def ship_kernel(src, route, weights, tracer, mask, out, seen, wide):
@@ -195,7 +195,7 @@
     half = mixed.shape[1] // LANES
     peers = back.shape[0] // 4
     pitch = 2 * (half + 1)
-    flat[...] = got[...].astype(F32)
+    flat[: got.shape[0], :] = got[...].astype(F32)
     row = lambda rank, q: flat[pl.ds(rank * (half + 1) + q, peers, stride=pitch), :]
     first, second = row(0, half), row(1, half)
     named = jnp.concatenate([first, second], axis=0).astype(BF16)
@@ -288,7 +288,7 @@
     ]
     peers = got.shape[0] // 4
     count = half // LANES
-    flat[...] = got[...].astype(F32)
+    flat[: got.shape[0], :] = got[...].astype(F32)
     low = iota((16, LANES), 1) < TILE
 
     def lookup(k, which):
@@ -435,8 +435,8 @@
             pltpu.VMEM((rows, fields), F32),
             pltpu.VMEM((entries, TILE * TILE), BF16),
             pltpu.VMEM((cells // TILE, 4 * rows, TILE // 2), BF16),
-            pltpu.VMEM((entries * PITCH, LANES), F32),
-            pltpu.VMEM((peers * pitch, LANES), F32),
+            pltpu.VMEM(((entries + 1) * PITCH, LANES), F32),
+            pltpu.VMEM((peers * pitch + 8, LANES), F32),
             pltpu.SMEM((peers,), i32),
             pltpu.SemaphoreType.DMA((7,)),
         ],
@@ -453,7 +453,7 @@
         shape((entries * TILE // 2 + 96, LANES), BF16),
         [SMEM, SMEM, VMEM, VMEM, VMEM],
         VMEM,
-        [pltpu.SMEM((peers,), i32), pltpu.VMEM((entries * WIDE, LANES), F32)],
+        [pltpu.SMEM((peers,), i32), pltpu.VMEM(((entries + 1) * WIDE, LANES), F32)],
     )(*(in_hbm(x) for x in (entry_src, route, weight_tiles, tracer, mask)))
     axes = ("grp", "blk")
     count = lax.axis_size(axes)
@@ -478,7 +478,7 @@
         (shape((16, half * LANES), F32), shape((peers * 4, LANES), BF16)),
         [SMEM, VMEM, VMEM, VMEM],
         (VMEM, VMEM),
-        [pltpu.VMEM((peers * pitch, LANES), F32)],
+        [pltpu.VMEM((peers * pitch + 16, LANES), F32)],
     )(heat_coef, got, mixed, shares)
     back, neighbours, tracer = lax.optimization_barrier((back, neighbours, tracer))
     returned = lax.all_to_all(
@@ -508,7 +508,7 @@
         ),
         [VMEM] * 7,
         (VMEM,) * 4,
-        [pltpu.VMEM((peers * 4, LANES), F32)],
+        [pltpu.VMEM((peers * 4 + 8, LANES), F32)],
     )(returned, chosen, here, before, after, mask, depth)
     swapped = lax.ppermute(forced, axes, seams)
     closing = lax.ppermute(ends, axes, [(0, count - 1)])

time: 61.3 us -> 61.3 us (level)
  no operation moved by 1% of the time
where the time goes in v7:
time: 61.3 us; the launch traced here: 60.6 us
  starting transfers between devices  39.2 us (64%)
  Pallas kernels  10.8 us (18%)
  waiting for transfers between devices  9.71 us (16%)
  between operations  0.85 us (1%)
    all_to_all x1, starting transfers between devices, shards(): lax.all_to_all(sent.reshape(peers, half + 1, 2, LANES), 'blk', split_axis...  14.1 us
    all_to_all x1, waiting for transfers between devices, shards(): lax.all_to_all(back.reshape(peers, 2, 2, LANES), 'blk', split_axis=0, con...  8.74 us
    all_to_all x1, starting transfers between devices, shards(): lax.all_to_all(back.reshape(peers, 2, 2, LANES), 'blk', split_axis=0, con...  8.08 us
    ppermute x1, starting transfers between devices, shards(): swapped = lax.ppermute(forced, axes, seams)  7.94 us
    ppermute x1, starting transfers between devices, shards(): after = lax.ppermute(here, axes, down)  6.55 us
    pallas_call x1, Pallas kernels, shards(): call(base_kernel, (shape((cells, cells), BF16), shape((2 * HALO, cells),...  2.31 us
    pallas_call x1, Pallas kernels, shards(): call(pack_kernel, shape((peers * pitch, LANES), BF16), [HBM] * 7, VMEM, [...  2.27 us
    ppermute x1, starting transfers between devices, shards(): before = lax.ppermute(here, axes, up)  1.92 us
  transfers between devices with their start and end apart: 6, of which 2 were waited for; matrix products, arithmetic and copies ran while one was open for 0% of the time, Pallas kernels for 12%

profile of v7, /device:TPU:1, one launch (start us, length us, event | category | flops | bytes accessed | tf_op | source)
XLA Modules:
  0.0 60.6 jit_solution(5950729754845286938)
XLA Ops:
  0.6 2.3 %shard_map.140 = bf16[640,128]{1,0:T(8,128)(2,1)} custom-call(s32[24]{0:T(128)} %src.3, s32[24]{0:T(128)} %bitcast.16, s32[24]{0:T(128)} %tile_hbm.1, bf16[40,896]{1,0:T(8,128)(2,1)} %fields_hbm.1, s32[7,128]{1,0:T(8,128)} %bitcast.9, f32[8,40]{1,0:T(8,128)} %couple.1, bf16[24,4096]{1,0:T(8,128)(2,1)} %weights), custom_call_target="tpu_custom_call" | custom-call | flops 2000000000 | bytes 30000000 | tf_op jit(solution)/shard_map/pallas_call | solution.py:424
  2.9 14.1 %all-to-all-start = ((bf16[64,5,2,128]{3,2,1,0:T(2,128)(2,1)}), bf16[64,5,2,128]{3,2,1,0:T(2,128)(2,1)S(1)}, u32[]{:S(2)}, u32[]{:S(2)}) async-start(bf16[64,5,2,128]{3,2,1,0:T(2,128)(2,1)} %bitcast.15), calls=%async_computation | async-start | bytes 327680 | tf_op jit(solution)/shard_map/all_to_all | solution.py:448
  17.0 0.0 copy-start.2
  17.0 0.0 copy-start.4
  17.0 0.0 copy-start.5
  17.0 0.0 copy-start.6
  17.0 1.4 %shard_map.143.here = bf16[864,128]{1,0:T(8,128)(2,1)S(1)} custom-call(s32[24]{0:T(128)} %src.3, s32[24]{0:T(128)} %bitcast.17, bf16[24,4096]{1,0:T(8,128)(2,1)} %weights, f32[30,896]{1,0:T(8,128)} %tracer.1, s32[7,128]{1,0:T(8,128)} %bitcast.10), custom_call_target="tpu_custom_call" | custom-call | flops 2000000000 | bytes 30000000 | tf_op jit(solution)/shard_map/pallas_call | solution.py:451
  18.5 6.6 %collective-permute-start.1 = (bf16[864,128]{1,0:T(8,128)(2,1)S(1)}, bf16[864,128]{1,0:T(8,128)(2,1)S(1)}, u32[]{:S(2)}, u32[]{:S(2)}) collective-permute-start(bf16[864,128]{1,0:T(8,128)(2,1)S(1)} %shard_map.143.here), channel_id=1, source_target_pairs={{1,0},{2,1},{3,2},{4,3},{5,4},{6,5},{7,6},{8,7},{9,8},{10,9},{11,1... | collective-permute-start | bytes 663560 | tf_op jit(solution)/shard_map/ppermute | solution.py:465
  25.0 1.9 %collective-permute-start = (bf16[864,128]{1,0:T(8,128)(2,1)S(1)}, bf16[864,128]{1,0:T(8,128)(2,1)S(1)}, u32[]{:S(2)}, u32[]{:S(2)}) collective-permute-start(bf16[864,128]{1,0:T(8,128)(2,1)S(1)} %shard_map.143.here), channel_id=1, source_target_pairs={{0,1},{1,2},{2,3},{3,4},{4,5},{5,6},{6,7},{7,8},{8,9},{9,10},{10,1... | collective-permute-start | bytes 663560 | tf_op jit(solution)/shard_map/ppermute | solution.py:464
  27.0 0.0 copy-done.2
  27.0 0.0 copy-done.4
  27.0 0.0 copy-done.5
  27.0 0.0 copy-done.6
  27.0 0.0 copy-start.7
  27.0 0.7 %shard_map.141 = (f32[16,512]{1,0:T(8,128)S(1)}, f32[16,128]{1,0:T(8,128)S(1)}, f32[16,1536]{1,0:T(8,128)S(1)}) custom-call(s32[24]{0:T(128)S(1)} %copy-done.6, bf16[40,768]{1,0:T(8,128)(2,1)S(1)} %copy-done.2, f32[6,128]{1,0:T(8,128)S(1)} %bitcast.14, f32[8,40]{1,0:T(8,128)S(1)} %copy-done.4), custom_call_target="tpu_custom_call" | custom-call | flops 2000000000 | bytes 30000000 | tf_op jit(solution)/shard_map/pallas_call | solution.py:466
  27.8 0.9 %all-to-all-done = bf16[64,5,2,128]{3,2,1,0:T(2,128)(2,1)S(1)} async-done(((bf16[64,5,2,128]{3,2,1,0:T(2,128)(2,1)}), bf16[64,5,2,128]{3,2,1,0:T(2,128)(2,1)S(1)}, u32[]{:S(2)}, u32[]{:S(2)}) %all-to-all-start) | async-done | bytes 163872 | tf_op jit(solution)/shard_map/all_to_all | solution.py:448
  28.7 0.0 copy-done.7
  28.7 0.0 copy-start
  28.7 0.0 copy-start.1
  28.7 0.0 copy-start.3
  28.7 0.0 copy-start.8
  28.7 1.7 %shard_map.142 = (f32[16,512]{1,0:T(8,128)S(1)}, bf16[256,128]{1,0:T(8,128)(2,1)}) custom-call(f32[8]{0:T(128)S(1)} %copy-done.7, bf16[640,128]{1,0:T(8,128)(2,1)S(1)} %bitcast.7, f32[16,512]{1,0:T(8,128)S(1)} %get-tuple-element.29.mixed, f32[16,128]{1,0:T(8,128)S(1)} %get-tuple-element.30.shares), custom_call_target="tpu_custom_call" | custom-call | flops 2000000000 | bytes 30000000 | tf_op jit(solution)/shard_map/pallas_call | solution.py:476
  30.4 8.1 %all-to-all-start.1 = ((bf16[64,2,2,128]{3,2,1,0:T(2,128)(2,1)}), bf16[64,2,2,128]{3,2,1,0:T(2,128)(2,1)S(1)}, u32[]{:S(2)}, u32[]{:S(2)}) async-start(bf16[64,2,2,128]{3,2,1,0:T(2,128)(2,1)} %bitcast.5), calls=%async_computation.1 | async-start | bytes 131072 | tf_op jit(solution)/shard_map/all_to_all | solution.py:484
  38.5 0.0 copy-done
  38.5 0.0 copy-done.1
  38.5 0.0 copy-done.3
  38.5 0.0 copy-done.8
  38.5 2.3 %shard_map.144 = (bf16[896,896]{1,0:T(8,128)(2,1)S(1)}, bf16[128,896]{1,0:T(8,128)(2,1)S(1)}, f32[30,896]{1,0:T(8,128)S(1)}, f32[30,128]{1,0:T(8,128)S(1)}, f32[...) custom-call(f32[30]{0:T(128)S(1)} %copy-done.8, s32[6,896]{1,0:T(8,128)S(1)} %copy-done.3, f32[30,896]{1,0:T(8,128)S(1)} %copy-done.1, ...), custom_call_target="tpu_custom_call" | custom-call | flops 1000000000 | bytes 30000000 | tf_op jit(solution)/shard_map/pallas_call | solution.py:487
  40.9 0.0 collective-permute-done.1.after
  40.9 0.0 collective-permute-done.before
  40.9 8.7 %all-to-all-done.1 = bf16[64,2,2,128]{3,2,1,0:T(2,128)(2,1)S(1)} async-done(((bf16[64,2,2,128]{3,2,1,0:T(2,128)(2,1)}), bf16[64,2,2,128]{3,2,1,0:T(2,128)(2,1)S(1)}, u32[]{:S(2)}, u32[]{:S(2)}) %all-to-all-start.1) | async-done | bytes 65568 | tf_op jit(solution)/shard_map/all_to_all | solution.py:484
  49.6 0.6 shard_map.145
  50.2 7.9 %collective-permute-start.2 = (f32[30,128]{1,0:T(8,128)S(1)}, f32[30,128]{1,0:T(8,128)S(1)}, u32[]{:S(2)}, u32[]{:S(2)}) collective-permute-start(f32[30,128]{1,0:T(8,128)S(1)} %get-tuple-element.47), channel_id=1, source_target_pairs={{0,64},{64,128},{128,192},{192,256},{256,320},{320,384},{384,448},... | collective-permute-start | bytes 46088 | tf_op jit(solution)/shard_map/ppermute | solution.py:513
  58.2 0.7 %collective-permute-start.3 = (f32[30,128]{1,0:T(8,128)S(1)}, f32[30,128]{1,0:T(8,128)S(1)}, u32[]{:S(2)}, u32[]{:S(2)}) collective-permute-start(f32[30,128]{1,0:T(8,128)S(1)} %get-tuple-element.48), channel_id=1, source_target_pairs={{0,1023}} | collective-permute-start | bytes 46088 | tf_op jit(solution)/shard_map/ppermute | solution.py:514
  58.8 0.9 %shard_map.146 = (f32[30,896]{1,0:T(8,128)S(1)}, bf16[8,768]{1,0:T(8,128)(2,1)}) custom-call(f32[1,896]{1,0:T(1,128)S(1)} %get-tuple-element.40.heat, bf16[896,896]{1,0:T(8,128)(2,1)S(1)} %get-tuple-element.41.own, f32[30,896]{1,0:T(8,128)S(1)} %get-tuple-element.42.base, s32[7,128]{1,0:T(8,128)S(1)} %bitcast.13, f32[30,128]{1,0:T(8,128)S(1)} %get-tuple-element.39.depth, ...), custom_call_target="tpu_custom_call" | custom-call | flops 100000000 | bytes 30000000 | tf_op jit(solution)/shard_map/pallas_call | solution.py:515
  59.7 0.0 collective-permute-done.2.swapped
  59.8 0.0 collective-permute-done.3.closing
  59.8 0.8 %shard_map.147 = f32[30,896]{1,0:T(8,128)} custom-call(f32[1,128]{1,0:T(1,128)S(1)} %get-tuple-element.46.halo, f32[30,128]{1,0:T(8,128)S(1)} %collective-permute-done.2.swapped, f32[30,128]{1,0:T(8,128)S(1)} %collective-permute-done.3.closing, bf16[864,128]{1,0:T(8,128)(2,1)S(1)} %collective-permute-done.before, ...), custom_call_target="tpu_custom_call" | custom-call | flops 2000000000 | bytes 30000000 | tf_op jit(solution)/shard_map/pallas_call | solution.py:522
Async XLA Ops:
  2.9 25.8 %all-to-all-start = ((bf16[64,5,2,128]{3,2,1,0:T(2,128)(2,1)}), bf16[64,5,2,128]{3,2,1,0:T(2,128)(2,1)S(1)}, u32[]{:S(2)}, u32[]{:S(2)}) async-start(bf16[64,5,2,128]{3,2,1,0:T(2,128)(2,1)} %bitcast.15), calls=%async_computation | async-start | bytes 327680 | tf_op jit(solution)/shard_map/all_to_all | solution.py:448
  17.0 10.0 %copy-start.2 = (bf16[40,768]{1,0:T(8,128)(2,1)S(1)}, bf16[40,768]{1,0:T(8,128)(2,1)}, u32[]{:S(2)}) copy-start(bf16[40,768]{1,0:T(8,128)(2,1)} %state) | copy-start | bytes 184324
  17.0 10.0 %copy-start.4 = (f32[8,40]{1,0:T(8,128)S(1)}, f32[8,40]{1,0:T(8,128)}, u32[]{:S(2)}) copy-start(f32[8,40]{1,0:T(8,128)} %couple.1) | copy-start | bytes 3844
  17.0 10.0 %copy-start.5 = (f32[768]{0:T(1024)S(1)}, f32[768]{0:T(1024)}, u32[]{:S(2)}) copy-start(f32[768]{0:T(1024)} %param.20) | copy-start | bytes 9220
  17.0 10.0 %copy-start.6 = (s32[24]{0:T(128)S(1)}, s32[24]{0:T(128)}, u32[]{:S(2)}) copy-start(s32[24]{0:T(128)} %src.3) | copy-start | bytes 292
  18.5 22.4 %collective-permute-start.1 = (bf16[864,128]{1,0:T(8,128)(2,1)S(1)}, bf16[864,128]{1,0:T(8,128)(2,1)S(1)}, u32[]{:S(2)}, u32[]{:S(2)}) collective-permute-start(bf16[864,128]{1,0:T(8,128)(2,1)S(1)} %shard_map.143.here), channel_id=1, source_target_pairs={{1,0},{2,1},{3,2},{4,3},{5,4},{6,5},{7,6},{8,7},{9,8},{10,9},{11,1... | collective-permute-start | bytes 663560 | tf_op jit(solution)/shard_map/ppermute | solution.py:465
  25.0 15.8 %collective-permute-start = (bf16[864,128]{1,0:T(8,128)(2,1)S(1)}, bf16[864,128]{1,0:T(8,128)(2,1)S(1)}, u32[]{:S(2)}, u32[]{:S(2)}) collective-permute-start(bf16[864,128]{1,0:T(8,128)(2,1)S(1)} %shard_map.143.here), channel_id=1, source_target_pairs={{0,1},{1,2},{2,3},{3,4},{4,5},{5,6},{6,7},{7,8},{8,9},{9,10},{10,1... | collective-permute-start | bytes 663560 | tf_op jit(solution)/shard_map/ppermute | solution.py:464
  27.0 1.7 %copy-start.7 = (f32[8]{0:T(128)S(1)}, f32[8]{0:T(128)}, u32[]{:S(2)}) copy-start(f32[8]{0:T(128)} %heat_coef.1) | copy-start | bytes 100
  28.7 9.8 %copy-start = (s32[896]{0:T(1024)S(1)}, s32[896]{0:T(1024)}, u32[]{:S(2)}) copy-start(s32[896]{0:T(1024)} %param.14) | copy-start | bytes 10756
  28.7 9.8 %copy-start.1 = (f32[30,896]{1,0:T(8,128)S(1)}, f32[30,896]{1,0:T(8,128)}, u32[]{:S(2)}) copy-start(f32[30,896]{1,0:T(8,128)} %tracer.1) | copy-start | bytes 322564
  28.7 9.8 %copy-start.3 = (s32[6,896]{1,0:T(8,128)S(1)}, s32[6,896]{1,0:T(8,128)}, u32[]{:S(2)}) copy-start(s32[6,896]{1,0:T(8,128)} %near) | copy-start | bytes 64516
  28.7 9.8 %copy-start.8 = (f32[30]{0:T(128)S(1)}, f32[30]{0:T(128)}, u32[]{:S(2)}) copy-start(f32[30]{0:T(128)} %kappa.1) | copy-start | bytes 364
  30.4 19.2 %all-to-all-start.1 = ((bf16[64,2,2,128]{3,2,1,0:T(2,128)(2,1)}), bf16[64,2,2,128]{3,2,1,0:T(2,128)(2,1)S(1)}, u32[]{:S(2)}, u32[]{:S(2)}) async-start(bf16[64,2,2,128]{3,2,1,0:T(2,128)(2,1)} %bitcast.5), calls=%async_computation.1 | async-start | bytes 131072 | tf_op jit(solution)/shard_map/all_to_all | solution.py:484
  50.2 9.6 %collective-permute-start.2 = (f32[30,128]{1,0:T(8,128)S(1)}, f32[30,128]{1,0:T(8,128)S(1)}, u32[]{:S(2)}, u32[]{:S(2)}) collective-permute-start(f32[30,128]{1,0:T(8,128)S(1)} %get-tuple-element.47), channel_id=1, source_target_pairs={{0,64},{64,128},{128,192},{192,256},{256,320},{320,384},{384,448},... | collective-permute-start | bytes 46088 | tf_op jit(solution)/shard_map/ppermute | solution.py:513
  58.2 1.6 %collective-permute-start.3 = (f32[30,128]{1,0:T(8,128)S(1)}, f32[30,128]{1,0:T(8,128)S(1)}, u32[]{:S(2)}, u32[]{:S(2)}) collective-permute-start(f32[30,128]{1,0:T(8,128)S(1)} %get-tuple-element.48), channel_id=1, source_target_pairs={{0,1023}} | collective-permute-start | bytes 46088 | tf_op jit(solution)/shard_map/ppermute | solution.py:514
